TPU v7x, 1024 devices: a whole 4x8x16 slice. The times are simulated.
1024 devices in a mesh: row: 8 (over z_lo), col: 16 (over y, z_hi), depth: 8 (over x, core).
Axes of the slice: x: 4, y: 8, z: 16 (z_hi: 2, z_lo: 8; z = z_hi * 8 + z_lo), core: 2. Of those that a mesh axis runs over, the one named last changes fastest.
Arguments:
- grad_out: bfloat16 [32768, 1024], P(('col', 'row')), may hold values from -6 to 6
- relu_mask: int32 [32768, 1024], P(('col', 'row')), may hold values 0 or 1
- aggregated: bfloat16 [32768, 1024], P(('col', 'row'), 'depth'), may hold values from -0.03125 to 0.03125
- weight: bfloat16 [1024, 1024], P('depth'), may hold values from -0.1875 to 0.1875
- adj_tiles: bfloat16 [8, 16, 160, 128, 128], P('row', 'col'), may hold values from -0.078125 to 0.078125
- tile_row: int32 [8, 16, 160], P('row', 'col'), may hold values from 0 to 31
- tile_col: int32 [8, 16, 160], P('row', 'col'), may hold values from 0 to 15
- tile_count: int32 [8, 16], P('row', 'col'), may hold values from 20 to 160, as said below
Outputs:
- grad_features: bfloat16 [32768, 1024], P(('row', 'col'), 'depth')
- grad_weight: float32 [1024, 1024], P('depth')
Inputs may be any that keep to these rules, and one draw needn't show every extreme that they name: `tile_count`: some block has all 160 slots live.
All inputs are finite; a program needn't handle non-finite values. No bound on the sum of `relu_mask` on one device may be relied on, other than what follows from the above.
Results may differ from a plain program's by a relative error of at most 0.018.
Values may be sent and summed in bfloat16 or wider, within the bound.
No kernel may reach another device: no remote copies, remote signals or barrier semaphores. Data moves between devices by JAX's collectives and lax.ppermute only.
A program may use at most 64 MiB of HBM per device.

v0:
```python
import jax
import jax.numpy as jnp
from jax import lax
from jax.sharding import PartitionSpec as P


def shards(grad_out, relu_mask, aggregated, weight, adj_tiles, tile_row, tile_col, tile_count):
    masked = grad_out * relu_mask.astype(jnp.bfloat16)
    tile_data = adj_tiles[0, 0]
    row_ids = tile_row[0, 0]
    col_ids = tile_col[0, 0]
    live_count = tile_count[0, 0]
    tile_size = tile_data.shape[1]
    feat_width = weight.shape[0]
    contract_out = (((1,), (1,)), ((), ()))
    own_panel = lax.dot_general(
        masked, weight, contract_out, preferred_element_type=jnp.float32
    ).astype(jnp.bfloat16)
    panel_rows = lax.all_gather(own_panel, "row", axis=0, tiled=True)
    gathered = panel_rows.reshape(panel_rows.shape[0] // tile_size, tile_size, feat_width)[col_ids]
    products = jnp.einsum("tij,tjf->tif", tile_data, gathered, preferred_element_type=jnp.float32)
    is_live = jnp.arange(tile_data.shape[0], dtype=jnp.int32) < live_count
    block_rows = masked.shape[0] * lax.axis_size("col")
    first_tile = 0 // tile_size
    tile_span = block_rows // tile_size
    wanted = first_tile + jnp.arange(tile_span, dtype=jnp.int32)
    picker = ((row_ids[None, :] == wanted[:, None]) & is_live[None, :]).astype(jnp.float32)
    placed = jnp.einsum("kt,tif->kif", picker, products, precision=lax.Precision.HIGHEST)
    summed = lax.psum_scatter(
        placed.reshape(block_rows, feat_width).astype(jnp.bfloat16),
        "col",
        scatter_dimension=0,
        tiled=True,
    )
    local_weight = lax.dot_general(
        aggregated, masked, (((0,), (0,)), ((), ())), preferred_element_type=jnp.float32
    )
    grad_weight = lax.psum(local_weight, ("row", "col"))
    return (summed, grad_weight)


def solution(mesh):
    placed = (
        P(("col", "row"), None),
        P(("col", "row"), None),
        P(("col", "row"), "depth"),
        P("depth", None),
        P("row", "col", None, None, None),
        P("row", "col", None),
        P("row", "col", None),
        P("row", "col"),
    )
    return jax.shard_map(
        shards,
        mesh=mesh,
        in_specs=placed,
        out_specs=(P(("row", "col"), "depth"), P("depth", None)),
        check_vma=False,
    )
```

profile of v0, /device:TPU:6, one launch (start us, length us, event | category | flops | bytes accessed | tf_op | source)
XLA Modules:
  0.0 376.5 jit_solution(17319955551205198664)
XLA Ops:
  8.0 0.0 copy-start
  8.0 0.0 all-reduce.2.cloned.1.call-start
  8.1 2.6 convolution_bitcast_fusion
  10.6 0.0 all-reduce.2.cloned.1.call-update
  10.6 0.0 reduce-scatter.2.cloned.1.call-start
  10.7 0.0 copy-done
  10.7 1.7 convolution_convert_fusion
  12.4 53.7 %all_gather.3 = bf16[2048,128]{1,0:T(8,128)(2,1)S(1)} all-gather(bf16[256,128]{1,0:T(8,128)(2,1)S(1)} %convolution_convert_fusion), channel_id=1, replica_groups=mesh['row'=8,'col'=16,'depth'=8] {'row'}, dimensions={0}, use_global_device_ids=true | all-gather | bytes 589824 | tf_op jit(solution)/shard_map/all_gather | solution.py:19
  66.1 0.7 compare_select_fusion
  67.4 7.8 %gather_fusion = bf16[160,128,128]{2,1,0:T(8,128)(2,1)} fusion(bf16[16,128,128]{2,1,0:T(8,128)(2,1)S(1)} %bitcast.24, s32[1024]{0:T(1024)S(1)} %pad_clamp_fusion), kind=kCustom, calls=%fused_computation | custom fusion | bytes 10486400 | tf_op jit(solution)/shard_map/gather | solution.py:20
  75.2 11.9 %fusion.2 = f32[160,128,128]{2,1,0:T(8,128)} fusion(bf16[160,128,128]{2,1,0:T(8,128)(2,1)} %gather_fusion, bf16[1,1,160,128,128]{4,3,2,1,0:T(8,128)(2,1)} %param.12), kind=kOutput, calls=%fused_computation.3 | convolution fusion | flops 671088640 | bytes 20971520 | tf_op jit(solution)/shard_map/tij,tjf->tif/dot_general | solution.py:21
  87.0 0.0 copy-start.1
  87.0 11.6 %copy.13 = f32[160,128,128]{1,0,2:T(8,128)} copy(f32[160,128,128]{2,1,0:T(8,128)} %fusion.2) | data formatting | bytes 20971520 | tf_op jit(solution)/shard_map/tij,tjf->tif/dot_general | solution.py:21
  98.6 0.0 copy-done.1
  98.6 7.9 %fusion.4 = bf16[32,128,128]{2,0,1:T(8,128)(2,1)S(1)} fusion(f32[160,128,128]{1,0,2:T(8,128)} %copy.13, s32[160]{0:T(256)S(1)} %bitcast.27, pred[160]{0:T(512)(128)(4,1)S(1)} %iota_compare_fusion.1), kind=kOutput, calls=%fused_computation.5 | convolution fusion | flops 1007167488 | bytes 11535136 | tf_op jit(solution)/shard_map/kt,tif->kif/dot_general | solution.py:28
  106.5 1.4 copy.11
  107.9 0.0 reduce-scatter.2.cloned.1.call-update
  107.9 190.1 %all-reduce.2.cloned.1.call-done = f32[128,1024]{0,1:T(8,128)} async-done(((f32[128,1024]{0,1:T(8,128)}), f32[128,1024]{0,1:T(8,128)}) %all-reduce.2.cloned.1.call-update) | async-done | bytes 524304 | tf_op jit(solution)/shard_map/psum | solution.py:38
  298.0 2.0 copy.12
  300.1 69.0 %reduce-scatter.2.cloned.1.call-done = bf16[256,128]{1,0:T(8,128)(2,1)} async-done(((bf16[4096,128]{1,0:T(8,128)(2,1)}), bf16[256,128]{1,0:T(8,128)(2,1)}) %reduce-scatter.2.cloned.1.call-update) | async-done | bytes 65552 | tf_op jit(solution)/shard_map/reduce_scatter | solution.py:29
  (2 shorter events, 0.0 us)
Async XLA Ops:
  8.0 2.7 copy-start
  8.0 290.0 %all-reduce.2.cloned.1.call-start = ((), (), s32[]{:S(2)}) async-start(), calls=%async_computation.2 | async-start | bytes 1048576 | tf_op jit(solution)/shard_map/psum | solution.py:38
  10.6 358.5 %reduce-scatter.2.cloned.1.call-start = ((), (), s32[]{:S(2)}) async-start(), calls=%async_computation.1 | async-start | bytes 1114112 | tf_op jit(solution)/shard_map/reduce_scatter | solution.py:29
  87.0 11.6 %copy-start.1 = (s32[1,1,160]{2,1,0:T(1,128)S(1)}, s32[1,1,160]{2,1,0:T(1,128)}, u32[]{:S(2)}) copy-start(s32[1,1,160]{2,1,0:T(1,128)} %param.13) | copy-start | bytes 1924
Sparse Core Ops, SparseCore 0:
  13.3 284.7 all-reduce.1
Sparse Core Ops, SparseCore 1:
  108.0 261.0 reduce-scatter.1
where the time goes:
time: 377 us
  waiting for transfers between devices  259 us (69%)
  blocking collectives  53.7 us (14%)
  matrix products  24 us (6%)
  local copies, waits for them, and re-layouts  22.8 us (6%)
  between operations  16.2 us (4%)
    psum x1, waiting for transfers between devices, shards(): grad_weight = lax.psum(local_weight, ('row', 'col'))  190 us
    reduce_scatter x1, waiting for transfers between devices, shards(): lax.psum_scatter(placed.reshape(block_rows, feat_width).astype(jnp.bfloat...  69 us
    all_gather x1, blocking collectives, shards(): panel_rows = lax.all_gather(own_panel, 'row', axis=0, tiled=True)  53.7 us
    dot_general x1, matrix products, shards(): jnp.einsum('tij,tjf->tif', tile_data, gathered, preferred_element_type=jn...  11.9 us
    dot_general x1, local copies, waits for them, and re-layouts, shards(): jnp.einsum('tij,tjf->tif', tile_data, gathered, preferred_element_type=jn...  11.6 us
    dot_general x1, matrix products, shards(): jnp.einsum('kt,tif->kif', picker, products, precision=lax.Precision.HIGHEST)  7.91 us
    gather x1, local copies, waits for them, and re-layouts, shards(): panel_rows.reshape(panel_rows.shape[0] // tile_size, tile_size, feat_width)  7.76 us
  transfers between devices with their start and end apart: 2, of which 2 were waited for; matrix products, arithmetic and copies ran while one was open for 12% of the time, Pallas kernels for 0%

commit v1 on v0

v1 whole, which is shorter than its diff:
```python
import jax
import jax.numpy as jnp
from jax import lax
from jax.experimental import pallas as pl
from jax.experimental.pallas import tpu as pltpu
from jax.sharding import PartitionSpec as P

LANES = 128
GROUP = 8
CHUNK = 16
VMEM = pl.BlockSpec(memory_space=pltpu.VMEM)
SMEM = pl.BlockSpec(memory_space=pltpu.SMEM)
HBM = pl.BlockSpec(memory_space=pl.ANY)


def params(mib):
    return pltpu.CompilerParams(vmem_limit_bytes=mib * 2**20)


def cost(flops, moved):
    return pl.CostEstimate(flops=flops, bytes_accessed=moved, transcendentals=0)


def panel_kernel(grad_ref, mask_ref, weight_ref, panel_ref, masked_ref):
    masked = grad_ref[...] * mask_ref[...].astype(jnp.float32).astype(jnp.bfloat16)
    masked_ref[...] = masked
    panel_ref[...] = lax.dot_general(
        masked, weight_ref[...], (((1,), (1,)), ((), ())), preferred_element_type=jnp.float32
    ).astype(jnp.bfloat16)


def weight_kernel(aggregated_ref, masked_ref, out_ref):
    flipped = aggregated_ref[...].T
    feats = flipped.shape[0]
    for j in range(masked_ref.shape[1] // LANES):
        term = jnp.dot(
            flipped, masked_ref[:, j * LANES : (j + 1) * LANES], preferred_element_type=jnp.float32
        )
        out_ref[j * feats : (j + 1) * feats, :] = term.astype(jnp.bfloat16)


def tiles_kernel(
    live_ref, row_ref, col_ref, tiles_hbm, near, four, two, one, weight_term, out_ref,
    tiles, panel, total, arrived,
):
    slots, size = tiles.shape[0], tiles.shape[1]
    copies = []
    for k in range(slots // CHUNK):
        part = pl.ds(k * CHUNK, CHUNK)
        copies.append(pltpu.make_async_copy(tiles_hbm.at[part], tiles.at[part], arrived.at[k]))
        copies[-1].start()
    total[...] = jnp.zeros_like(total)
    place = 0
    for part in (near, four, two, one):
        for k in range(part.shape[0] // size):
            panel[place] = part[k * size : (k + 1) * size, :]
            place += 1
    live = live_ref[0]

    def group(g, carry):
        first = g * GROUP
        terms = []
        for u in range(GROUP):
            terms.append(
                jnp.dot(
                    tiles[first + u], panel[col_ref[first + u]], preferred_element_type=jnp.float32
                )
            )
        for u in range(GROUP):
            r = row_ref[first + u]
            total[r] = total[r] + terms[u]
        return carry

    for k in range(slots // CHUNK):
        copies[k].wait()
        last = jnp.minimum((k + 1) * CHUNK, live)
        lax.fori_loop(k * CHUNK // GROUP, (last + GROUP - 1) // GROUP, group, 0)
    owners, height = out_ref.shape[0], out_ref.shape[1]
    extra = weight_term.shape[0]
    own = height - extra
    for c in range(owners):
        for k in range(own // size):
            out_ref[c, k * size : (k + 1) * size, :] = total[c * (own // size) + k].astype(
                jnp.bfloat16
            )
        out_ref[c, own:, :] = weight_term[...]


def finish_kernel(got_ref, features_ref, weight_ref):
    owners, height = got_ref.shape[0], got_ref.shape[1]
    own, feats = features_ref.shape[0], weight_ref.shape[0]
    extra = height - own
    for k in range(own // feats):
        rows = slice(k * feats, (k + 1) * feats)
        acc = got_ref[0, rows, :].astype(jnp.float32)
        for c in range(1, owners):
            acc = acc + got_ref[c, rows, :].astype(jnp.float32)
        features_ref[rows, :] = acc.astype(jnp.bfloat16)
    step = min(extra, feats)
    for g in range(0, owners * extra, step):
        c, at = g // extra, g % extra
        j, f = g // feats, g % feats
        weight_ref[f : f + step, j * LANES : (j + 1) * LANES] = got_ref[
            c, own + at : own + at + step, :
        ].astype(jnp.float32)


def shards(grad_out, relu_mask, aggregated, weight, adj_tiles, tile_row, tile_col, tile_count):
    n_row, n_col = lax.axis_size("row"), lax.axis_size("col")
    nodes, width = grad_out.shape
    feats = weight.shape[0]
    tile_data = adj_tiles[0, 0]
    slots, size = tile_data.shape[0], tile_data.shape[1]
    block_tiles = nodes * n_col // size
    per_owner = nodes // size
    bf, f32 = jnp.bfloat16, jnp.float32

    def swap(value, mask):
        return lax.ppermute(value, "row", [(i, i ^ mask) for i in range(n_row)])

    near, masked = pl.pallas_call(
        panel_kernel,
        out_shape=(
            jax.ShapeDtypeStruct((nodes, feats), bf),
            jax.ShapeDtypeStruct((nodes, width), bf),
        ),
        in_specs=[VMEM] * 3,
        out_specs=(VMEM, VMEM),
        compiler_params=params(16),
        cost_estimate=cost(2 * nodes * width * feats, nodes * width * 8),
    )(grad_out, relu_mask, weight)

    four = swap(near, 4)

    term = pl.pallas_call(
        weight_kernel,
        out_shape=jax.ShapeDtypeStruct((width // LANES * feats, LANES), bf),
        in_specs=[VMEM] * 2,
        out_specs=VMEM,
        compiler_params=params(16),
        cost_estimate=cost(2 * nodes * width * feats, nodes * width * 4),
    )(aggregated, masked)
    extra = term.shape[0] // n_col
    spread = lax.all_to_all(term.reshape(n_col, extra, LANES), "col", 0, 0, tiled=True)
    share = jnp.sum(spread.astype(f32), axis=0)

    two = swap(jnp.concatenate([near, four]), 2)
    share = share + swap(share, 4)
    one = swap(jnp.concatenate([near, four, two]), 1)
    share = share + swap(share, 2)
    share = share + swap(share, 1)

    live = tile_count[0, 0]
    away = (tile_col[0, 0] * size // nodes) ^ lax.axis_index("row")
    chunk = (away & 1) * 4 + (away & 2) + (away >> 2)
    col_at = chunk * per_owner + tile_col[0, 0] % per_owner
    row_at = jnp.where(jnp.arange(slots, dtype=jnp.int32) < live, tile_row[0, 0], block_tiles)

    sent = pl.pallas_call(
        tiles_kernel,
        out_shape=jax.ShapeDtypeStruct((n_col, nodes + extra, feats), bf),
        in_specs=[SMEM] * 3 + [HBM] + [VMEM] * 5,
        out_specs=VMEM,
        scratch_shapes=[
            pltpu.VMEM((slots, size, size), bf),
            pltpu.VMEM((n_row * per_owner, size, feats), bf),
            pltpu.VMEM((block_tiles + 1, size, feats), f32),
            pltpu.SemaphoreType.DMA((slots // CHUNK,)),
        ],
        compiler_params=params(32),
        cost_estimate=cost(2 * slots * size * size * feats, slots * size * size * 2),
    )(live.reshape(1), row_at, col_at, tile_data, near, four, two, one, share.astype(bf))
    got = lax.all_to_all(sent, "col", 0, 0, tiled=True)
    return pl.pallas_call(
        finish_kernel,
        out_shape=(
            jax.ShapeDtypeStruct((nodes, feats), bf),
            jax.ShapeDtypeStruct((feats, width), f32),
        ),
        in_specs=[VMEM],
        out_specs=(VMEM, VMEM),
        compiler_params=params(16),
        cost_estimate=cost(nodes * feats * n_col, nodes * feats * n_col * 2),
    )(got)


def solution(mesh):
    placed = (
        P(("col", "row"), None),
        P(("col", "row"), None),
        P(("col", "row"), "depth"),
        P("depth", None),
        P("row", "col", None, None, None),
        P("row", "col", None),
        P("row", "col", None),
        P("row", "col"),
    )
    return jax.shard_map(
        shards,
        mesh=mesh,
        in_specs=placed,
        out_specs=(P(("row", "col"), "depth"), P("depth", None)),
        check_vma=False,
    )
```

time: 377 us -> 163 us (0.43)
  the two profiles are of different devices: /device:TPU:6 before, /device:TPU:256 now
where the time goes in v1:
time: 163 us
  blocking collectives  82.4 us (51%)
  starting transfers between devices  39.9 us (24%)
  waiting for transfers between devices  28.1 us (17%)
  local copies, waits for them, and re-layouts  6.21 us (4%)
  Pallas kernels  4.45 us (3%)
    all_to_all x1, blocking collectives, shards(): got = lax.all_to_all(sent, 'col', 0, 0, tiled=True)  82.4 us
    ppermute x6, waiting for transfers between devices, swap(): return lax.ppermute(value, 'row', [(i, i ^ mask) for i in range(n_row)])  21.6 us
    ppermute x6, starting transfers between devices, swap(): return lax.ppermute(value, 'row', [(i, i ^ mask) for i in range(n_row)])  20.6 us
    all_to_all x1, starting transfers between devices, shards(): lax.all_to_all(term.reshape(n_col, extra, LANES), 'col', 0, 0, tiled=True)  19.3 us
    all_to_all x1, waiting for transfers between devices, shards(): lax.all_to_all(term.reshape(n_col, extra, LANES), 'col', 0, 0, tiled=True)  6.55 us
    unnamed x14, local copies, waits for them, and re-layouts  6.21 us
  transfers between devices with their start and end apart: 7, of which 4 were waited for; matrix products, arithmetic and copies ran while one was open for 0% of the time, Pallas kernels for 0%

profile of v1, /device:TPU:256, one launch (start us, length us, event | category | flops | bytes accessed | tf_op | source)
XLA Modules:
  0.0 162.6 jit_solution(5244576550682979795)
XLA Ops:
  0.6 0.0 copy-start.1
  0.6 1.2 copy-done.1
  1.9 0.0 copy-start.2
  1.9 1.0 copy-done.2
  2.9 0.0 copy-start.3
  2.9 0.9 copy-done.3
  3.8 0.0 copy-start.4
  3.9 0.3 shard_map.95
  4.2 0.5 copy-done.4
  4.7 0.0 copy-start.5
  4.7 1.0 shard_map.96
  5.7 19.3 %all-to-all-start = ((bf16[16,64,128]{2,1,0:T(8,128)(2,1)}), bf16[16,64,128]{2,1,0:T(8,128)(2,1)S(1)}, u32[]{:S(2)}, u32[]{:S(2)}) async-start(bf16[16,64,128]{2,1,0:T(8,128)(2,1)} %bitcast.5), calls=%async_computation | async-start | bytes 524288 | tf_op jit(solution)/shard_map/all_to_all | solution.py:144
  25.0 3.6 %collective-permute-start = (bf16[256,128]{1,0:T(8,128)(2,1)S(1)}, bf16[256,128]{1,0:T(8,128)(2,1)S(1)}, u32[]{:S(2)}, u32[]{:S(2)}) collective-permute-start(bf16[256,128]{1,0:T(8,128)(2,1)S(1)} %get-tuple-element.4.near), channel_id=1, source_target_pairs={{0,512},{128,640},{256,768},{384,896},{512,0},{640,128},{768,256},... | collective-permute-start | bytes 196616 | tf_op jit(solution)/shard_map/ppermute | solution.py:119
  28.7 12.6 %collective-permute-done.four = bf16[256,128]{1,0:T(8,128)(2,1)S(1)} collective-permute-done((bf16[256,128]{1,0:T(8,128)(2,1)S(1)}, bf16[256,128]{1,0:T(8,128)(2,1)S(1)}, u32[]{:S(2)}, u32[]{:S(2)}) %collective-permute-start) | collective-permute-done | bytes 65568 | tf_op jit(solution)/shard_map/ppermute | solution.py:119
  41.3 1.9 %collective-permute-start.1 = (bf16[512,128]{1,0:T(8,128)(2,1)S(1)}, bf16[512,128]{1,0:T(8,128)(2,1)S(1)}, u32[]{:S(2)}, u32[]{:S(2)}) collective-permute-start(bf16[512,128]{1,0:T(8,128)(2,1)S(1)} %pad_maximum_fusion.1), channel_id=1, source_target_pairs={{0,256},{128,384},{256,0},{384,128},{512,768},{640,896},{768,512},... | collective-permute-start | bytes 393224 | tf_op jit(solution)/shard_map/ppermute | solution.py:119
  43.2 6.5 %all-to-all-done = bf16[16,64,128]{2,1,0:T(8,128)(2,1)S(1)} async-done(((bf16[16,64,128]{2,1,0:T(8,128)(2,1)}), bf16[16,64,128]{2,1,0:T(8,128)(2,1)S(1)}, u32[]{:S(2)}, u32[]{:S(2)}) %all-to-all-start) | async-done | bytes 262176 | tf_op jit(solution)/shard_map/all_to_all | solution.py:144
  49.8 3.4 %collective-permute-start.3 = (f32[64,128]{1,0:T(8,128)S(1)}, f32[64,128]{1,0:T(8,128)S(1)}, u32[]{:S(2)}, u32[]{:S(2)}) collective-permute-start(f32[64,128]{1,0:T(8,128)S(1)} %convert_reduce_fusion), channel_id=1, source_target_pairs={{0,512},{128,640},{256,768},{384,896},{512,0},{640,128},{768,256},... | collective-permute-start | bytes 98312 | tf_op jit(solution)/shard_map/ppermute | solution.py:119
  53.9 5.7 %collective-permute-done.3 = f32[64,128]{1,0:T(8,128)S(1)} collective-permute-done((f32[64,128]{1,0:T(8,128)S(1)}, f32[64,128]{1,0:T(8,128)S(1)}, u32[]{:S(2)}, u32[]{:S(2)}) %collective-permute-start.3) | collective-permute-done | bytes 32800 | tf_op jit(solution)/shard_map/ppermute | solution.py:119
  59.6 5.8 %collective-permute-start.4 = (f32[64,128]{1,0:T(8,128)S(1)}, f32[64,128]{1,0:T(8,128)S(1)}, u32[]{:S(2)}, u32[]{:S(2)}) collective-permute-start(f32[64,128]{1,0:T(8,128)S(1)} %add.29), channel_id=1, source_target_pairs={{0,256},{128,384},{256,0},{384,128},{512,768},{640,896},{768,512},... | collective-permute-start | bytes 98312 | tf_op jit(solution)/shard_map/ppermute | solution.py:119
  65.4 0.0 collective-permute-done.1.two
  65.4 1.9 %collective-permute-start.2 = (bf16[1024,128]{1,0:T(8,128)(2,1)S(1)}, bf16[1024,128]{1,0:T(8,128)(2,1)S(1)}, u32[]{:S(2)}, u32[]{:S(2)}) collective-permute-start(bf16[1024,128]{1,0:T(8,128)(2,1)S(1)} %pad_maximum_fusion), channel_id=1, source_target_pairs={{0,128},{128,0},{256,384},{384,256},{512,640},{640,512},{768,896},... | collective-permute-start | bytes 786440 | tf_op jit(solution)/shard_map/ppermute | solution.py:119
  67.4 0.0 collective-permute-done.4
  67.4 3.9 %collective-permute-start.5 = (f32[64,128]{1,0:T(8,128)S(1)}, f32[64,128]{1,0:T(8,128)S(1)}, u32[]{:S(2)}, u32[]{:S(2)}) collective-permute-start(f32[64,128]{1,0:T(8,128)S(1)} %add.30), channel_id=1, source_target_pairs={{0,128},{128,0},{256,384},{384,256},{512,640},{640,512},{768,896},... | collective-permute-start | bytes 98312 | tf_op jit(solution)/shard_map/ppermute | solution.py:119
  71.3 0.0 copy-done.5
  71.3 0.0 copy-done.6
  71.4 3.2 %collective-permute-done.5 = f32[64,128]{1,0:T(8,128)S(1)} collective-permute-done((f32[64,128]{1,0:T(8,128)S(1)}, f32[64,128]{1,0:T(8,128)S(1)}, u32[]{:S(2)}, u32[]{:S(2)}) %collective-permute-start.5) | collective-permute-done | bytes 32800 | tf_op jit(solution)/shard_map/ppermute | solution.py:119
  74.6 0.0 collective-permute-done.2.one
  74.6 0.0 copy-start
  74.6 2.5 %copy-done = bf16[1,1,160,128,128]{4,3,2,1,0:T(8,128)(2,1)S(1)} copy-done((bf16[1,1,160,128,128]{4,3,2,1,0:T(8,128)(2,1)S(1)}, bf16[1,1,160,128,128]{4,3,2,1,0:T(8,128)(2,1)}, u32[]{:S(2)}) %copy-start) | copy-done | bytes 5242904
  77.1 2.1 %shard_map.97 = bf16[16,320,128]{2,1,0:T(8,128)(2,1)S(1)} custom-call(s32[1]{0:T(128)} %bitcast.6.live_ref, s32[160]{0:T(256)S(1)} %get-tuple-element.6.row_ref, s32[160]{0:T(256)S(1)} %get-tuple-element.7.col_ref, bf16[160,128,128]{2,1,0:T(8,128)(2,1)S(1)} %bitcast.8, bf16[256,128]{1,0:T(8,128)(2,1)S(1)} %get-tuple-element.4.near, ...), custom_call_target="tpu_custom_call" | custom-call | flops 671088640 | bytes 5242880 | tf_op jit(solution)/shard_map/pallas_call | solution.py:159
  79.2 82.4 %all_to_all.10.got_ref = bf16[16,320,128]{2,1,0:T(8,128)(2,1)S(1)} all-to-all(bf16[16,320,128]{2,1,0:T(8,128)(2,1)S(1)} %shard_map.97), channel_id=1, replica_groups=mesh['row'=8,'col'=16,'depth'=8] {'col'}, dimensions={0} | all-to-all | bytes 2621440 | tf_op jit(solution)/shard_map/all_to_all | solution.py:173
  161.6 1.0 shard_map.98
  (8 shorter events, 0.1 us)
Async XLA Ops:
  0.6 1.2 copy-start.1
  1.9 1.0 copy-start.2
  2.9 0.9 copy-start.3
  3.8 0.8 copy-start.4
  4.7 66.6 %copy-start.5 = (s32[1,1,160]{2,1,0:T(1,128)S(1)}, s32[1,1,160]{2,1,0:T(1,128)}, u32[]{:S(2)}) copy-start(s32[1,1,160]{2,1,0:T(1,128)} %param.13) | copy-start | bytes 1924
  4.7 66.6 %copy-start.6 = (s32[1,1,160]{2,1,0:T(1,128)S(1)}, s32[1,1,160]{2,1,0:T(1,128)}, u32[]{:S(2)}) copy-start(s32[1,1,160]{2,1,0:T(1,128)} %param.14) | copy-start | bytes 1924
  5.7 44.1 %all-to-all-start = ((bf16[16,64,128]{2,1,0:T(8,128)(2,1)}), bf16[16,64,128]{2,1,0:T(8,128)(2,1)S(1)}, u32[]{:S(2)}, u32[]{:S(2)}) async-start(bf16[16,64,128]{2,1,0:T(8,128)(2,1)} %bitcast.5), calls=%async_computation | async-start | bytes 524288 | tf_op jit(solution)/shard_map/all_to_all | solution.py:144
  25.0 16.3 %collective-permute-start = (bf16[256,128]{1,0:T(8,128)(2,1)S(1)}, bf16[256,128]{1,0:T(8,128)(2,1)S(1)}, u32[]{:S(2)}, u32[]{:S(2)}) collective-permute-start(bf16[256,128]{1,0:T(8,128)(2,1)S(1)} %get-tuple-element.4.near), channel_id=1, source_target_pairs={{0,512},{128,640},{256,768},{384,896},{512,0},{640,128},{768,256},... | collective-permute-start | bytes 196616 | tf_op jit(solution)/shard_map/ppermute | solution.py:119
  41.3 24.1 %collective-permute-start.1 = (bf16[512,128]{1,0:T(8,128)(2,1)S(1)}, bf16[512,128]{1,0:T(8,128)(2,1)S(1)}, u32[]{:S(2)}, u32[]{:S(2)}) collective-permute-start(bf16[512,128]{1,0:T(8,128)(2,1)S(1)} %pad_maximum_fusion.1), channel_id=1, source_target_pairs={{0,256},{128,384},{256,0},{384,128},{512,768},{640,896},{768,512},... | collective-permute-start | bytes 393224 | tf_op jit(solution)/shard_map/ppermute | solution.py:119
  49.8 9.7 %collective-permute-start.3 = (f32[64,128]{1,0:T(8,128)S(1)}, f32[64,128]{1,0:T(8,128)S(1)}, u32[]{:S(2)}, u32[]{:S(2)}) collective-permute-start(f32[64,128]{1,0:T(8,128)S(1)} %convert_reduce_fusion), channel_id=1, source_target_pairs={{0,512},{128,640},{256,768},{384,896},{512,0},{640,128},{768,256},... | collective-permute-start | bytes 98312 | tf_op jit(solution)/shard_map/ppermute | solution.py:119
  59.6 7.8 %collective-permute-start.4 = (f32[64,128]{1,0:T(8,128)S(1)}, f32[64,128]{1,0:T(8,128)S(1)}, u32[]{:S(2)}, u32[]{:S(2)}) collective-permute-start(f32[64,128]{1,0:T(8,128)S(1)} %add.29), channel_id=1, source_target_pairs={{0,256},{128,384},{256,0},{384,128},{512,768},{640,896},{768,512},... | collective-permute-start | bytes 98312 | tf_op jit(solution)/shard_map/ppermute | solution.py:119
  65.4 9.1 %collective-permute-start.2 = (bf16[1024,128]{1,0:T(8,128)(2,1)S(1)}, bf16[1024,128]{1,0:T(8,128)(2,1)S(1)}, u32[]{:S(2)}, u32[]{:S(2)}) collective-permute-start(bf16[1024,128]{1,0:T(8,128)(2,1)S(1)} %pad_maximum_fusion), channel_id=1, source_target_pairs={{0,128},{128,0},{256,384},{384,256},{512,640},{640,512},{768,896},... | collective-permute-start | bytes 786440 | tf_op jit(solution)/shard_map/ppermute | solution.py:119
  67.4 7.2 %collective-permute-start.5 = (f32[64,128]{1,0:T(8,128)S(1)}, f32[64,128]{1,0:T(8,128)S(1)}, u32[]{:S(2)}, u32[]{:S(2)}) collective-permute-start(f32[64,128]{1,0:T(8,128)S(1)} %add.30), channel_id=1, source_target_pairs={{0,128},{128,0},{256,384},{384,256},{512,640},{640,512},{768,896},... | collective-permute-start | bytes 98312 | tf_op jit(solution)/shard_map/ppermute | solution.py:119
  74.6 2.5 %copy-start = (bf16[1,1,160,128,128]{4,3,2,1,0:T(8,128)(2,1)S(1)}, bf16[1,1,160,128,128]{4,3,2,1,0:T(8,128)(2,1)}, u32[]{:S(2)}) copy-start(bf16[1,1,160,128,128]{4,3,2,1,0:T(8,128)(2,1)} %param.12) | copy-start | bytes 15728644

commit v2 on v1

v2 whole, which is shorter than its diff:
```python
import jax
import jax.numpy as jnp
from jax import lax
from jax.experimental import pallas as pl
from jax.experimental.pallas import tpu as pltpu
from jax.sharding import PartitionSpec as P

LANES = 128
GROUP = 8
PAIR = 2
VMEM = pl.BlockSpec(memory_space=pltpu.VMEM)
SMEM = pl.BlockSpec(memory_space=pltpu.SMEM)
HBM = pl.BlockSpec(memory_space=pl.ANY)


def params(mib):
    return pltpu.CompilerParams(vmem_limit_bytes=int(mib * 2**20))


def cost(flops, moved):
    return pl.CostEstimate(flops=flops, bytes_accessed=moved, transcendentals=0)


def panel_kernel(grad_hbm, mask_hbm, weight_hbm, panel_ref, grad, mask, weight, arrived):
    copies = [
        pltpu.make_async_copy(mask_hbm, mask, arrived.at[0]),
        pltpu.make_async_copy(grad_hbm, grad, arrived.at[1]),
        pltpu.make_async_copy(weight_hbm, weight, arrived.at[2]),
    ]
    for copy in copies:
        copy.start()
    for copy in copies:
        copy.wait()
    masked = grad[...] * mask[...].astype(jnp.float32).astype(jnp.bfloat16)
    panel_ref[...] = lax.dot_general(
        masked, weight[...], (((1,), (1,)), ((), ())), preferred_element_type=jnp.float32
    ).astype(jnp.bfloat16)


def weight_kernel(
    grad_hbm, mask_hbm, aggregated_hbm, after_ref, out_ref, grad, mask, aggregated, arrived
):
    copies = [
        pltpu.make_async_copy(mask_hbm, mask, arrived.at[0]),
        pltpu.make_async_copy(grad_hbm, grad, arrived.at[1]),
        pltpu.make_async_copy(aggregated_hbm, aggregated, arrived.at[2]),
    ]
    for copy in copies:
        copy.start()
    for copy in copies:
        copy.wait()
    flipped = aggregated[...].T
    feats = flipped.shape[0]
    for j in range(grad.shape[1] // LANES):
        part = slice(j * LANES, (j + 1) * LANES)
        masked = grad[:, part] * mask[:, part].astype(jnp.float32).astype(jnp.bfloat16)
        term = jnp.dot(flipped, masked, preferred_element_type=jnp.float32)
        out_ref[j * feats : (j + 1) * feats, :] = term.astype(jnp.bfloat16)


def pack_kernel(spread_ref, near, four, packed_ref):
    acc = spread_ref[0].astype(jnp.float32)
    for c in range(1, spread_ref.shape[0]):
        acc = acc + spread_ref[c].astype(jnp.float32)
    nodes = near.shape[0]
    packed_ref[0:nodes, :] = near[...]
    packed_ref[nodes : 2 * nodes, :] = four[...]
    packed_ref[2 * nodes :, :] = acc.astype(jnp.bfloat16)


def tiles_kernel(
    live_ref, row_ref, col_ref, tiles, near, four, got_1, got_2, got_3, out_ref, panel, total
):
    size = tiles.shape[1]
    total[...] = jnp.zeros_like(total)
    per_owner = near.shape[0] // size
    place = 0
    for part, count in (
        (near, per_owner),
        (four, per_owner),
        (got_1, 2 * per_owner),
        (got_2, 2 * per_owner),
        (got_3, 2 * per_owner),
    ):
        for k in range(count):
            panel[place] = part[k * size : (k + 1) * size, :]
            place += 1

    def group(g, carry):
        first = g * GROUP
        terms = []
        for u in range(GROUP):
            terms.append(
                jnp.dot(
                    tiles[first + u], panel[col_ref[first + u]], preferred_element_type=jnp.float32
                )
            )
        for u in range(GROUP):
            r = row_ref[first + u]
            total[r] = total[r] + terms[u]
        return carry

    lax.fori_loop(0, (live_ref[0] + GROUP - 1) // GROUP, group, 0)
    owners, height = out_ref.shape[0], out_ref.shape[1]
    for c in range(owners):
        for k in range(height // size):
            out_ref[c, k * size : (k + 1) * size, :] = total[c * (height // size) + k].astype(
                jnp.bfloat16
            )


def halves_kernel(half_ref, got_ref, keep_ref, send_ref, total):
    owners, height = got_ref.shape[0], got_ref.shape[1]
    for k in range(height // LANES):
        rows = slice(k * LANES, (k + 1) * LANES)
        acc = got_ref[0, rows, :].astype(jnp.float32)
        for c in range(1, owners):
            acc = acc + got_ref[c, rows, :].astype(jnp.float32)
        total[rows, :] = acc
    own = keep_ref.shape[0]
    half = half_ref[0]
    keep_ref[...] = total[pl.ds(pl.multiple_of(half * own, own), own), :]
    send_ref[...] = total[pl.ds(pl.multiple_of((1 - half) * own, own), own), :].astype(jnp.bfloat16)


def share_kernel(after_ref, own, got_4, got_pair, got_both, out_ref):
    f32 = jnp.float32
    total = (own[...].astype(f32) + got_4[...].astype(f32)) + (
        got_pair[...].astype(f32) + got_both[...].astype(f32)
    )
    total = total.astype(jnp.bfloat16)
    for c in range(out_ref.shape[0]):
        out_ref[c] = total


def finish_kernel(keep_ref, got_ref, shares_ref, features_ref, weight_ref):
    features_ref[...] = (keep_ref[...] + got_ref[...].astype(jnp.float32)).astype(jnp.bfloat16)
    owners, rows = shares_ref.shape[0], shares_ref.shape[1]
    feats = weight_ref.shape[0]
    for g in range(owners * rows // feats):
        c, at = g * feats // rows, g * feats % rows
        weight_ref[:, g * LANES : (g + 1) * LANES] = shares_ref[c, at : at + feats, :].astype(
            jnp.float32
        )


def shards(grad_out, relu_mask, aggregated, weight, adj_tiles, tile_row, tile_col, tile_count):
    n_row, n_col = lax.axis_size("row"), lax.axis_size("col")
    n_y = n_col // PAIR
    lines = [[y * PAIR + h for y in range(n_y)] for h in range(PAIR)]
    nodes, width = grad_out.shape
    feats = weight.shape[0]
    tile_data = adj_tiles[0, 0]
    slots, size = tile_data.shape[0], tile_data.shape[1]
    block_tiles = nodes * n_col // size
    per_owner = nodes // size
    bf, f32 = jnp.bfloat16, jnp.float32
    shape = jax.ShapeDtypeStruct

    def swap(value, mask):
        return lax.ppermute(value, "row", [(i, i ^ mask) for i in range(n_row)])

    def swap_pair(value, mask=0):
        if mask == 0:
            return lax.ppermute(value, "col", [(i, i ^ 1) for i in range(n_col)])
        count = n_row * n_col
        return lax.ppermute(
            value, ("row", "col"), [(i, i ^ (mask * n_col + 1)) for i in range(count)]
        )

    def line_all_to_all(value):
        return lax.all_to_all(value, "col", 0, 0, axis_index_groups=lines, tiled=True)

    near = pl.pallas_call(
        panel_kernel,
        out_shape=shape((nodes, feats), bf),
        in_specs=[HBM] * 3,
        out_specs=VMEM,
        scratch_shapes=[
            pltpu.VMEM((nodes, width), bf),
            pltpu.VMEM((nodes, width), jnp.int32),
            pltpu.VMEM((feats, width), bf),
            pltpu.SemaphoreType.DMA((3,)),
        ],
        compiler_params=params(53.75),
        cost_estimate=cost(2 * nodes * width * feats, nodes * width * 8),
    )(grad_out, relu_mask, weight)

    four = swap(near, 4)

    term = pl.pallas_call(
        weight_kernel,
        out_shape=shape((width // LANES * feats, LANES), bf),
        in_specs=[HBM] * 4,
        out_specs=VMEM,
        scratch_shapes=[
            pltpu.VMEM((nodes, width), bf),
            pltpu.VMEM((nodes, width), jnp.int32),
            pltpu.VMEM((nodes, feats), bf),
            pltpu.SemaphoreType.DMA((3,)),
        ],
        compiler_params=params(53),
        cost_estimate=cost(2 * 10**10, nodes * width * 4),
    )(grad_out, relu_mask, aggregated, near)
    spread = line_all_to_all(term.reshape(n_y, term.shape[0] // n_y, LANES))
    extra = spread.shape[1]
    packed = pl.pallas_call(
        pack_kernel,
        out_shape=shape((2 * nodes + extra, LANES), bf),
        in_specs=[VMEM] * 3,
        out_specs=VMEM,
        compiler_params=params(16),
        cost_estimate=cost(nodes * feats * n_y, nodes * feats * n_y * 2),
    )(spread, near, four)
    got_1, got_2, got_3 = swap(packed, 1), swap(packed, 2), swap(packed, 3)

    def tail(value):
        return value[2 * nodes :].astype(f32)

    share = ((tail(packed) + tail(got_1)) + (tail(got_2) + tail(got_3))).astype(bf)
    far_4, far_pair, far_both = swap(share, 4), swap_pair(share), swap_pair(share, 4)

    live = tile_count[0, 0]
    away = (tile_col[0, 0] * size // nodes) ^ lax.axis_index("row")
    chunk = (away & 3) * 2 + (away >> 2)
    col_at = chunk * per_owner + tile_col[0, 0] % per_owner
    row_at = jnp.where(jnp.arange(slots, dtype=jnp.int32) < live, tile_row[0, 0], block_tiles)

    sent = pl.pallas_call(
        tiles_kernel,
        out_shape=shape((n_y, PAIR * nodes, feats), bf),
        in_specs=[SMEM] * 3 + [VMEM] * 6,
        out_specs=VMEM,
        scratch_shapes=[
            pltpu.VMEM((n_row * per_owner, size, feats), bf),
            pltpu.VMEM((block_tiles + 1, size, feats), f32),
        ],
        compiler_params=params(32),
        cost_estimate=cost(2 * 10**10, slots * size * size * 2),
    )(live.reshape(1), row_at, col_at, tile_data, near, four, got_1, got_2, got_3)
    got = line_all_to_all(sent)
    half = (lax.axis_index("col") & (PAIR - 1)).astype(jnp.int32).reshape(1)
    keep, send = pl.pallas_call(
        halves_kernel,
        out_shape=(shape((nodes, feats), f32), shape((nodes, feats), bf)),
        in_specs=[SMEM, VMEM],
        out_specs=(VMEM, VMEM),
        scratch_shapes=[pltpu.VMEM((PAIR * nodes, feats), f32)],
        compiler_params=params(16),
        cost_estimate=cost(nodes * feats * n_col, nodes * feats * n_col * 2),
    )(half, got)
    other = swap_pair(send)
    whole = pl.pallas_call(
        share_kernel,
        out_shape=shape((n_y, extra, LANES), bf),
        in_specs=[HBM] + [VMEM] * 4,
        out_specs=VMEM,
        compiler_params=params(16),
        cost_estimate=cost(2 * 10**10, n_y * extra * LANES * 2),
    )(send, share, far_4, far_pair, far_both)
    shares = line_all_to_all(whole)
    return pl.pallas_call(
        finish_kernel,
        out_shape=(shape((nodes, feats), bf), shape((feats, width), f32)),
        in_specs=[VMEM] * 3,
        out_specs=(VMEM, VMEM),
        compiler_params=params(16),
        cost_estimate=cost(nodes * feats, feats * width * 6),
    )(keep, other, shares)


def solution(mesh):
    placed = (
        P(("col", "row"), None),
        P(("col", "row"), None),
        P(("col", "row"), "depth"),
        P("depth", None),
        P("row", "col", None, None, None),
        P("row", "col", None),
        P("row", "col", None),
        P("row", "col"),
    )
    return jax.shard_map(
        shards,
        mesh=mesh,
        in_specs=placed,
        out_specs=(P(("row", "col"), "depth"), P("depth", None)),
        check_vma=False,
    )
```

time: 163 us -> 118 us (0.72)
  the two profiles are of different devices: /device:TPU:256 before, /device:TPU:6 now
where the time goes in v2:
time: 118 us; the launch traced here: 117 us
  starting transfers between devices  81.5 us (69%)
  waiting for transfers between devices  20.5 us (17%)
  Pallas kernels  8.88 us (8%)
  local copies, waits for them, and re-layouts  4.37 us (4%)
  between operations  1.42 us (1%)
    ppermute x5, starting transfers between devices, swap(): return lax.ppermute(value, 'row', [(i, i ^ mask) for i in range(n_row)])  30.5 us
    all_to_all x3, starting transfers between devices, line_all_to_all(): lax.all_to_all(value, 'col', 0, 0, axis_index_groups=lines, tiled=True)  23.1 us
    ppermute x1, starting transfers between devices, swap_pair(): lax.ppermute(value, ('row', 'col'), [(i, i ^ mask * n_col + 1) for i in r...  15.1 us
    ppermute x2, starting transfers between devices, swap_pair(): return lax.ppermute(value, 'col', [(i, i ^ 1) for i in range(n_col)])  12.8 us
    ppermute x5, waiting for transfers between devices, swap(): return lax.ppermute(value, 'row', [(i, i ^ mask) for i in range(n_row)])  10.2 us
    ppermute x2, waiting for transfers between devices, swap_pair(): return lax.ppermute(value, 'col', [(i, i ^ 1) for i in range(n_col)])  7.22 us
    unnamed x10, local copies, waits for them, and re-layouts  4.37 us
    all_to_all x3, waiting for transfers between devices, line_all_to_all(): lax.all_to_all(value, 'col', 0, 0, axis_index_groups=lines, tiled=True)  3.08 us
  transfers between devices with their start and end apart: 11, of which 7 were waited for; matrix products, arithmetic and copies ran while one was open for 0% of the time, Pallas kernels for 0%

profile of v2, /device:TPU:6, one launch (start us, length us, event | category | flops | bytes accessed | tf_op | source)
XLA Modules:
  0.0 116.7 jit_solution(17206154045396100640)
XLA Ops:
  0.6 1.8 %shard_map.95.after_ref.near = bf16[256,128]{1,0:T(8,128)(2,1)S(1)} custom-call(bf16[256,1024]{1,0:T(8,128)(2,1)} %grad_hbm.3, s32[256,1024]{1,0:T(8,128)} %mask_hbm.3, bf16[128,1024]{1,0:T(8,128)(2,1)} %weight_hbm.1), custom_call_target="tpu_custom_call" | custom-call | flops 67108864 | bytes 2097152 | tf_op jit(solution)/shard_map/pallas_call | solution.py:174
  2.4 0.0 copy-start
  2.4 1.0 copy-done
  3.5 0.8 copy-done.2
  4.3 2.3 %shard_map.96 = bf16[1024,128]{1,0:T(8,128)(2,1)} custom-call(bf16[256,1024]{1,0:T(8,128)(2,1)S(1)} %copy-done, s32[256,1024]{1,0:T(8,128)} %mask_hbm.3, bf16[256,128]{1,0:T(8,128)(2,1)S(1)} %copy-done.2, bf16[256,128]{1,0:T(8,128)(2,1)S(1)} %shard_map.95.after_ref.near), custom_call_target="tpu_custom_call" | custom-call | flops 20000000000 | bytes 1048576 | tf_op jit(solution)/shard_map/pallas_call | solution.py:191
  6.6 7.1 %all-to-all-start = ((bf16[8,128,128]{2,1,0:T(8,128)(2,1)}), bf16[8,128,128]{2,1,0:T(8,128)(2,1)S(1)}, u32[]{:S(2)}, u32[]{:S(2)}) async-start(bf16[8,128,128]{2,1,0:T(8,128)(2,1)} %bitcast.6), calls=%async_computation | async-start | bytes 524288 | tf_op jit(solution)/shard_map/all_to_all | solution.py:172
  13.7 10.9 %collective-permute-start = (bf16[256,128]{1,0:T(8,128)(2,1)S(1)}, bf16[256,128]{1,0:T(8,128)(2,1)S(1)}, u32[]{:S(2)}, u32[]{:S(2)}) collective-permute-start(bf16[256,128]{1,0:T(8,128)(2,1)S(1)} %shard_map.95.after_ref.near), channel_id=1, source_target_pairs={{0,512},{128,640},{256,768},{384,896},{512,0},{640,128},{768,256},... | collective-permute-start | bytes 196616 | tf_op jit(solution)/shard_map/ppermute | solution.py:161
  25.3 1.6 %collective-permute-done.four = bf16[256,128]{1,0:T(8,128)(2,1)S(1)} collective-permute-done((bf16[256,128]{1,0:T(8,128)(2,1)S(1)}, bf16[256,128]{1,0:T(8,128)(2,1)S(1)}, u32[]{:S(2)}, u32[]{:S(2)}) %collective-permute-start) | collective-permute-done | bytes 65568 | tf_op jit(solution)/shard_map/ppermute | solution.py:161
  26.9 0.0 all-to-all-done.spread_ref
  26.9 8.4 %collective-permute-start.3 = (bf16[640,128]{1,0:T(8,128)(2,1)S(1)}, bf16[640,128]{1,0:T(8,128)(2,1)S(1)}, u32[]{:S(2)}, u32[]{:S(2)}) collective-permute-start(bf16[640,128]{1,0:T(8,128)(2,1)S(1)} %shard_map.97), channel_id=1, source_target_pairs={{0,384},{128,256},{256,128},{384,0},{512,896},{640,768},{768,640},... | collective-permute-start | bytes 491528 | tf_op jit(solution)/shard_map/ppermute | solution.py:161
  35.3 1.9 %collective-permute-start.2 = (bf16[640,128]{1,0:T(8,128)(2,1)S(1)}, bf16[640,128]{1,0:T(8,128)(2,1)S(1)}, u32[]{:S(2)}, u32[]{:S(2)}) collective-permute-start(bf16[640,128]{1,0:T(8,128)(2,1)S(1)} %shard_map.97), channel_id=1, source_target_pairs={{0,256},{128,384},{256,0},{384,128},{512,768},{640,896},{768,512},... | collective-permute-start | bytes 491528 | tf_op jit(solution)/shard_map/ppermute | solution.py:161
  37.3 2.5 %collective-permute-start.1 = (bf16[640,128]{1,0:T(8,128)(2,1)S(1)}, bf16[640,128]{1,0:T(8,128)(2,1)S(1)}, u32[]{:S(2)}, u32[]{:S(2)}) collective-permute-start(bf16[640,128]{1,0:T(8,128)(2,1)S(1)} %shard_map.97), channel_id=1, source_target_pairs={{0,128},{128,0},{256,384},{384,256},{512,640},{640,512},{768,896},... | collective-permute-start | bytes 491528 | tf_op jit(solution)/shard_map/ppermute | solution.py:161
  39.8 0.7 collective-permute-done.3.got_3
  40.5 7.5 %collective-permute-done.2.got_2 = bf16[640,128]{1,0:T(8,128)(2,1)S(1)} collective-permute-done((bf16[640,128]{1,0:T(8,128)(2,1)S(1)}, bf16[640,128]{1,0:T(8,128)(2,1)S(1)}, u32[]{:S(2)}, u32[]{:S(2)}) %collective-permute-start.2) | collective-permute-done | bytes 163872 | tf_op jit(solution)/shard_map/ppermute | solution.py:161
  47.9 0.5 collective-permute-done.1.got_1
  48.4 2.5 %copy-done.1 = bf16[1,1,160,128,128]{4,3,2,1,0:T(8,128)(2,1)S(1)} copy-done((bf16[1,1,160,128,128]{4,3,2,1,0:T(8,128)(2,1)S(1)}, bf16[1,1,160,128,128]{4,3,2,1,0:T(8,128)(2,1)}, u32[]{:S(2)}) %copy-start.1) | copy-done | bytes 5242904
  50.9 3.0 %shard_map.98 = bf16[8,512,128]{2,1,0:T(8,128)(2,1)} custom-call(s32[1]{0:T(128)} %bitcast.7.live_ref, s32[160]{0:T(256)S(1)} %get-tuple-element.6.row_ref, s32[160]{0:T(256)S(1)} %get-tuple-element.7.col_ref, bf16[160,128,128]{2,1,0:T(8,128)(2,1)S(1)} %bitcast.9, bf16[256,128]{1,0:T(8,128)(2,1)S(1)} %shard_map.95.after_ref.near, ...), custom_call_target="tpu_custom_call" | custom-call | flops 20000000000 | bytes 5242880 | tf_op jit(solution)/shard_map/pallas_call | solution.py:229
  53.9 8.8 %all-to-all-start.1 = ((bf16[8,512,128]{2,1,0:T(8,128)(2,1)}), bf16[8,512,128]{2,1,0:T(8,128)(2,1)S(1)}, u32[]{:S(2)}, u32[]{:S(2)}) async-start(bf16[8,512,128]{2,1,0:T(8,128)(2,1)} %shard_map.98), calls=%async_computation.1 | async-start | bytes 2097152 | tf_op jit(solution)/shard_map/all_to_all | solution.py:172
  62.7 15.1 %collective-permute-start.7 = (bf16[128,128]{1,0:T(8,128)(2,1)S(1)}, bf16[128,128]{1,0:T(8,128)(2,1)S(1)}, u32[]{:S(2)}, u32[]{:S(2)}) collective-permute-start(bf16[128,128]{1,0:T(8,128)(2,1)S(1)} %add_convert_fusion.own), channel_id=1, source_target_pairs={{0,520},{8,512},{16,536},{24,528},{32,552},{40,544},{48,568},{56,5... | collective-permute-start | bytes 98312 | tf_op jit(solution)/shard_map/ppermute | solution.py:167
  77.8 2.4 %collective-permute-start.6 = (bf16[128,128]{1,0:T(8,128)(2,1)S(1)}, bf16[128,128]{1,0:T(8,128)(2,1)S(1)}, u32[]{:S(2)}, u32[]{:S(2)}) collective-permute-start(bf16[128,128]{1,0:T(8,128)(2,1)S(1)} %add_convert_fusion.own), channel_id=1, source_target_pairs={{0,8},{8,0},{16,24},{24,16},{32,40},{40,32},{48,56},{56,48},{64,72... | collective-permute-start | bytes 98312 | tf_op jit(solution)/shard_map/ppermute | solution.py:165
  80.2 6.8 %collective-permute-start.5 = (bf16[128,128]{1,0:T(8,128)(2,1)S(1)}, bf16[128,128]{1,0:T(8,128)(2,1)S(1)}, u32[]{:S(2)}, u32[]{:S(2)}) collective-permute-start(bf16[128,128]{1,0:T(8,128)(2,1)S(1)} %add_convert_fusion.own), channel_id=1, source_target_pairs={{0,512},{128,640},{256,768},{384,896},{512,0},{640,128},{768,256},... | collective-permute-start | bytes 98312 | tf_op jit(solution)/shard_map/ppermute | solution.py:161
  87.0 3.1 %all-to-all-done.1.got_ref = bf16[8,512,128]{2,1,0:T(8,128)(2,1)S(1)} async-done(((bf16[8,512,128]{2,1,0:T(8,128)(2,1)}), bf16[8,512,128]{2,1,0:T(8,128)(2,1)S(1)}, u32[]{:S(2)}, u32[]{:S(2)}) %all-to-all-start.1) | async-done | bytes 1048608 | tf_op jit(solution)/shard_map/all_to_all | solution.py:172
  90.1 0.1 shard_map.99
  90.2 0.0 collective-permute-done.7.got_both
  90.2 2.1 %collective-permute-done.6.got_pair = bf16[128,128]{1,0:T(8,128)(2,1)S(1)} collective-permute-done((bf16[128,128]{1,0:T(8,128)(2,1)S(1)}, bf16[128,128]{1,0:T(8,128)(2,1)S(1)}, u32[]{:S(2)}, u32[]{:S(2)}) %collective-permute-start.6) | collective-permute-done | bytes 32800 | tf_op jit(solution)/shard_map/ppermute | solution.py:165
  92.3 0.0 collective-permute-done.5.got_4
  92.3 0.7 shard_map.100
  93.0 7.2 %all-to-all-start.2 = ((bf16[8,128,128]{2,1,0:T(8,128)(2,1)}), bf16[8,128,128]{2,1,0:T(8,128)(2,1)S(1)}, u32[]{:S(2)}, u32[]{:S(2)}) async-start(bf16[8,128,128]{2,1,0:T(8,128)(2,1)} %shard_map.100), calls=%async_computation.2 | async-start | bytes 524288 | tf_op jit(solution)/shard_map/all_to_all | solution.py:172
  100.3 10.4 %collective-permute-start.4 = (bf16[256,128]{1,0:T(8,128)(2,1)S(1)}, bf16[256,128]{1,0:T(8,128)(2,1)S(1)}, u32[]{:S(2)}, u32[]{:S(2)}) collective-permute-start(bf16[256,128]{1,0:T(8,128)(2,1)S(1)} %get-tuple-element.5.after_ref), channel_id=1, source_target_pairs={{0,8},{8,0},{16,24},{24,16},{32,40},{40,32},{48,56},{56,48},{64,72... | collective-permute-start | bytes 196616 | tf_op jit(solution)/shard_map/ppermute | solution.py:165
  110.7 5.1 %collective-permute-done.4.got_ref = bf16[256,128]{1,0:T(8,128)(2,1)S(1)} collective-permute-done((bf16[256,128]{1,0:T(8,128)(2,1)S(1)}, bf16[256,128]{1,0:T(8,128)(2,1)S(1)}, u32[]{:S(2)}, u32[]{:S(2)}) %collective-permute-start.4) | collective-permute-done | bytes 65568 | tf_op jit(solution)/shard_map/ppermute | solution.py:165
  115.8 0.0 all-to-all-done.2.shares_ref
  115.8 0.9 shard_map.101
  (9 shorter events, 0.1 us)
Async XLA Ops:
  2.4 1.0 copy-start
  3.5 0.8 copy-start.2
  4.3 35.5 %copy-start.3 = (s32[1,1,160]{2,1,0:T(1,128)S(1)}, s32[1,1,160]{2,1,0:T(1,128)}, u32[]{:S(2)}) copy-start(s32[1,1,160]{2,1,0:T(1,128)} %param.13) | copy-start | bytes 1924
  4.3 35.5 %copy-start.4 = (s32[1,1,160]{2,1,0:T(1,128)S(1)}, s32[1,1,160]{2,1,0:T(1,128)}, u32[]{:S(2)}) copy-start(s32[1,1,160]{2,1,0:T(1,128)} %param.14) | copy-start | bytes 1924
  6.6 20.3 %all-to-all-start = ((bf16[8,128,128]{2,1,0:T(8,128)(2,1)}), bf16[8,128,128]{2,1,0:T(8,128)(2,1)S(1)}, u32[]{:S(2)}, u32[]{:S(2)}) async-start(bf16[8,128,128]{2,1,0:T(8,128)(2,1)} %bitcast.6), calls=%async_computation | async-start | bytes 524288 | tf_op jit(solution)/shard_map/all_to_all | solution.py:172
  13.7 13.2 %collective-permute-start = (bf16[256,128]{1,0:T(8,128)(2,1)S(1)}, bf16[256,128]{1,0:T(8,128)(2,1)S(1)}, u32[]{:S(2)}, u32[]{:S(2)}) collective-permute-start(bf16[256,128]{1,0:T(8,128)(2,1)S(1)} %shard_map.95.after_ref.near), channel_id=1, source_target_pairs={{0,512},{128,640},{256,768},{384,896},{512,0},{640,128},{768,256},... | collective-permute-start | bytes 196616 | tf_op jit(solution)/shard_map/ppermute | solution.py:161
  26.9 13.5 %collective-permute-start.3 = (bf16[640,128]{1,0:T(8,128)(2,1)S(1)}, bf16[640,128]{1,0:T(8,128)(2,1)S(1)}, u32[]{:S(2)}, u32[]{:S(2)}) collective-permute-start(bf16[640,128]{1,0:T(8,128)(2,1)S(1)} %shard_map.97), channel_id=1, source_target_pairs={{0,384},{128,256},{256,128},{384,0},{512,896},{640,768},{768,640},... | collective-permute-start | bytes 491528 | tf_op jit(solution)/shard_map/ppermute | solution.py:161
  35.3 12.6 %collective-permute-start.2 = (bf16[640,128]{1,0:T(8,128)(2,1)S(1)}, bf16[640,128]{1,0:T(8,128)(2,1)S(1)}, u32[]{:S(2)}, u32[]{:S(2)}) collective-permute-start(bf16[640,128]{1,0:T(8,128)(2,1)S(1)} %shard_map.97), channel_id=1, source_target_pairs={{0,256},{128,384},{256,0},{384,128},{512,768},{640,896},{768,512},... | collective-permute-start | bytes 491528 | tf_op jit(solution)/shard_map/ppermute | solution.py:161
  37.3 11.1 %collective-permute-start.1 = (bf16[640,128]{1,0:T(8,128)(2,1)S(1)}, bf16[640,128]{1,0:T(8,128)(2,1)S(1)}, u32[]{:S(2)}, u32[]{:S(2)}) collective-permute-start(bf16[640,128]{1,0:T(8,128)(2,1)S(1)} %shard_map.97), channel_id=1, source_target_pairs={{0,128},{128,0},{256,384},{384,256},{512,640},{640,512},{768,896},... | collective-permute-start | bytes 491528 | tf_op jit(solution)/shard_map/ppermute | solution.py:161
  48.4 2.5 %copy-start.1 = (bf16[1,1,160,128,128]{4,3,2,1,0:T(8,128)(2,1)S(1)}, bf16[1,1,160,128,128]{4,3,2,1,0:T(8,128)(2,1)}, u32[]{:S(2)}) copy-start(bf16[1,1,160,128,128]{4,3,2,1,0:T(8,128)(2,1)} %param.12) | copy-start | bytes 15728644
  53.9 36.2 %all-to-all-start.1 = ((bf16[8,512,128]{2,1,0:T(8,128)(2,1)}), bf16[8,512,128]{2,1,0:T(8,128)(2,1)S(1)}, u32[]{:S(2)}, u32[]{:S(2)}) async-start(bf16[8,512,128]{2,1,0:T(8,128)(2,1)} %shard_map.98), calls=%async_computation.1 | async-start | bytes 2097152 | tf_op jit(solution)/shard_map/all_to_all | solution.py:172
  62.7 27.6 %collective-permute-start.7 = (bf16[128,128]{1,0:T(8,128)(2,1)S(1)}, bf16[128,128]{1,0:T(8,128)(2,1)S(1)}, u32[]{:S(2)}, u32[]{:S(2)}) collective-permute-start(bf16[128,128]{1,0:T(8,128)(2,1)S(1)} %add_convert_fusion.own), channel_id=1, source_target_pairs={{0,520},{8,512},{16,536},{24,528},{32,552},{40,544},{48,568},{56,5... | collective-permute-start | bytes 98312 | tf_op jit(solution)/shard_map/ppermute | solution.py:167
  77.8 14.5 %collective-permute-start.6 = (bf16[128,128]{1,0:T(8,128)(2,1)S(1)}, bf16[128,128]{1,0:T(8,128)(2,1)S(1)}, u32[]{:S(2)}, u32[]{:S(2)}) collective-permute-start(bf16[128,128]{1,0:T(8,128)(2,1)S(1)} %add_convert_fusion.own), channel_id=1, source_target_pairs={{0,8},{8,0},{16,24},{24,16},{32,40},{40,32},{48,56},{56,48},{64,72... | collective-permute-start | bytes 98312 | tf_op jit(solution)/shard_map/ppermute | solution.py:165
  80.2 12.1 %collective-permute-start.5 = (bf16[128,128]{1,0:T(8,128)(2,1)S(1)}, bf16[128,128]{1,0:T(8,128)(2,1)S(1)}, u32[]{:S(2)}, u32[]{:S(2)}) collective-permute-start(bf16[128,128]{1,0:T(8,128)(2,1)S(1)} %add_convert_fusion.own), channel_id=1, source_target_pairs={{0,512},{128,640},{256,768},{384,896},{512,0},{640,128},{768,256},... | collective-permute-start | bytes 98312 | tf_op jit(solution)/shard_map/ppermute | solution.py:161
  93.0 22.8 %all-to-all-start.2 = ((bf16[8,128,128]{2,1,0:T(8,128)(2,1)}), bf16[8,128,128]{2,1,0:T(8,128)(2,1)S(1)}, u32[]{:S(2)}, u32[]{:S(2)}) async-start(bf16[8,128,128]{2,1,0:T(8,128)(2,1)} %shard_map.100), calls=%async_computation.2 | async-start | bytes 524288 | tf_op jit(solution)/shard_map/all_to_all | solution.py:172
  100.3 15.6 %collective-permute-start.4 = (bf16[256,128]{1,0:T(8,128)(2,1)S(1)}, bf16[256,128]{1,0:T(8,128)(2,1)S(1)}, u32[]{:S(2)}, u32[]{:S(2)}) collective-permute-start(bf16[256,128]{1,0:T(8,128)(2,1)S(1)} %get-tuple-element.5.after_ref), channel_id=1, source_target_pairs={{0,8},{8,0},{16,24},{24,16},{32,40},{40,32},{48,56},{56,48},{64,72... | collective-permute-start | bytes 196616 | tf_op jit(solution)/shard_map/ppermute | solution.py:165

commit v3 on v2

--- a/solution.py
+++ b/solution.py
@@ -7,6 +7,7 @@
 
 LANES = 128
 GROUP = 8
+CHUNK = 16
 PAIR = 2
 VMEM = pl.BlockSpec(memory_space=pltpu.VMEM)
 SMEM = pl.BlockSpec(memory_space=pltpu.SMEM)
@@ -58,33 +59,30 @@
         out_ref[j * feats : (j + 1) * feats, :] = term.astype(jnp.bfloat16)
 
 
-def pack_kernel(spread_ref, near, four, packed_ref):
+def sum_kernel(after_ref, spread_ref, out_ref):
     acc = spread_ref[0].astype(jnp.float32)
     for c in range(1, spread_ref.shape[0]):
         acc = acc + spread_ref[c].astype(jnp.float32)
-    nodes = near.shape[0]
-    packed_ref[0:nodes, :] = near[...]
-    packed_ref[nodes : 2 * nodes, :] = four[...]
-    packed_ref[2 * nodes :, :] = acc.astype(jnp.bfloat16)
+    out_ref[...] = acc.astype(jnp.bfloat16)
 
 
 def tiles_kernel(
-    live_ref, row_ref, col_ref, tiles, near, four, got_1, got_2, got_3, out_ref, panel, total
+    live_ref, row_ref, col_ref, tiles_hbm, near, four, got_1, got_2, got_3, out_ref,
+    tiles, panel, total, arrived,
 ):
-    size = tiles.shape[1]
+    slots, size = tiles.shape[0], tiles.shape[1]
+    copies = []
+    for k in range(slots // CHUNK):
+        part = pl.ds(k * CHUNK, CHUNK)
+        copies.append(pltpu.make_async_copy(tiles_hbm.at[part], tiles.at[part], arrived.at[k]))
+        copies[-1].start()
     total[...] = jnp.zeros_like(total)
-    per_owner = near.shape[0] // size
     place = 0
-    for part, count in (
-        (near, per_owner),
-        (four, per_owner),
-        (got_1, 2 * per_owner),
-        (got_2, 2 * per_owner),
-        (got_3, 2 * per_owner),
-    ):
-        for k in range(count):
+    for part in (near, four, got_1, got_2, got_3):
+        for k in range(part.shape[0] // size):
             panel[place] = part[k * size : (k + 1) * size, :]
             place += 1
+    live = live_ref[0]
 
     def group(g, carry):
         first = g * GROUP
@@ -100,7 +98,10 @@
             total[r] = total[r] + terms[u]
         return carry
 
-    lax.fori_loop(0, (live_ref[0] + GROUP - 1) // GROUP, group, 0)
+    for k in range(slots // CHUNK):
+        copies[k].wait()
+        last = jnp.minimum((k + 1) * CHUNK, live)
+        lax.fori_loop(k * CHUNK // GROUP, (last + GROUP - 1) // GROUP, group, 0)
     owners, height = out_ref.shape[0], out_ref.shape[1]
     for c in range(owners):
         for k in range(height // size):
@@ -133,8 +134,12 @@
         out_ref[c] = total
 
 
-def finish_kernel(keep_ref, got_ref, shares_ref, features_ref, weight_ref):
+def features_kernel(keep_ref, got_ref, features_ref, after_ref):
+    after_ref[...] = jnp.zeros_like(after_ref)
     features_ref[...] = (keep_ref[...] + got_ref[...].astype(jnp.float32)).astype(jnp.bfloat16)
+
+
+def spread_kernel(after_ref, shares_ref, weight_ref):
     owners, rows = shares_ref.shape[0], shares_ref.shape[1]
     feats = weight_ref.shape[0]
     for g in range(owners * rows // feats):
@@ -199,26 +204,13 @@
             pltpu.VMEM((nodes, feats), bf),
             pltpu.SemaphoreType.DMA((3,)),
         ],
-        compiler_params=params(53),
+        compiler_params=params(54),
         cost_estimate=cost(2 * 10**10, nodes * width * 4),
-    )(grad_out, relu_mask, aggregated, near)
+    )(grad_out, relu_mask, aggregated, four)
     spread = line_all_to_all(term.reshape(n_y, term.shape[0] // n_y, LANES))
     extra = spread.shape[1]
-    packed = pl.pallas_call(
-        pack_kernel,
-        out_shape=shape((2 * nodes + extra, LANES), bf),
-        in_specs=[VMEM] * 3,
-        out_specs=VMEM,
-        compiler_params=params(16),
-        cost_estimate=cost(nodes * feats * n_y, nodes * feats * n_y * 2),
-    )(spread, near, four)
+    packed = jnp.concatenate([near, four])
     got_1, got_2, got_3 = swap(packed, 1), swap(packed, 2), swap(packed, 3)
-
-    def tail(value):
-        return value[2 * nodes :].astype(f32)
-
-    share = ((tail(packed) + tail(got_1)) + (tail(got_2) + tail(got_3))).astype(bf)
-    far_4, far_pair, far_both = swap(share, 4), swap_pair(share), swap_pair(share, 4)
 
     live = tile_count[0, 0]
     away = (tile_col[0, 0] * size // nodes) ^ lax.axis_index("row")
@@ -229,16 +221,31 @@
     sent = pl.pallas_call(
         tiles_kernel,
         out_shape=shape((n_y, PAIR * nodes, feats), bf),
-        in_specs=[SMEM] * 3 + [VMEM] * 6,
+        in_specs=[SMEM] * 3 + [HBM] + [VMEM] * 5,
         out_specs=VMEM,
         scratch_shapes=[
+            pltpu.VMEM((slots, size, size), bf),
             pltpu.VMEM((n_row * per_owner, size, feats), bf),
             pltpu.VMEM((block_tiles + 1, size, feats), f32),
+            pltpu.SemaphoreType.DMA((slots // CHUNK,)),
         ],
-        compiler_params=params(32),
+        compiler_params=params(50),
         cost_estimate=cost(2 * 10**10, slots * size * size * 2),
     )(live.reshape(1), row_at, col_at, tile_data, near, four, got_1, got_2, got_3)
     got = line_all_to_all(sent)
+
+    share = pl.pallas_call(
+        sum_kernel,
+        out_shape=shape((extra, LANES), bf),
+        in_specs=[HBM, VMEM],
+        out_specs=VMEM,
+        compiler_params=params(16),
+        cost_estimate=cost(n_y * extra * LANES, n_y * extra * LANES * 2),
+    )(sent, spread)
+    row_1, row_2, row_3 = swap(share, 1), swap(share, 2), swap(share, 3)
+    share = ((share.astype(f32) + row_1.astype(f32)) + (row_2.astype(f32) + row_3.astype(f32))).astype(bf)
+    far_4, far_pair, far_both = swap(share, 4), swap_pair(share), swap_pair(share, 4)
+
     half = (lax.axis_index("col") & (PAIR - 1)).astype(jnp.int32).reshape(1)
     keep, send = pl.pallas_call(
         halves_kernel,
@@ -259,14 +266,23 @@
         cost_estimate=cost(2 * 10**10, n_y * extra * LANES * 2),
     )(send, share, far_4, far_pair, far_both)
     shares = line_all_to_all(whole)
-    return pl.pallas_call(
-        finish_kernel,
-        out_shape=(shape((nodes, feats), bf), shape((feats, width), f32)),
-        in_specs=[VMEM] * 3,
+    features, after = pl.pallas_call(
+        features_kernel,
+        out_shape=(shape((nodes, feats), bf), shape((8, LANES), f32)),
+        in_specs=[VMEM] * 2,
         out_specs=(VMEM, VMEM),
         compiler_params=params(16),
-        cost_estimate=cost(nodes * feats, feats * width * 6),
-    )(keep, other, shares)
+        cost_estimate=cost(2 * 10**10, nodes * feats * 4),
+    )(keep, other)
+    grad_weight = pl.pallas_call(
+        spread_kernel,
+        out_shape=shape((feats, width), f32),
+        in_specs=[HBM, VMEM],
+        out_specs=VMEM,
+        compiler_params=params(16),
+        cost_estimate=cost(feats * width, feats * width * 6),
+    )(after, shares)
+    return features, grad_weight
 
 
 def solution(mesh):

time: 118 us -> 119 us (level)
  local copies, waits for them, and re-layouts: 4.37 us -> 0.84 us
  Pallas kernels: 8.88 us -> 11.8 us
  starting transfers between devices: 81.5 us -> 84.4 us
  waiting for transfers between devices: 20.5 us -> 19 us
    all_to_all x3, waiting for transfers between devices: 3.08 us -> 15.1 us  [line_all_to_all(): lax.all_to_all(value, 'col', 0, 0, axis_index_groups=lines, tiled=True)]
    ppermute x5 -> x8, starting transfers between devices: 30.5 us -> 41.4 us  [swap(): return lax.ppermute(value, 'row', [(i, i ^ mask) for i in range(n_row)])]
    ppermute x2, waiting for transfers between devices: 7.22 us -> 0.01 us  [swap_pair(): return lax.ppermute(value, 'col', [(i, i ^ 1) for i in range(n_col)])]
    ppermute x5 -> x8, waiting for transfers between devices: 10.2 us -> 3.91 us  [swap(): return lax.ppermute(value, 'row', [(i, i ^ mask) for i in range(n_row)])]
    all_to_all x3, starting transfers between devices: 23.1 us -> 17.7 us  [line_all_to_all(): lax.all_to_all(value, 'col', 0, 0, axis_index_groups=lines, tiled=True)]
    unnamed x10 -> x4, local copies, waits for them, and re-layouts: 4.37 us -> 0.84 us
    ppermute x2, starting transfers between devices: 12.8 us -> 9.84 us  [swap_pair(): return lax.ppermute(value, 'col', [(i, i ^ 1) for i in range(n_col)])]
    pallas_call x1, Pallas kernels: 3.01 us -> 5.23 us  [shards(): pl.pallas_call(tiles_kernel, out_shape=shape((n_y, PAIR * nodes, feats),...]
  transfers between devices with their start and end apart: 11 -> 14, of which waited for: 7 -> 5; matrix products, arithmetic and copies ran while one was open for 0% -> 1% of each run, Pallas kernels for 0% -> 8%
where the time goes in v3:
time: 119 us; the launch traced here: 118 us
  starting transfers between devices  84.4 us (71%)
  waiting for transfers between devices  19 us (16%)
  Pallas kernels  11.8 us (10%)
  between operations  1.51 us (1%)
    ppermute x8, starting transfers between devices, swap(): return lax.ppermute(value, 'row', [(i, i ^ mask) for i in range(n_row)])  41.4 us
    all_to_all x3, starting transfers between devices, line_all_to_all(): lax.all_to_all(value, 'col', 0, 0, axis_index_groups=lines, tiled=True)  17.7 us
    ppermute x1, starting transfers between devices, swap_pair(): lax.ppermute(value, ('row', 'col'), [(i, i ^ mask * n_col + 1) for i in r...  15.5 us
    all_to_all x3, waiting for transfers between devices, line_all_to_all(): lax.all_to_all(value, 'col', 0, 0, axis_index_groups=lines, tiled=True)  15.1 us
    ppermute x2, starting transfers between devices, swap_pair(): return lax.ppermute(value, 'col', [(i, i ^ 1) for i in range(n_col)])  9.84 us
    pallas_call x1, Pallas kernels, shards(): pl.pallas_call(tiles_kernel, out_shape=shape((n_y, PAIR * nodes, feats),...  5.23 us
    ppermute x8, waiting for transfers between devices, swap(): return lax.ppermute(value, 'row', [(i, i ^ mask) for i in range(n_row)])  3.91 us
    pallas_call x1, Pallas kernels, shards(): pl.pallas_call(weight_kernel, out_shape=shape((width // LANES * feats, LA...  2.42 us
  transfers between devices with their start and end apart: 14, of which 5 were waited for; matrix products, arithmetic and copies ran while one was open for 1% of the time, Pallas kernels for 8%

profile of v3, /device:TPU:6, one launch (start us, length us, event | category | flops | bytes accessed | tf_op | source)
XLA Modules:
  0.0 118.3 jit_solution(10731468925389596014)
XLA Ops:
  0.6 1.8 %shard_map.95.near = bf16[256,128]{1,0:T(8,128)(2,1)S(1)} custom-call(bf16[256,1024]{1,0:T(8,128)(2,1)} %grad_hbm.3, s32[256,1024]{1,0:T(8,128)} %mask_hbm.3, bf16[128,1024]{1,0:T(8,128)(2,1)} %weight_hbm.1), custom_call_target="tpu_custom_call" | custom-call | flops 67108864 | bytes 2097152 | tf_op jit(solution)/shard_map/pallas_call | solution.py:179
  2.4 10.9 %collective-permute-start = (bf16[256,128]{1,0:T(8,128)(2,1)S(1)}, bf16[256,128]{1,0:T(8,128)(2,1)S(1)}, u32[]{:S(2)}, u32[]{:S(2)}) collective-permute-start(bf16[256,128]{1,0:T(8,128)(2,1)S(1)} %shard_map.95.near), channel_id=1, source_target_pairs={{0,512},{128,640},{256,768},{384,896},{512,0},{640,128},{768,256},... | collective-permute-start | bytes 196616 | tf_op jit(solution)/shard_map/ppermute | solution.py:166
  14.0 0.7 compare_select_fusion.2
  14.7 0.9 collective-permute-done.four.after_ref
  15.6 8.7 %collective-permute-start.3 = (bf16[512,128]{1,0:T(8,128)(2,1)S(1)}, bf16[512,128]{1,0:T(8,128)(2,1)S(1)}, u32[]{:S(2)}, u32[]{:S(2)}) collective-permute-start(bf16[512,128]{1,0:T(8,128)(2,1)S(1)} %pad_maximum_fusion), channel_id=1, source_target_pairs={{0,384},{128,256},{256,128},{384,0},{512,896},{640,768},{768,640},... | collective-permute-start | bytes 393224 | tf_op jit(solution)/shard_map/ppermute | solution.py:166
  24.3 1.9 %collective-permute-start.2 = (bf16[512,128]{1,0:T(8,128)(2,1)S(1)}, bf16[512,128]{1,0:T(8,128)(2,1)S(1)}, u32[]{:S(2)}, u32[]{:S(2)}) collective-permute-start(bf16[512,128]{1,0:T(8,128)(2,1)S(1)} %pad_maximum_fusion), channel_id=1, source_target_pairs={{0,256},{128,384},{256,0},{384,128},{512,768},{640,896},{768,512},... | collective-permute-start | bytes 393224 | tf_op jit(solution)/shard_map/ppermute | solution.py:166
  26.2 2.5 %collective-permute-start.1 = (bf16[512,128]{1,0:T(8,128)(2,1)S(1)}, bf16[512,128]{1,0:T(8,128)(2,1)S(1)}, u32[]{:S(2)}, u32[]{:S(2)}) collective-permute-start(bf16[512,128]{1,0:T(8,128)(2,1)S(1)} %pad_maximum_fusion), channel_id=1, source_target_pairs={{0,128},{128,0},{256,384},{384,256},{512,640},{640,512},{768,896},... | collective-permute-start | bytes 393224 | tf_op jit(solution)/shard_map/ppermute | solution.py:166
  28.7 2.4 %shard_map.99 = bf16[1024,128]{1,0:T(8,128)(2,1)} custom-call(bf16[256,1024]{1,0:T(8,128)(2,1)} %grad_hbm.3, s32[256,1024]{1,0:T(8,128)} %mask_hbm.3, bf16[256,128]{1,0:T(8,128)(2,1)} %aggregated_hbm.1, bf16[256,128]{1,0:T(8,128)(2,1)} %copy-done), custom_call_target="tpu_custom_call" | custom-call | flops 20000000000 | bytes 1048576 | tf_op jit(solution)/shard_map/pallas_call | solution.py:196
  31.1 7.1 %all-to-all-start.1 = ((bf16[8,128,128]{2,1,0:T(8,128)(2,1)}), bf16[8,128,128]{2,1,0:T(8,128)(2,1)S(1)}, u32[]{:S(2)}, u32[]{:S(2)}) async-start(bf16[8,128,128]{2,1,0:T(8,128)(2,1)} %bitcast.9), calls=%async_computation.1 | async-start | bytes 524288 | tf_op jit(solution)/shard_map/all_to_all | solution.py:177
  38.2 0.0 collective-permute-done.3.got_3
  38.3 0.0 copy-start.1
  38.3 0.8 copy-done.1
  39.1 5.2 %shard_map.96.after_ref = bf16[8,512,128]{2,1,0:T(8,128)(2,1)} custom-call(s32[1]{0:T(128)} %bitcast.7.live_ref, s32[160]{0:T(256)S(1)} %get-tuple-element.10.row_ref, s32[160]{0:T(256)S(1)} %get-tuple-element.11.col_ref, bf16[160,128,128]{2,1,0:T(8,128)(2,1)} %bitcast.12, bf16[256,128]{1,0:T(8,128)(2,1)S(1)} %shard_map.95.near, ...), custom_call_target="tpu_custom_call" | custom-call | flops 20000000000 | bytes 5242880 | tf_op jit(solution)/shard_map/pallas_call | solution.py:221
  44.3 5.2 %all-to-all-done.1.spread_ref = bf16[8,128,128]{2,1,0:T(8,128)(2,1)S(1)} async-done(((bf16[8,128,128]{2,1,0:T(8,128)(2,1)}), bf16[8,128,128]{2,1,0:T(8,128)(2,1)S(1)}, u32[]{:S(2)}, u32[]{:S(2)}) %all-to-all-start.1) | async-done | bytes 262176 | tf_op jit(solution)/shard_map/all_to_all | solution.py:177
  49.6 3.6 %all-to-all-start = ((bf16[8,512,128]{2,1,0:T(8,128)(2,1)}), bf16[8,512,128]{2,1,0:T(8,128)(2,1)S(1)}, u32[]{:S(2)}, u32[]{:S(2)}) async-start(bf16[8,512,128]{2,1,0:T(8,128)(2,1)} %shard_map.96.after_ref), calls=%async_computation | async-start | bytes 2097152 | tf_op jit(solution)/shard_map/all_to_all | solution.py:177
  53.2 5.4 %collective-permute-start.7 = (bf16[128,128]{1,0:T(8,128)(2,1)S(1)}, bf16[128,128]{1,0:T(8,128)(2,1)S(1)}, u32[]{:S(2)}, u32[]{:S(2)}) collective-permute-start(bf16[128,128]{1,0:T(8,128)(2,1)S(1)} %shard_map.100), channel_id=1, source_target_pairs={{0,384},{128,256},{256,128},{384,0},{512,896},{640,768},{768,640},... | collective-permute-start | bytes 98312 | tf_op jit(solution)/shard_map/ppermute | solution.py:166
  58.7 1.9 %collective-permute-start.6 = (bf16[128,128]{1,0:T(8,128)(2,1)S(1)}, bf16[128,128]{1,0:T(8,128)(2,1)S(1)}, u32[]{:S(2)}, u32[]{:S(2)}) collective-permute-start(bf16[128,128]{1,0:T(8,128)(2,1)S(1)} %shard_map.100), channel_id=1, source_target_pairs={{0,256},{128,384},{256,0},{384,128},{512,768},{640,896},{768,512},... | collective-permute-start | bytes 98312 | tf_op jit(solution)/shard_map/ppermute | solution.py:166
  60.6 2.8 %collective-permute-start.5 = (bf16[128,128]{1,0:T(8,128)(2,1)S(1)}, bf16[128,128]{1,0:T(8,128)(2,1)S(1)}, u32[]{:S(2)}, u32[]{:S(2)}) collective-permute-start(bf16[128,128]{1,0:T(8,128)(2,1)S(1)} %shard_map.100), channel_id=1, source_target_pairs={{0,128},{128,0},{256,384},{384,256},{512,640},{640,512},{768,896},... | collective-permute-start | bytes 98312 | tf_op jit(solution)/shard_map/ppermute | solution.py:166
  63.4 2.0 %collective-permute-done.6 = bf16[128,128]{1,0:T(8,128)(2,1)S(1)} collective-permute-done((bf16[128,128]{1,0:T(8,128)(2,1)S(1)}, bf16[128,128]{1,0:T(8,128)(2,1)S(1)}, u32[]{:S(2)}, u32[]{:S(2)}) %collective-permute-start.6) | collective-permute-done | bytes 32800 | tf_op jit(solution)/shard_map/ppermute | solution.py:166
  65.4 1.0 collective-permute-done.5
  66.4 15.5 %collective-permute-start.10 = (bf16[128,128]{1,0:T(8,128)(2,1)S(1)}, bf16[128,128]{1,0:T(8,128)(2,1)S(1)}, u32[]{:S(2)}, u32[]{:S(2)}) collective-permute-start(bf16[128,128]{1,0:T(8,128)(2,1)S(1)} %add_convert_fusion.own), channel_id=1, source_target_pairs={{0,520},{8,512},{16,536},{24,528},{32,552},{40,544},{48,568},{56,5... | collective-permute-start | bytes 98312 | tf_op jit(solution)/shard_map/ppermute | solution.py:172
  81.9 2.0 %collective-permute-start.9 = (bf16[128,128]{1,0:T(8,128)(2,1)S(1)}, bf16[128,128]{1,0:T(8,128)(2,1)S(1)}, u32[]{:S(2)}, u32[]{:S(2)}) collective-permute-start(bf16[128,128]{1,0:T(8,128)(2,1)S(1)} %add_convert_fusion.own), channel_id=1, source_target_pairs={{0,8},{8,0},{16,24},{24,16},{32,40},{40,32},{48,56},{56,48},{64,72... | collective-permute-start | bytes 98312 | tf_op jit(solution)/shard_map/ppermute | solution.py:170
  83.9 7.2 %collective-permute-start.8 = (bf16[128,128]{1,0:T(8,128)(2,1)S(1)}, bf16[128,128]{1,0:T(8,128)(2,1)S(1)}, u32[]{:S(2)}, u32[]{:S(2)}) collective-permute-start(bf16[128,128]{1,0:T(8,128)(2,1)S(1)} %add_convert_fusion.own), channel_id=1, source_target_pairs={{0,512},{128,640},{256,768},{384,896},{512,0},{640,128},{768,256},... | collective-permute-start | bytes 98312 | tf_op jit(solution)/shard_map/ppermute | solution.py:166
  91.2 0.0 all-to-all-done.got_ref
  91.2 0.1 shard_map.97
  91.3 7.9 %collective-permute-start.4 = (bf16[256,128]{1,0:T(8,128)(2,1)S(1)}, bf16[256,128]{1,0:T(8,128)(2,1)S(1)}, u32[]{:S(2)}, u32[]{:S(2)}) collective-permute-start(bf16[256,128]{1,0:T(8,128)(2,1)S(1)} %get-tuple-element.7.after_ref), channel_id=1, source_target_pairs={{0,8},{8,0},{16,24},{24,16},{32,40},{40,32},{48,56},{56,48},{64,72... | collective-permute-start | bytes 196616 | tf_op jit(solution)/shard_map/ppermute | solution.py:170
  99.2 0.0 collective-permute-done.8.got_4
  99.2 0.7 shard_map.101
  100.0 7.0 %all-to-all-start.2 = ((bf16[8,128,128]{2,1,0:T(8,128)(2,1)}), bf16[8,128,128]{2,1,0:T(8,128)(2,1)S(1)}, u32[]{:S(2)}, u32[]{:S(2)}) async-start(bf16[8,128,128]{2,1,0:T(8,128)(2,1)} %shard_map.101), calls=%async_computation.2 | async-start | bytes 524288 | tf_op jit(solution)/shard_map/all_to_all | solution.py:177
  107.0 0.6 shard_map.98
  107.6 9.8 %all-to-all-done.2.shares_ref = bf16[8,128,128]{2,1,0:T(8,128)(2,1)S(1)} async-done(((bf16[8,128,128]{2,1,0:T(8,128)(2,1)}), bf16[8,128,128]{2,1,0:T(8,128)(2,1)S(1)}, u32[]{:S(2)}, u32[]{:S(2)}) %all-to-all-start.2) | async-done | bytes 262176 | tf_op jit(solution)/shard_map/all_to_all | solution.py:177
  117.5 0.8 shard_map.102
  (11 shorter events, 0.1 us)
Async XLA Ops:
  2.4 13.2 %collective-permute-start = (bf16[256,128]{1,0:T(8,128)(2,1)S(1)}, bf16[256,128]{1,0:T(8,128)(2,1)S(1)}, u32[]{:S(2)}, u32[]{:S(2)}) collective-permute-start(bf16[256,128]{1,0:T(8,128)(2,1)S(1)} %shard_map.95.near), channel_id=1, source_target_pairs={{0,512},{128,640},{256,768},{384,896},{512,0},{640,128},{768,256},... | collective-permute-start | bytes 196616 | tf_op jit(solution)/shard_map/ppermute | solution.py:166
  15.6 13.1 %copy-start = (bf16[256,128]{1,0:T(8,128)(2,1)}, bf16[256,128]{1,0:T(8,128)(2,1)S(1)}, u32[]{:S(2)}) copy-start(bf16[256,128]{1,0:T(8,128)(2,1)S(1)} %collective-permute-done.four.after_ref) | copy-start | bytes 196612
  15.6 22.7 %collective-permute-start.3 = (bf16[512,128]{1,0:T(8,128)(2,1)S(1)}, bf16[512,128]{1,0:T(8,128)(2,1)S(1)}, u32[]{:S(2)}, u32[]{:S(2)}) collective-permute-start(bf16[512,128]{1,0:T(8,128)(2,1)S(1)} %pad_maximum_fusion), channel_id=1, source_target_pairs={{0,384},{128,256},{256,128},{384,0},{512,896},{640,768},{768,640},... | collective-permute-start | bytes 393224 | tf_op jit(solution)/shard_map/ppermute | solution.py:166
  24.3 14.0 %collective-permute-start.2 = (bf16[512,128]{1,0:T(8,128)(2,1)S(1)}, bf16[512,128]{1,0:T(8,128)(2,1)S(1)}, u32[]{:S(2)}, u32[]{:S(2)}) collective-permute-start(bf16[512,128]{1,0:T(8,128)(2,1)S(1)} %pad_maximum_fusion), channel_id=1, source_target_pairs={{0,256},{128,384},{256,0},{384,128},{512,768},{640,896},{768,512},... | collective-permute-start | bytes 393224 | tf_op jit(solution)/shard_map/ppermute | solution.py:166
  26.2 12.0 %collective-permute-start.1 = (bf16[512,128]{1,0:T(8,128)(2,1)S(1)}, bf16[512,128]{1,0:T(8,128)(2,1)S(1)}, u32[]{:S(2)}, u32[]{:S(2)}) collective-permute-start(bf16[512,128]{1,0:T(8,128)(2,1)S(1)} %pad_maximum_fusion), channel_id=1, source_target_pairs={{0,128},{128,0},{256,384},{384,256},{512,640},{640,512},{768,896},... | collective-permute-start | bytes 393224 | tf_op jit(solution)/shard_map/ppermute | solution.py:166
  31.1 18.5 %all-to-all-start.1 = ((bf16[8,128,128]{2,1,0:T(8,128)(2,1)}), bf16[8,128,128]{2,1,0:T(8,128)(2,1)S(1)}, u32[]{:S(2)}, u32[]{:S(2)}) async-start(bf16[8,128,128]{2,1,0:T(8,128)(2,1)} %bitcast.9), calls=%async_computation.1 | async-start | bytes 524288 | tf_op jit(solution)/shard_map/all_to_all | solution.py:177
  38.3 0.8 copy-start.1
  49.6 41.6 %all-to-all-start = ((bf16[8,512,128]{2,1,0:T(8,128)(2,1)}), bf16[8,512,128]{2,1,0:T(8,128)(2,1)S(1)}, u32[]{:S(2)}, u32[]{:S(2)}) async-start(bf16[8,512,128]{2,1,0:T(8,128)(2,1)} %shard_map.96.after_ref), calls=%async_computation | async-start | bytes 2097152 | tf_op jit(solution)/shard_map/all_to_all | solution.py:177
  53.2 10.1 %collective-permute-start.7 = (bf16[128,128]{1,0:T(8,128)(2,1)S(1)}, bf16[128,128]{1,0:T(8,128)(2,1)S(1)}, u32[]{:S(2)}, u32[]{:S(2)}) collective-permute-start(bf16[128,128]{1,0:T(8,128)(2,1)S(1)} %shard_map.100), channel_id=1, source_target_pairs={{0,384},{128,256},{256,128},{384,0},{512,896},{640,768},{768,640},... | collective-permute-start | bytes 98312 | tf_op jit(solution)/shard_map/ppermute | solution.py:166
  58.7 6.7 %collective-permute-start.6 = (bf16[128,128]{1,0:T(8,128)(2,1)S(1)}, bf16[128,128]{1,0:T(8,128)(2,1)S(1)}, u32[]{:S(2)}, u32[]{:S(2)}) collective-permute-start(bf16[128,128]{1,0:T(8,128)(2,1)S(1)} %shard_map.100), channel_id=1, source_target_pairs={{0,256},{128,384},{256,0},{384,128},{512,768},{640,896},{768,512},... | collective-permute-start | bytes 98312 | tf_op jit(solution)/shard_map/ppermute | solution.py:166
  60.6 5.8 %collective-permute-start.5 = (bf16[128,128]{1,0:T(8,128)(2,1)S(1)}, bf16[128,128]{1,0:T(8,128)(2,1)S(1)}, u32[]{:S(2)}, u32[]{:S(2)}) collective-permute-start(bf16[128,128]{1,0:T(8,128)(2,1)S(1)} %shard_map.100), channel_id=1, source_target_pairs={{0,128},{128,0},{256,384},{384,256},{512,640},{640,512},{768,896},... | collective-permute-start | bytes 98312 | tf_op jit(solution)/shard_map/ppermute | solution.py:166
  66.4 32.8 %collective-permute-start.10 = (bf16[128,128]{1,0:T(8,128)(2,1)S(1)}, bf16[128,128]{1,0:T(8,128)(2,1)S(1)}, u32[]{:S(2)}, u32[]{:S(2)}) collective-permute-start(bf16[128,128]{1,0:T(8,128)(2,1)S(1)} %add_convert_fusion.own), channel_id=1, source_target_pairs={{0,520},{8,512},{16,536},{24,528},{32,552},{40,544},{48,568},{56,5... | collective-permute-start | bytes 98312 | tf_op jit(solution)/shard_map/ppermute | solution.py:172
  81.9 17.3 %collective-permute-start.9 = (bf16[128,128]{1,0:T(8,128)(2,1)S(1)}, bf16[128,128]{1,0:T(8,128)(2,1)S(1)}, u32[]{:S(2)}, u32[]{:S(2)}) collective-permute-start(bf16[128,128]{1,0:T(8,128)(2,1)S(1)} %add_convert_fusion.own), channel_id=1, source_target_pairs={{0,8},{8,0},{16,24},{24,16},{32,40},{40,32},{48,56},{56,48},{64,72... | collective-permute-start | bytes 98312 | tf_op jit(solution)/shard_map/ppermute | solution.py:170
  83.9 15.3 %collective-permute-start.8 = (bf16[128,128]{1,0:T(8,128)(2,1)S(1)}, bf16[128,128]{1,0:T(8,128)(2,1)S(1)}, u32[]{:S(2)}, u32[]{:S(2)}) collective-permute-start(bf16[128,128]{1,0:T(8,128)(2,1)S(1)} %add_convert_fusion.own), channel_id=1, source_target_pairs={{0,512},{128,640},{256,768},{384,896},{512,0},{640,128},{768,256},... | collective-permute-start | bytes 98312 | tf_op jit(solution)/shard_map/ppermute | solution.py:166
  91.3 15.7 %collective-permute-start.4 = (bf16[256,128]{1,0:T(8,128)(2,1)S(1)}, bf16[256,128]{1,0:T(8,128)(2,1)S(1)}, u32[]{:S(2)}, u32[]{:S(2)}) collective-permute-start(bf16[256,128]{1,0:T(8,128)(2,1)S(1)} %get-tuple-element.7.after_ref), channel_id=1, source_target_pairs={{0,8},{8,0},{16,24},{24,16},{32,40},{40,32},{48,56},{56,48},{64,72... | collective-permute-start | bytes 196616 | tf_op jit(solution)/shard_map/ppermute | solution.py:170
  100.0 17.5 %all-to-all-start.2 = ((bf16[8,128,128]{2,1,0:T(8,128)(2,1)}), bf16[8,128,128]{2,1,0:T(8,128)(2,1)S(1)}, u32[]{:S(2)}, u32[]{:S(2)}) async-start(bf16[8,128,128]{2,1,0:T(8,128)(2,1)} %shard_map.101), calls=%async_computation.2 | async-start | bytes 524288 | tf_op jit(solution)/shard_map/all_to_all | solution.py:177

commit v4 on v3

--- a/solution.py
+++ b/solution.py
@@ -39,7 +39,7 @@
 
 
 def weight_kernel(
-    grad_hbm, mask_hbm, aggregated_hbm, after_ref, out_ref, grad, mask, aggregated, arrived
+    grad_hbm, mask_hbm, aggregated_hbm, out_ref, grad, mask, aggregated, arrived
 ):
     copies = [
         pltpu.make_async_copy(mask_hbm, mask, arrived.at[0]),
@@ -59,11 +59,18 @@
         out_ref[j * feats : (j + 1) * feats, :] = term.astype(jnp.bfloat16)
 
 
-def sum_kernel(after_ref, spread_ref, out_ref):
+def token_kernel(four_ref, token_ref):
+    token_ref[...] = jnp.zeros_like(token_ref)
+
+
+def pack_kernel(token_ref, spread_ref, near, four, packed_ref):
     acc = spread_ref[0].astype(jnp.float32)
     for c in range(1, spread_ref.shape[0]):
         acc = acc + spread_ref[c].astype(jnp.float32)
-    out_ref[...] = acc.astype(jnp.bfloat16)
+    nodes = near.shape[0]
+    packed_ref[0:nodes, :] = near[...]
+    packed_ref[nodes : 2 * nodes, :] = four[...]
+    packed_ref[2 * nodes :, :] = acc.astype(jnp.bfloat16)
 
 
 def tiles_kernel(
@@ -79,7 +86,7 @@
     total[...] = jnp.zeros_like(total)
     place = 0
     for part in (near, four, got_1, got_2, got_3):
-        for k in range(part.shape[0] // size):
+        for k in range(min(part.shape[0], 2 * near.shape[0]) // size):
             panel[place] = part[k * size : (k + 1) * size, :]
             place += 1
     live = live_ref[0]
@@ -196,7 +203,7 @@
     term = pl.pallas_call(
         weight_kernel,
         out_shape=shape((width // LANES * feats, LANES), bf),
-        in_specs=[HBM] * 4,
+        in_specs=[HBM] * 3,
         out_specs=VMEM,
         scratch_shapes=[
             pltpu.VMEM((nodes, width), bf),
@@ -206,11 +213,29 @@
         ],
         compiler_params=params(54),
         cost_estimate=cost(2 * 10**10, nodes * width * 4),
-    )(grad_out, relu_mask, aggregated, four)
+    )(grad_out, relu_mask, aggregated)
     spread = line_all_to_all(term.reshape(n_y, term.shape[0] // n_y, LANES))
     extra = spread.shape[1]
-    packed = jnp.concatenate([near, four])
+    token = pl.pallas_call(
+        token_kernel,
+        out_shape=shape((8, LANES), f32),
+        in_specs=[HBM],
+        out_specs=VMEM,
+        compiler_params=params(16),
+        cost_estimate=cost(2 * 10**10, 8 * LANES),
+    )(four)
+    packed = pl.pallas_call(
+        pack_kernel,
+        out_shape=shape((2 * nodes + extra, LANES), bf),
+        in_specs=[HBM] + [VMEM] * 3,
+        out_specs=VMEM,
+        compiler_params=params(16),
+        cost_estimate=cost(nodes * feats * n_y, nodes * feats * n_y * 2),
+    )(token, spread, near, four)
     got_1, got_2, got_3 = swap(packed, 1), swap(packed, 2), swap(packed, 3)
+
+    def tail(value):
+        return value[2 * nodes :].astype(f32)
 
     live = tile_count[0, 0]
     away = (tile_col[0, 0] * size // nodes) ^ lax.axis_index("row")
@@ -234,16 +259,7 @@
     )(live.reshape(1), row_at, col_at, tile_data, near, four, got_1, got_2, got_3)
     got = line_all_to_all(sent)
 
-    share = pl.pallas_call(
-        sum_kernel,
-        out_shape=shape((extra, LANES), bf),
-        in_specs=[HBM, VMEM],
-        out_specs=VMEM,
-        compiler_params=params(16),
-        cost_estimate=cost(n_y * extra * LANES, n_y * extra * LANES * 2),
-    )(sent, spread)
-    row_1, row_2, row_3 = swap(share, 1), swap(share, 2), swap(share, 3)
-    share = ((share.astype(f32) + row_1.astype(f32)) + (row_2.astype(f32) + row_3.astype(f32))).astype(bf)
+    share = ((tail(packed) + tail(got_1)) + (tail(got_2) + tail(got_3))).astype(bf)
     far_4, far_pair, far_both = swap(share, 4), swap_pair(share), swap_pair(share, 4)
 
     half = (lax.axis_index("col") & (PAIR - 1)).astype(jnp.int32).reshape(1)

time: 119 us -> 123 us (1.034)
  waiting for transfers between devices: 19 us -> 40 us
  starting transfers between devices: 84.4 us -> 67.1 us
  Pallas kernels: 11.8 us -> 14.2 us
    all_to_all x3, waiting for transfers between devices: 15.1 us -> 32.2 us  [line_all_to_all(): lax.all_to_all(value, 'col', 0, 0, axis_index_groups=lines, tiled=True)]
    ppermute x8 -> x5, starting transfers between devices: 41.4 us -> 26.3 us  [swap(): return lax.ppermute(value, 'row', [(i, i ^ mask) for i in range(n_row)])]
    ppermute x2, starting transfers between devices: 9.84 us -> 19.2 us  [swap_pair(): return lax.ppermute(value, 'col', [(i, i ^ 1) for i in range(n_col)])]
    ppermute x1, starting transfers between devices: 15.5 us -> 7.49 us  [swap_pair(): lax.ppermute(value, ('row', 'col'), [(i, i ^ mask * n_col + 1) for i in r...]
    ppermute x8 -> x5, waiting for transfers between devices: 3.91 us -> 7.77 us  [swap(): return lax.ppermute(value, 'row', [(i, i ^ mask) for i in range(n_row)])]
    all_to_all x3, starting transfers between devices: 17.7 us -> 14.1 us  [line_all_to_all(): lax.all_to_all(value, 'col', 0, 0, axis_index_groups=lines, tiled=True)]
    pallas_call x1, Pallas kernels: 5.23 us -> 7.56 us  [shards(): pl.pallas_call(tiles_kernel, out_shape=shape((n_y, PAIR * nodes, feats),...]
  transfers between devices with their start and end apart: 14 -> 11, of which waited for: 5 -> 6; matrix products, arithmetic and copies ran while one was open for 1% -> 0% of each run, Pallas kernels for 8% -> 3%
where the time goes in v4:
time: 123 us
  starting transfers between devices  67.1 us (55%)
  waiting for transfers between devices  40 us (33%)
  Pallas kernels  14.2 us (12%)
  between operations  1.49 us (1%)
    all_to_all x3, waiting for transfers between devices, line_all_to_all(): lax.all_to_all(value, 'col', 0, 0, axis_index_groups=lines, tiled=True)  32.2 us
    ppermute x5, starting transfers between devices, swap(): return lax.ppermute(value, 'row', [(i, i ^ mask) for i in range(n_row)])  26.3 us
    ppermute x2, starting transfers between devices, swap_pair(): return lax.ppermute(value, 'col', [(i, i ^ 1) for i in range(n_col)])  19.2 us
    all_to_all x3, starting transfers between devices, line_all_to_all(): lax.all_to_all(value, 'col', 0, 0, axis_index_groups=lines, tiled=True)  14.1 us
    ppermute x5, waiting for transfers between devices, swap(): return lax.ppermute(value, 'row', [(i, i ^ mask) for i in range(n_row)])  7.77 us
    pallas_call x1, Pallas kernels, shards(): pl.pallas_call(tiles_kernel, out_shape=shape((n_y, PAIR * nodes, feats),...  7.56 us
    ppermute x1, starting transfers between devices, swap_pair(): lax.ppermute(value, ('row', 'col'), [(i, i ^ mask * n_col + 1) for i in r...  7.49 us
  transfers between devices with their start and end apart: 11, of which 6 were waited for; matrix products, arithmetic and copies ran while one was open for 0% of the time, Pallas kernels for 3%

profile of v4, /device:TPU:6, one launch (start us, length us, event | category | flops | bytes accessed | tf_op | source)
XLA Modules:
  0.0 122.8 jit_solution(1844694071131654722)
XLA Ops:
  0.6 1.8 %shard_map.95.near = bf16[256,128]{1,0:T(8,128)(2,1)S(1)} custom-call(bf16[256,1024]{1,0:T(8,128)(2,1)} %grad_hbm.3, s32[256,1024]{1,0:T(8,128)} %mask_hbm.3, bf16[128,1024]{1,0:T(8,128)(2,1)} %weight_hbm.1), custom_call_target="tpu_custom_call" | custom-call | flops 67108864 | bytes 2097152 | tf_op jit(solution)/shard_map/pallas_call | solution.py:186
  2.4 10.9 %collective-permute-start = (bf16[256,128]{1,0:T(8,128)(2,1)S(1)}, bf16[256,128]{1,0:T(8,128)(2,1)S(1)}, u32[]{:S(2)}, u32[]{:S(2)}) collective-permute-start(bf16[256,128]{1,0:T(8,128)(2,1)S(1)} %shard_map.95.near), channel_id=1, source_target_pairs={{0,512},{128,640},{256,768},{384,896},{512,0},{640,128},{768,256},... | collective-permute-start | bytes 196616 | tf_op jit(solution)/shard_map/ppermute | solution.py:173
  13.3 2.4 %shard_map.97 = bf16[1024,128]{1,0:T(8,128)(2,1)} custom-call(bf16[256,1024]{1,0:T(8,128)(2,1)} %grad_hbm.3, s32[256,1024]{1,0:T(8,128)} %mask_hbm.3, bf16[256,128]{1,0:T(8,128)(2,1)} %aggregated_hbm.1), custom_call_target="tpu_custom_call" | custom-call | flops 20000000000 | bytes 1048576 | tf_op jit(solution)/shard_map/pallas_call | solution.py:203
  15.8 7.1 %all-to-all-start = ((bf16[8,128,128]{2,1,0:T(8,128)(2,1)}), bf16[8,128,128]{2,1,0:T(8,128)(2,1)S(1)}, u32[]{:S(2)}, u32[]{:S(2)}) async-start(bf16[8,128,128]{2,1,0:T(8,128)(2,1)} %bitcast.9), calls=%async_computation | async-start | bytes 524288 | tf_op jit(solution)/shard_map/all_to_all | solution.py:184
  23.5 0.0 copy-start
  23.5 0.0 copy-start.1
  23.6 0.0 collective-permute-done.four_ref.four
  23.6 10.9 %all-to-all-done.spread_ref = bf16[8,128,128]{2,1,0:T(8,128)(2,1)S(1)} async-done(((bf16[8,128,128]{2,1,0:T(8,128)(2,1)}), bf16[8,128,128]{2,1,0:T(8,128)(2,1)S(1)}, u32[]{:S(2)}, u32[]{:S(2)}) %all-to-all-start) | async-done | bytes 262176 | tf_op jit(solution)/shard_map/all_to_all | solution.py:184
  34.5 7.9 %collective-permute-start.3 = (bf16[640,128]{1,0:T(8,128)(2,1)S(1)}, bf16[640,128]{1,0:T(8,128)(2,1)S(1)}, u32[]{:S(2)}, u32[]{:S(2)}) collective-permute-start(bf16[640,128]{1,0:T(8,128)(2,1)S(1)} %shard_map.98), channel_id=1, source_target_pairs={{0,384},{128,256},{256,128},{384,0},{512,896},{640,768},{768,640},... | collective-permute-start | bytes 491528 | tf_op jit(solution)/shard_map/ppermute | solution.py:173
  42.4 1.9 %collective-permute-start.2 = (bf16[640,128]{1,0:T(8,128)(2,1)S(1)}, bf16[640,128]{1,0:T(8,128)(2,1)S(1)}, u32[]{:S(2)}, u32[]{:S(2)}) collective-permute-start(bf16[640,128]{1,0:T(8,128)(2,1)S(1)} %shard_map.98), channel_id=1, source_target_pairs={{0,256},{128,384},{256,0},{384,128},{512,768},{640,896},{768,512},... | collective-permute-start | bytes 491528 | tf_op jit(solution)/shard_map/ppermute | solution.py:173
  44.4 2.5 %collective-permute-start.1 = (bf16[640,128]{1,0:T(8,128)(2,1)S(1)}, bf16[640,128]{1,0:T(8,128)(2,1)S(1)}, u32[]{:S(2)}, u32[]{:S(2)}) collective-permute-start(bf16[640,128]{1,0:T(8,128)(2,1)S(1)} %shard_map.98), channel_id=1, source_target_pairs={{0,128},{128,0},{256,384},{384,256},{512,640},{640,512},{768,896},... | collective-permute-start | bytes 491528 | tf_op jit(solution)/shard_map/ppermute | solution.py:173
  46.8 0.0 copy-done
  46.9 0.3 collective-permute-done.3.got_3
  47.2 6.2 %collective-permute-done.2.got_2 = bf16[640,128]{1,0:T(8,128)(2,1)S(1)} collective-permute-done((bf16[640,128]{1,0:T(8,128)(2,1)S(1)}, bf16[640,128]{1,0:T(8,128)(2,1)S(1)}, u32[]{:S(2)}, u32[]{:S(2)}) %collective-permute-start.2) | collective-permute-done | bytes 163872 | tf_op jit(solution)/shard_map/ppermute | solution.py:173
  53.4 1.2 collective-permute-done.1.got_1
  54.6 7.6 %shard_map.99 = bf16[8,512,128]{2,1,0:T(8,128)(2,1)} custom-call(s32[1]{0:T(128)} %bitcast.7.live_ref, s32[160]{0:T(256)S(1)} %get-tuple-element.10.row_ref, s32[160]{0:T(256)S(1)} %get-tuple-element.11.col_ref, bf16[160,128,128]{2,1,0:T(8,128)(2,1)} %bitcast.12, bf16[256,128]{1,0:T(8,128)(2,1)S(1)} %shard_map.95.near, ...), custom_call_target="tpu_custom_call" | custom-call | flops 20000000000 | bytes 5242880 | tf_op jit(solution)/shard_map/pallas_call | solution.py:246
  62.2 3.6 %all-to-all-start.1 = ((bf16[8,512,128]{2,1,0:T(8,128)(2,1)}), bf16[8,512,128]{2,1,0:T(8,128)(2,1)S(1)}, u32[]{:S(2)}, u32[]{:S(2)}) async-start(bf16[8,512,128]{2,1,0:T(8,128)(2,1)} %shard_map.99), calls=%async_computation.1 | async-start | bytes 2097152 | tf_op jit(solution)/shard_map/all_to_all | solution.py:184
  65.8 7.5 %collective-permute-start.7 = (bf16[128,128]{1,0:T(8,128)(2,1)S(1)}, bf16[128,128]{1,0:T(8,128)(2,1)S(1)}, u32[]{:S(2)}, u32[]{:S(2)}) collective-permute-start(bf16[128,128]{1,0:T(8,128)(2,1)S(1)} %add_convert_fusion.own), channel_id=1, source_target_pairs={{0,520},{8,512},{16,536},{24,528},{32,552},{40,544},{48,568},{56,5... | collective-permute-start | bytes 98312 | tf_op jit(solution)/shard_map/ppermute | solution.py:179
  73.3 6.5 %collective-permute-start.6 = (bf16[128,128]{1,0:T(8,128)(2,1)S(1)}, bf16[128,128]{1,0:T(8,128)(2,1)S(1)}, u32[]{:S(2)}, u32[]{:S(2)}) collective-permute-start(bf16[128,128]{1,0:T(8,128)(2,1)S(1)} %add_convert_fusion.own), channel_id=1, source_target_pairs={{0,8},{8,0},{16,24},{24,16},{32,40},{40,32},{48,56},{56,48},{64,72... | collective-permute-start | bytes 98312 | tf_op jit(solution)/shard_map/ppermute | solution.py:177
  79.8 3.1 %collective-permute-start.5 = (bf16[128,128]{1,0:T(8,128)(2,1)S(1)}, bf16[128,128]{1,0:T(8,128)(2,1)S(1)}, u32[]{:S(2)}, u32[]{:S(2)}) collective-permute-start(bf16[128,128]{1,0:T(8,128)(2,1)S(1)} %add_convert_fusion.own), channel_id=1, source_target_pairs={{0,512},{128,640},{256,768},{384,896},{512,0},{640,128},{768,256},... | collective-permute-start | bytes 98312 | tf_op jit(solution)/shard_map/ppermute | solution.py:173
  82.9 10.0 %all-to-all-done.1.got_ref = bf16[8,512,128]{2,1,0:T(8,128)(2,1)S(1)} async-done(((bf16[8,512,128]{2,1,0:T(8,128)(2,1)}), bf16[8,512,128]{2,1,0:T(8,128)(2,1)S(1)}, u32[]{:S(2)}, u32[]{:S(2)}) %all-to-all-start.1) | async-done | bytes 1048608 | tf_op jit(solution)/shard_map/all_to_all | solution.py:184
  92.8 0.1 shard_map.100
  93.0 12.8 %collective-permute-start.4 = (bf16[256,128]{1,0:T(8,128)(2,1)S(1)}, bf16[256,128]{1,0:T(8,128)(2,1)S(1)}, u32[]{:S(2)}, u32[]{:S(2)}) collective-permute-start(bf16[256,128]{1,0:T(8,128)(2,1)S(1)} %get-tuple-element.7.after_ref), channel_id=1, source_target_pairs={{0,8},{8,0},{16,24},{24,16},{32,40},{40,32},{48,56},{56,48},{64,72... | collective-permute-start | bytes 196616 | tf_op jit(solution)/shard_map/ppermute | solution.py:177
  105.8 0.0 collective-permute-done.7.got_both
  105.8 0.0 collective-permute-done.6.got_pair
  105.8 0.0 collective-permute-done.5.got_4
  105.8 0.7 shard_map.102
  106.5 3.4 %all-to-all-start.2 = ((bf16[8,128,128]{2,1,0:T(8,128)(2,1)}), bf16[8,128,128]{2,1,0:T(8,128)(2,1)S(1)}, u32[]{:S(2)}, u32[]{:S(2)}) async-start(bf16[8,128,128]{2,1,0:T(8,128)(2,1)} %shard_map.102), calls=%async_computation.2 | async-start | bytes 524288 | tf_op jit(solution)/shard_map/all_to_all | solution.py:184
  109.9 0.0 collective-permute-done.4.got_ref
  110.0 0.6 shard_map.101
  110.6 11.3 %all-to-all-done.2.shares_ref = bf16[8,128,128]{2,1,0:T(8,128)(2,1)S(1)} async-done(((bf16[8,128,128]{2,1,0:T(8,128)(2,1)}), bf16[8,128,128]{2,1,0:T(8,128)(2,1)S(1)}, u32[]{:S(2)}, u32[]{:S(2)}) %all-to-all-start.2) | async-done | bytes 262176 | tf_op jit(solution)/shard_map/all_to_all | solution.py:184
  121.9 0.8 shard_map.103
  (5 shorter events, 0.1 us)
Async XLA Ops:
  2.4 21.2 %collective-permute-start = (bf16[256,128]{1,0:T(8,128)(2,1)S(1)}, bf16[256,128]{1,0:T(8,128)(2,1)S(1)}, u32[]{:S(2)}, u32[]{:S(2)}) collective-permute-start(bf16[256,128]{1,0:T(8,128)(2,1)S(1)} %shard_map.95.near), channel_id=1, source_target_pairs={{0,512},{128,640},{256,768},{384,896},{512,0},{640,128},{768,256},... | collective-permute-start | bytes 196616 | tf_op jit(solution)/shard_map/ppermute | solution.py:173
  15.8 18.7 %all-to-all-start = ((bf16[8,128,128]{2,1,0:T(8,128)(2,1)}), bf16[8,128,128]{2,1,0:T(8,128)(2,1)S(1)}, u32[]{:S(2)}, u32[]{:S(2)}) async-start(bf16[8,128,128]{2,1,0:T(8,128)(2,1)} %bitcast.9), calls=%async_computation | async-start | bytes 524288 | tf_op jit(solution)/shard_map/all_to_all | solution.py:184
  23.5 23.3 %copy-start = (s32[1,1,160]{2,1,0:T(1,128)S(1)}, s32[1,1,160]{2,1,0:T(1,128)}, u32[]{:S(2)}) copy-start(s32[1,1,160]{2,1,0:T(1,128)} %param.13) | copy-start | bytes 1924
  23.5 23.3 %copy-start.1 = (s32[1,1,160]{2,1,0:T(1,128)S(1)}, s32[1,1,160]{2,1,0:T(1,128)}, u32[]{:S(2)}) copy-start(s32[1,1,160]{2,1,0:T(1,128)} %param.14) | copy-start | bytes 1924
  34.5 12.7 %collective-permute-start.3 = (bf16[640,128]{1,0:T(8,128)(2,1)S(1)}, bf16[640,128]{1,0:T(8,128)(2,1)S(1)}, u32[]{:S(2)}, u32[]{:S(2)}) collective-permute-start(bf16[640,128]{1,0:T(8,128)(2,1)S(1)} %shard_map.98), channel_id=1, source_target_pairs={{0,384},{128,256},{256,128},{384,0},{512,896},{640,768},{768,640},... | collective-permute-start | bytes 491528 | tf_op jit(solution)/shard_map/ppermute | solution.py:173
  42.4 11.0 %collective-permute-start.2 = (bf16[640,128]{1,0:T(8,128)(2,1)S(1)}, bf16[640,128]{1,0:T(8,128)(2,1)S(1)}, u32[]{:S(2)}, u32[]{:S(2)}) collective-permute-start(bf16[640,128]{1,0:T(8,128)(2,1)S(1)} %shard_map.98), channel_id=1, source_target_pairs={{0,256},{128,384},{256,0},{384,128},{512,768},{640,896},{768,512},... | collective-permute-start | bytes 491528 | tf_op jit(solution)/shard_map/ppermute | solution.py:173
  44.4 10.3 %collective-permute-start.1 = (bf16[640,128]{1,0:T(8,128)(2,1)S(1)}, bf16[640,128]{1,0:T(8,128)(2,1)S(1)}, u32[]{:S(2)}, u32[]{:S(2)}) collective-permute-start(bf16[640,128]{1,0:T(8,128)(2,1)S(1)} %shard_map.98), channel_id=1, source_target_pairs={{0,128},{128,0},{256,384},{384,256},{512,640},{640,512},{768,896},... | collective-permute-start | bytes 491528 | tf_op jit(solution)/shard_map/ppermute | solution.py:173
  62.2 30.6 %all-to-all-start.1 = ((bf16[8,512,128]{2,1,0:T(8,128)(2,1)}), bf16[8,512,128]{2,1,0:T(8,128)(2,1)S(1)}, u32[]{:S(2)}, u32[]{:S(2)}) async-start(bf16[8,512,128]{2,1,0:T(8,128)(2,1)} %shard_map.99), calls=%async_computation.1 | async-start | bytes 2097152 | tf_op jit(solution)/shard_map/all_to_all | solution.py:184
  65.8 39.9 %collective-permute-start.7 = (bf16[128,128]{1,0:T(8,128)(2,1)S(1)}, bf16[128,128]{1,0:T(8,128)(2,1)S(1)}, u32[]{:S(2)}, u32[]{:S(2)}) collective-permute-start(bf16[128,128]{1,0:T(8,128)(2,1)S(1)} %add_convert_fusion.own), channel_id=1, source_target_pairs={{0,520},{8,512},{16,536},{24,528},{32,552},{40,544},{48,568},{56,5... | collective-permute-start | bytes 98312 | tf_op jit(solution)/shard_map/ppermute | solution.py:179
  73.3 32.5 %collective-permute-start.6 = (bf16[128,128]{1,0:T(8,128)(2,1)S(1)}, bf16[128,128]{1,0:T(8,128)(2,1)S(1)}, u32[]{:S(2)}, u32[]{:S(2)}) collective-permute-start(bf16[128,128]{1,0:T(8,128)(2,1)S(1)} %add_convert_fusion.own), channel_id=1, source_target_pairs={{0,8},{8,0},{16,24},{24,16},{32,40},{40,32},{48,56},{56,48},{64,72... | collective-permute-start | bytes 98312 | tf_op jit(solution)/shard_map/ppermute | solution.py:177
  79.8 26.0 %collective-permute-start.5 = (bf16[128,128]{1,0:T(8,128)(2,1)S(1)}, bf16[128,128]{1,0:T(8,128)(2,1)S(1)}, u32[]{:S(2)}, u32[]{:S(2)}) collective-permute-start(bf16[128,128]{1,0:T(8,128)(2,1)S(1)} %add_convert_fusion.own), channel_id=1, source_target_pairs={{0,512},{128,640},{256,768},{384,896},{512,0},{640,128},{768,256},... | collective-permute-start | bytes 98312 | tf_op jit(solution)/shard_map/ppermute | solution.py:173
  93.0 16.9 %collective-permute-start.4 = (bf16[256,128]{1,0:T(8,128)(2,1)S(1)}, bf16[256,128]{1,0:T(8,128)(2,1)S(1)}, u32[]{:S(2)}, u32[]{:S(2)}) collective-permute-start(bf16[256,128]{1,0:T(8,128)(2,1)S(1)} %get-tuple-element.7.after_ref), channel_id=1, source_target_pairs={{0,8},{8,0},{16,24},{24,16},{32,40},{40,32},{48,56},{56,48},{64,72... | collective-permute-start | bytes 196616 | tf_op jit(solution)/shard_map/ppermute | solution.py:177
  106.5 15.4 %all-to-all-start.2 = ((bf16[8,128,128]{2,1,0:T(8,128)(2,1)}), bf16[8,128,128]{2,1,0:T(8,128)(2,1)S(1)}, u32[]{:S(2)}, u32[]{:S(2)}) async-start(bf16[8,128,128]{2,1,0:T(8,128)(2,1)} %shard_map.102), calls=%async_computation.2 | async-start | bytes 524288 | tf_op jit(solution)/shard_map/all_to_all | solution.py:184

commit v5 on v3

--- a/solution.py
+++ b/solution.py
@@ -1,3 +1,5 @@
+import functools
+
 import jax
 import jax.numpy as jnp
 from jax import lax
@@ -11,7 +13,8 @@
 PAIR = 2
 VMEM = pl.BlockSpec(memory_space=pltpu.VMEM)
 SMEM = pl.BlockSpec(memory_space=pltpu.SMEM)
-HBM = pl.BlockSpec(memory_space=pl.ANY)
+HBM = pl.BlockSpec(memory_space=pltpu.HBM)
+ANY = pl.BlockSpec(memory_space=pl.ANY)
 
 
 def params(mib):
@@ -22,7 +25,10 @@
     return pl.CostEstimate(flops=flops, bytes_accessed=moved, transcendentals=0)
 
 
-def panel_kernel(grad_hbm, mask_hbm, weight_hbm, panel_ref, grad, mask, weight, arrived):
+def panel_kernel(
+    grad_hbm, mask_hbm, weight_hbm, panel_ref, after_ref, grad, mask, weight, arrived
+):
+    after_ref[...] = jnp.zeros_like(after_ref)
     copies = [
         pltpu.make_async_copy(mask_hbm, mask, arrived.at[0]),
         pltpu.make_async_copy(grad_hbm, grad, arrived.at[1]),
@@ -39,7 +45,7 @@
 
 
 def weight_kernel(
-    grad_hbm, mask_hbm, aggregated_hbm, after_ref, out_ref, grad, mask, aggregated, arrived
+    grad_hbm, mask_hbm, aggregated_hbm, before_ref, out_ref, after_ref, grad, mask, aggregated, arrived
 ):
     copies = [
         pltpu.make_async_copy(mask_hbm, mask, arrived.at[0]),
@@ -50,6 +56,7 @@
         copy.start()
     for copy in copies:
         copy.wait()
+    after_ref[...] = jnp.zeros_like(after_ref)
     flipped = aggregated[...].T
     feats = flipped.shape[0]
     for j in range(grad.shape[1] // LANES):
@@ -59,11 +66,16 @@
         out_ref[j * feats : (j + 1) * feats, :] = term.astype(jnp.bfloat16)
 
 
-def sum_kernel(after_ref, spread_ref, out_ref):
-    acc = spread_ref[0].astype(jnp.float32)
-    for c in range(1, spread_ref.shape[0]):
-        acc = acc + spread_ref[c].astype(jnp.float32)
-    out_ref[...] = acc.astype(jnp.bfloat16)
+def pack_kernel(after_ref, near, four, packed_ref):
+    nodes = near.shape[0]
+    packed_ref[0:nodes, :] = near[...]
+    packed_ref[nodes : 2 * nodes, :] = four[...]
+
+
+def sum_kernel(pieces, sent_in, spread_ref, sent_out, piece_ref):
+    rows, lanes = spread_ref.shape
+    terms = spread_ref[...].astype(jnp.float32).reshape(pieces, rows // pieces, lanes)
+    piece_ref[...] = jnp.sum(terms, axis=0)
 
 
 def tiles_kernel(
@@ -124,14 +136,11 @@
     send_ref[...] = total[pl.ds(pl.multiple_of((1 - half) * own, own), own), :].astype(jnp.bfloat16)
 
 
-def share_kernel(after_ref, own, got_4, got_pair, got_both, out_ref):
-    f32 = jnp.float32
-    total = (own[...].astype(f32) + got_4[...].astype(f32)) + (
-        got_pair[...].astype(f32) + got_both[...].astype(f32)
-    )
-    total = total.astype(jnp.bfloat16)
-    for c in range(out_ref.shape[0]):
-        out_ref[c] = total
+def share_kernel(after_ref, piece_ref, out_ref):
+    rows, lanes = out_ref.shape
+    piece = piece_ref[...]
+    repeated = jnp.broadcast_to(piece[None], (rows // piece.shape[0],) + piece.shape)
+    out_ref[...] = repeated.reshape(rows, lanes).astype(jnp.bfloat16)
 
 
 def features_kernel(keep_ref, got_ref, features_ref, after_ref):
@@ -140,13 +149,11 @@
 
 
 def spread_kernel(after_ref, shares_ref, weight_ref):
-    owners, rows = shares_ref.shape[0], shares_ref.shape[1]
     feats = weight_ref.shape[0]
-    for g in range(owners * rows // feats):
-        c, at = g * feats // rows, g * feats % rows
-        weight_ref[:, g * LANES : (g + 1) * LANES] = shares_ref[c, at : at + feats, :].astype(
-            jnp.float32
-        )
+    for g in range(shares_ref.shape[0] // feats):
+        weight_ref[:, g * LANES : (g + 1) * LANES] = shares_ref[
+            g * feats : (g + 1) * feats, :
+        ].astype(jnp.float32)
 
 
 def shards(grad_out, relu_mask, aggregated, weight, adj_tiles, tile_row, tile_col, tile_count):
@@ -161,26 +168,26 @@
     per_owner = nodes // size
     bf, f32 = jnp.bfloat16, jnp.float32
     shape = jax.ShapeDtypeStruct
+    token = shape((8, LANES), f32)
 
     def swap(value, mask):
         return lax.ppermute(value, "row", [(i, i ^ mask) for i in range(n_row)])
 
-    def swap_pair(value, mask=0):
-        if mask == 0:
-            return lax.ppermute(value, "col", [(i, i ^ 1) for i in range(n_col)])
-        count = n_row * n_col
-        return lax.ppermute(
-            value, ("row", "col"), [(i, i ^ (mask * n_col + 1)) for i in range(count)]
-        )
+    def swap_pair(value):
+        return lax.ppermute(value, "col", [(i, i ^ 1) for i in range(n_col)])
 
     def line_all_to_all(value):
         return lax.all_to_all(value, "col", 0, 0, axis_index_groups=lines, tiled=True)
 
-    near = pl.pallas_call(
+    def grid_all_to_all(value):
+        pieces = value.reshape(n_row * n_col, value.shape[0] // (n_row * n_col), LANES)
+        return lax.all_to_all(pieces, ("row", "col"), 0, 0, tiled=True).reshape(value.shape)
+
+    near, after = pl.pallas_call(
         panel_kernel,
-        out_shape=shape((nodes, feats), bf),
+        out_shape=(shape((nodes, feats), bf), token),
         in_specs=[HBM] * 3,
-        out_specs=VMEM,
+        out_specs=(VMEM, VMEM),
         scratch_shapes=[
             pltpu.VMEM((nodes, width), bf),
             pltpu.VMEM((nodes, width), jnp.int32),
@@ -193,23 +200,29 @@
 
     four = swap(near, 4)
 
-    term = pl.pallas_call(
+    term, ready = pl.pallas_call(
         weight_kernel,
-        out_shape=shape((width // LANES * feats, LANES), bf),
-        in_specs=[HBM] * 4,
-        out_specs=VMEM,
+        out_shape=(shape((width // LANES * feats, LANES), bf), token),
+        in_specs=[HBM] * 3 + [VMEM],
+        out_specs=(VMEM, VMEM),
         scratch_shapes=[
             pltpu.VMEM((nodes, width), bf),
             pltpu.VMEM((nodes, width), jnp.int32),
             pltpu.VMEM((nodes, feats), bf),
             pltpu.SemaphoreType.DMA((3,)),
         ],
-        compiler_params=params(54),
+        compiler_params=params(53.75),
         cost_estimate=cost(2 * 10**10, nodes * width * 4),
-    )(grad_out, relu_mask, aggregated, four)
-    spread = line_all_to_all(term.reshape(n_y, term.shape[0] // n_y, LANES))
-    extra = spread.shape[1]
-    packed = jnp.concatenate([near, four])
+    )(grad_out, relu_mask, aggregated, after)
+    spread = grid_all_to_all(term)
+    packed = pl.pallas_call(
+        pack_kernel,
+        out_shape=shape((2 * nodes, feats), bf),
+        in_specs=[VMEM] * 3,
+        out_specs=VMEM,
+        compiler_params=params(16),
+        cost_estimate=cost(nodes * feats, nodes * feats * 8),
+    )(ready, near, four)
     got_1, got_2, got_3 = swap(packed, 1), swap(packed, 2), swap(packed, 3)
 
     live = tile_count[0, 0]
@@ -232,19 +245,19 @@
         compiler_params=params(50),
         cost_estimate=cost(2 * 10**10, slots * size * size * 2),
     )(live.reshape(1), row_at, col_at, tile_data, near, four, got_1, got_2, got_3)
+    sent, piece = pl.pallas_call(
+        functools.partial(sum_kernel, n_row * n_col),
+        out_shape=(
+            shape(sent.shape, bf),
+            shape((term.shape[0] // (n_row * n_col), LANES), f32),
+        ),
+        in_specs=[ANY, VMEM],
+        out_specs=(ANY, VMEM),
+        input_output_aliases={0: 0},
+        compiler_params=params(16),
+        cost_estimate=cost(term.size, term.size * 2),
+    )(sent, spread)
     got = line_all_to_all(sent)
-
-    share = pl.pallas_call(
-        sum_kernel,
-        out_shape=shape((extra, LANES), bf),
-        in_specs=[HBM, VMEM],
-        out_specs=VMEM,
-        compiler_params=params(16),
-        cost_estimate=cost(n_y * extra * LANES, n_y * extra * LANES * 2),
-    )(sent, spread)
-    row_1, row_2, row_3 = swap(share, 1), swap(share, 2), swap(share, 3)
-    share = ((share.astype(f32) + row_1.astype(f32)) + (row_2.astype(f32) + row_3.astype(f32))).astype(bf)
-    far_4, far_pair, far_both = swap(share, 4), swap_pair(share), swap_pair(share, 4)
 
     half = (lax.axis_index("col") & (PAIR - 1)).astype(jnp.int32).reshape(1)
     keep, send = pl.pallas_call(
@@ -259,16 +272,16 @@
     other = swap_pair(send)
     whole = pl.pallas_call(
         share_kernel,
-        out_shape=shape((n_y, extra, LANES), bf),
-        in_specs=[HBM] + [VMEM] * 4,
+        out_shape=shape(term.shape, bf),
+        in_specs=[ANY, VMEM],
         out_specs=VMEM,
         compiler_params=params(16),
-        cost_estimate=cost(2 * 10**10, n_y * extra * LANES * 2),
-    )(send, share, far_4, far_pair, far_both)
-    shares = line_all_to_all(whole)
+        cost_estimate=cost(2 * 10**10, term.size * 4),
+    )(send, piece)
+    shares = grid_all_to_all(whole)
     features, after = pl.pallas_call(
         features_kernel,
-        out_shape=(shape((nodes, feats), bf), shape((8, LANES), f32)),
+        out_shape=(shape((nodes, feats), bf), token),
         in_specs=[VMEM] * 2,
         out_specs=(VMEM, VMEM),
         compiler_params=params(16),
@@ -277,7 +290,7 @@
     grad_weight = pl.pallas_call(
         spread_kernel,
         out_shape=shape((feats, width), f32),
-        in_specs=[HBM, VMEM],
+        in_specs=[ANY, VMEM],
         out_specs=VMEM,
         compiler_params=params(16),
         cost_estimate=cost(feats * width, feats * width * 6),

time: 119 us -> 146 us (1.23)
  waiting for transfers between devices: 19 us -> 62.2 us
  starting transfers between devices: 84.4 us -> 69.3 us
    all_to_all x0 -> x2, starting transfers between devices: none -> 27.6 us  [grid_all_to_all(): lax.all_to_all(pieces, ('row', 'col'), 0, 0, tiled=True)]
    all_to_all x0 -> x2, waiting for transfers between devices: none -> 21.2 us  [grid_all_to_all(): lax.all_to_all(pieces, ('row', 'col'), 0, 0, tiled=True)]
    ppermute x8 -> x4, starting transfers between devices: 41.4 us -> 21 us  [swap(): return lax.ppermute(value, 'row', [(i, i ^ mask) for i in range(n_row)])]
    ppermute x1 -> x0, starting transfers between devices: 15.5 us -> none  [swap_pair(): lax.ppermute(value, ('row', 'col'), [(i, i ^ mask * n_col + 1) for i in r...]
    all_to_all x3 -> x1, waiting for transfers between devices: 15.1 us -> 28.1 us  [line_all_to_all(): lax.all_to_all(value, 'col', 0, 0, axis_index_groups=lines, tiled=True)]
    ppermute x8 -> x4, waiting for transfers between devices: 3.91 us -> 12.9 us  [swap(): return lax.ppermute(value, 'row', [(i, i ^ mask) for i in range(n_row)])]
    all_to_all x3 -> x1, starting transfers between devices: 17.7 us -> 10.1 us  [line_all_to_all(): lax.all_to_all(value, 'col', 0, 0, axis_index_groups=lines, tiled=True)]
    ppermute x2 -> x1, starting transfers between devices: 9.84 us -> 10.6 us  [swap_pair(): return lax.ppermute(value, 'col', [(i, i ^ 1) for i in range(n_col)])]
  transfers between devices with their start and end apart: 14 -> 8, of which waited for: 5 -> 4; matrix products, arithmetic and copies ran while one was open for 1% -> 0% of each run, Pallas kernels for 8% -> 6%
where the time goes in v5:
time: 146 us; the launch traced here: 145 us
  starting transfers between devices  69.3 us (47%)
  waiting for transfers between devices  62.2 us (43%)
  Pallas kernels  10.9 us (7%)
    all_to_all x1, waiting for transfers between devices, line_all_to_all(): lax.all_to_all(value, 'col', 0, 0, axis_index_groups=lines, tiled=True)  28.1 us
    all_to_all x2, starting transfers between devices, grid_all_to_all(): lax.all_to_all(pieces, ('row', 'col'), 0, 0, tiled=True)  27.6 us
    all_to_all x2, waiting for transfers between devices, grid_all_to_all(): lax.all_to_all(pieces, ('row', 'col'), 0, 0, tiled=True)  21.2 us
    ppermute x4, starting transfers between devices, swap(): return lax.ppermute(value, 'row', [(i, i ^ mask) for i in range(n_row)])  21 us
    ppermute x4, waiting for transfers between devices, swap(): return lax.ppermute(value, 'row', [(i, i ^ mask) for i in range(n_row)])  12.9 us
    ppermute x1, starting transfers between devices, swap_pair(): return lax.ppermute(value, 'col', [(i, i ^ 1) for i in range(n_col)])  10.6 us
    all_to_all x1, starting transfers between devices, line_all_to_all(): lax.all_to_all(value, 'col', 0, 0, axis_index_groups=lines, tiled=True)  10.1 us
    pallas_call x1, Pallas kernels, shards(): pl.pallas_call(tiles_kernel, out_shape=shape((n_y, PAIR * nodes, feats),...  4.19 us
  transfers between devices with their start and end apart: 8, of which 4 were waited for; matrix products, arithmetic and copies ran while one was open for 0% of the time, Pallas kernels for 6%

profile of v5, /device:TPU:6, one launch (start us, length us, event | category | flops | bytes accessed | tf_op | source)
XLA Modules:
  0.0 144.7 jit_solution(16634429619543971502)
XLA Ops:
  0.6 1.8 %shard_map.95 = (bf16[256,128]{1,0:T(8,128)(2,1)S(1)}, f32[8,128]{1,0:T(8,128)S(1)}) custom-call(bf16[256,1024]{1,0:T(8,128)(2,1)} %grad_hbm.3, s32[256,1024]{1,0:T(8,128)} %mask_hbm.3, bf16[128,1024]{1,0:T(8,128)(2,1)} %weight_hbm.1), custom_call_target="tpu_custom_call" | custom-call | flops 67108864 | bytes 2097152 | tf_op jit(solution)/shard_map/pallas_call | solution.py:186
  2.4 10.9 %collective-permute-start = (bf16[256,128]{1,0:T(8,128)(2,1)S(1)}, bf16[256,128]{1,0:T(8,128)(2,1)S(1)}, u32[]{:S(2)}, u32[]{:S(2)}) collective-permute-start(bf16[256,128]{1,0:T(8,128)(2,1)S(1)} %get-tuple-element.12.near), channel_id=1, source_target_pairs={{0,512},{128,640},{256,768},{384,896},{512,0},{640,128},{768,256},... | collective-permute-start | bytes 196616 | tf_op jit(solution)/shard_map/ppermute | solution.py:174
  13.3 0.0 copy-start
  13.3 0.8 copy-done
  14.2 0.0 copy-start.1
  14.2 0.0 copy-start.2
  14.2 2.4 %shard_map.96 = (bf16[1024,128]{1,0:T(8,128)(2,1)}, f32[8,128]{1,0:T(8,128)S(1)}) custom-call(bf16[256,1024]{1,0:T(8,128)(2,1)} %grad_hbm.3, s32[256,1024]{1,0:T(8,128)} %mask_hbm.3, bf16[256,128]{1,0:T(8,128)(2,1)S(1)} %copy-done, f32[8,128]{1,0:T(8,128)S(1)} %get-tuple-element.13.before_ref), custom_call_target="tpu_custom_call" | custom-call | flops 20000000000 | bytes 1048576 | tf_op jit(solution)/shard_map/pallas_call | solution.py:203
  16.6 21.5 %all-to-all-start = ((bf16[128,8,128]{2,1,0:T(8,128)(2,1)}), bf16[128,8,128]{2,1,0:T(8,128)(2,1)S(1)}, u32[]{:S(2)}, u32[]{:S(2)}) async-start(bf16[128,8,128]{2,1,0:T(8,128)(2,1)} %bitcast.14), calls=%async_computation | async-start | bytes 524288 | tf_op jit(solution)/shard_map/all_to_all | solution.py:184
  38.8 0.0 collective-permute-done.four
  38.8 5.0 %collective-permute-start.3 = (bf16[512,128]{1,0:T(8,128)(2,1)S(1)}, bf16[512,128]{1,0:T(8,128)(2,1)S(1)}, u32[]{:S(2)}, u32[]{:S(2)}) collective-permute-start(bf16[512,128]{1,0:T(8,128)(2,1)S(1)} %shard_map.97), channel_id=1, source_target_pairs={{0,384},{128,256},{256,128},{384,0},{512,896},{640,768},{768,640},... | collective-permute-start | bytes 393224 | tf_op jit(solution)/shard_map/ppermute | solution.py:174
  43.8 1.9 %collective-permute-start.2 = (bf16[512,128]{1,0:T(8,128)(2,1)S(1)}, bf16[512,128]{1,0:T(8,128)(2,1)S(1)}, u32[]{:S(2)}, u32[]{:S(2)}) collective-permute-start(bf16[512,128]{1,0:T(8,128)(2,1)S(1)} %shard_map.97), channel_id=1, source_target_pairs={{0,256},{128,384},{256,0},{384,128},{512,768},{640,896},{768,512},... | collective-permute-start | bytes 393224 | tf_op jit(solution)/shard_map/ppermute | solution.py:174
  45.8 3.1 %collective-permute-start.1 = (bf16[512,128]{1,0:T(8,128)(2,1)S(1)}, bf16[512,128]{1,0:T(8,128)(2,1)S(1)}, u32[]{:S(2)}, u32[]{:S(2)}) collective-permute-start(bf16[512,128]{1,0:T(8,128)(2,1)S(1)} %shard_map.97), channel_id=1, source_target_pairs={{0,128},{128,0},{256,384},{384,256},{512,640},{640,512},{768,896},... | collective-permute-start | bytes 393224 | tf_op jit(solution)/shard_map/ppermute | solution.py:174
  48.9 0.0 copy-done.1
  48.9 0.0 copy-done.2
  49.0 5.4 %collective-permute-done.3.got_3 = bf16[512,128]{1,0:T(8,128)(2,1)S(1)} collective-permute-done((bf16[512,128]{1,0:T(8,128)(2,1)S(1)}, bf16[512,128]{1,0:T(8,128)(2,1)S(1)}, u32[]{:S(2)}, u32[]{:S(2)}) %collective-permute-start.3) | collective-permute-done | bytes 131104 | tf_op jit(solution)/shard_map/ppermute | solution.py:174
  54.4 7.5 %collective-permute-done.2.got_2 = bf16[512,128]{1,0:T(8,128)(2,1)S(1)} collective-permute-done((bf16[512,128]{1,0:T(8,128)(2,1)S(1)}, bf16[512,128]{1,0:T(8,128)(2,1)S(1)}, u32[]{:S(2)}, u32[]{:S(2)}) %collective-permute-start.2) | collective-permute-done | bytes 131104 | tf_op jit(solution)/shard_map/ppermute | solution.py:174
  61.9 0.0 collective-permute-done.1.got_1
  61.9 4.2 %shard_map.98.sent_in = bf16[8,512,128]{2,1,0:T(8,128)(2,1)} custom-call(s32[1]{0:T(128)} %bitcast.10.live_ref, s32[160]{0:T(256)S(1)} %get-tuple-element.22.row_ref, s32[160]{0:T(256)S(1)} %get-tuple-element.23.col_ref, bf16[160,128,128]{2,1,0:T(8,128)(2,1)} %bitcast.17, bf16[256,128]{1,0:T(8,128)(2,1)S(1)} %get-tuple-element.12.near, ...), custom_call_target="tpu_custom_call" | custom-call | flops 20000000000 | bytes 5242880 | tf_op jit(solution)/shard_map/pallas_call | solution.py:234
  66.1 0.0 all-to-all-done
  66.1 0.1 shard_map.99
  66.2 10.1 %all-to-all-start.1 = ((bf16[8,512,128]{2,1,0:T(8,128)(2,1)}), bf16[8,512,128]{2,1,0:T(8,128)(2,1)S(1)}, u32[]{:S(2)}, u32[]{:S(2)}) async-start(bf16[8,512,128]{2,1,0:T(8,128)(2,1)} %get-tuple-element.16), calls=%async_computation.1 | async-start | bytes 2097152 | tf_op jit(solution)/shard_map/all_to_all | solution.py:180
  76.3 28.1 %all-to-all-done.1.got_ref = bf16[8,512,128]{2,1,0:T(8,128)(2,1)S(1)} async-done(((bf16[8,512,128]{2,1,0:T(8,128)(2,1)}), bf16[8,512,128]{2,1,0:T(8,128)(2,1)S(1)}, u32[]{:S(2)}, u32[]{:S(2)}) %all-to-all-start.1) | async-done | bytes 1048608 | tf_op jit(solution)/shard_map/all_to_all | solution.py:180
  104.4 0.1 shard_map.100
  104.6 10.6 %collective-permute-start.4 = (bf16[256,128]{1,0:T(8,128)(2,1)S(1)}, bf16[256,128]{1,0:T(8,128)(2,1)S(1)}, u32[]{:S(2)}, u32[]{:S(2)}) collective-permute-start(bf16[256,128]{1,0:T(8,128)(2,1)S(1)} %get-tuple-element.18.after_ref), channel_id=1, source_target_pairs={{0,8},{8,0},{16,24},{24,16},{32,40},{40,32},{48,56},{56,48},{64,72... | collective-permute-start | bytes 196616 | tf_op jit(solution)/shard_map/ppermute | solution.py:177
  115.2 0.7 shard_map.102
  115.9 6.2 %all-to-all-start.2 = ((bf16[128,8,128]{2,1,0:T(8,128)(2,1)}), bf16[128,8,128]{2,1,0:T(8,128)(2,1)S(1)}, u32[]{:S(2)}, u32[]{:S(2)}) async-start(bf16[128,8,128]{2,1,0:T(8,128)(2,1)} %bitcast.8), calls=%async_computation.2 | async-start | bytes 524288 | tf_op jit(solution)/shard_map/all_to_all | solution.py:184
  122.1 0.0 collective-permute-done.4.got_ref
  122.1 0.6 shard_map.101
  122.7 21.2 %all-to-all-done.2 = bf16[128,8,128]{2,1,0:T(8,128)(2,1)S(1)} async-done(((bf16[128,8,128]{2,1,0:T(8,128)(2,1)}), bf16[128,8,128]{2,1,0:T(8,128)(2,1)S(1)}, u32[]{:S(2)}, u32[]{:S(2)}) %all-to-all-start.2) | async-done | bytes 262176 | tf_op jit(solution)/shard_map/all_to_all | solution.py:184
  143.9 0.8 shard_map.103
  (2 shorter events, 0.0 us)
Async XLA Ops:
  2.4 36.4 %collective-permute-start = (bf16[256,128]{1,0:T(8,128)(2,1)S(1)}, bf16[256,128]{1,0:T(8,128)(2,1)S(1)}, u32[]{:S(2)}, u32[]{:S(2)}) collective-permute-start(bf16[256,128]{1,0:T(8,128)(2,1)S(1)} %get-tuple-element.12.near), channel_id=1, source_target_pairs={{0,512},{128,640},{256,768},{384,896},{512,0},{640,128},{768,256},... | collective-permute-start | bytes 196616 | tf_op jit(solution)/shard_map/ppermute | solution.py:174
  13.3 0.8 copy-start
  14.2 34.8 %copy-start.1 = (s32[1,1,160]{2,1,0:T(1,128)S(1)}, s32[1,1,160]{2,1,0:T(1,128)}, u32[]{:S(2)}) copy-start(s32[1,1,160]{2,1,0:T(1,128)} %param.13) | copy-start | bytes 1924
  14.2 34.8 %copy-start.2 = (s32[1,1,160]{2,1,0:T(1,128)S(1)}, s32[1,1,160]{2,1,0:T(1,128)}, u32[]{:S(2)}) copy-start(s32[1,1,160]{2,1,0:T(1,128)} %param.14) | copy-start | bytes 1924
  16.6 49.5 %all-to-all-start = ((bf16[128,8,128]{2,1,0:T(8,128)(2,1)}), bf16[128,8,128]{2,1,0:T(8,128)(2,1)S(1)}, u32[]{:S(2)}, u32[]{:S(2)}) async-start(bf16[128,8,128]{2,1,0:T(8,128)(2,1)} %bitcast.14), calls=%async_computation | async-start | bytes 524288 | tf_op jit(solution)/shard_map/all_to_all | solution.py:184
  38.8 15.6 %collective-permute-start.3 = (bf16[512,128]{1,0:T(8,128)(2,1)S(1)}, bf16[512,128]{1,0:T(8,128)(2,1)S(1)}, u32[]{:S(2)}, u32[]{:S(2)}) collective-permute-start(bf16[512,128]{1,0:T(8,128)(2,1)S(1)} %shard_map.97), channel_id=1, source_target_pairs={{0,384},{128,256},{256,128},{384,0},{512,896},{640,768},{768,640},... | collective-permute-start | bytes 393224 | tf_op jit(solution)/shard_map/ppermute | solution.py:174
  43.8 18.0 %collective-permute-start.2 = (bf16[512,128]{1,0:T(8,128)(2,1)S(1)}, bf16[512,128]{1,0:T(8,128)(2,1)S(1)}, u32[]{:S(2)}, u32[]{:S(2)}) collective-permute-start(bf16[512,128]{1,0:T(8,128)(2,1)S(1)} %shard_map.97), channel_id=1, source_target_pairs={{0,256},{128,384},{256,0},{384,128},{512,768},{640,896},{768,512},... | collective-permute-start | bytes 393224 | tf_op jit(solution)/shard_map/ppermute | solution.py:174
  45.8 16.1 %collective-permute-start.1 = (bf16[512,128]{1,0:T(8,128)(2,1)S(1)}, bf16[512,128]{1,0:T(8,128)(2,1)S(1)}, u32[]{:S(2)}, u32[]{:S(2)}) collective-permute-start(bf16[512,128]{1,0:T(8,128)(2,1)S(1)} %shard_map.97), channel_id=1, source_target_pairs={{0,128},{128,0},{256,384},{384,256},{512,640},{640,512},{768,896},... | collective-permute-start | bytes 393224 | tf_op jit(solution)/shard_map/ppermute | solution.py:174
  66.2 38.2 %all-to-all-start.1 = ((bf16[8,512,128]{2,1,0:T(8,128)(2,1)}), bf16[8,512,128]{2,1,0:T(8,128)(2,1)S(1)}, u32[]{:S(2)}, u32[]{:S(2)}) async-start(bf16[8,512,128]{2,1,0:T(8,128)(2,1)} %get-tuple-element.16), calls=%async_computation.1 | async-start | bytes 2097152 | tf_op jit(solution)/shard_map/all_to_all | solution.py:180
  104.6 17.5 %collective-permute-start.4 = (bf16[256,128]{1,0:T(8,128)(2,1)S(1)}, bf16[256,128]{1,0:T(8,128)(2,1)S(1)}, u32[]{:S(2)}, u32[]{:S(2)}) collective-permute-start(bf16[256,128]{1,0:T(8,128)(2,1)S(1)} %get-tuple-element.18.after_ref), channel_id=1, source_target_pairs={{0,8},{8,0},{16,24},{24,16},{32,40},{40,32},{48,56},{56,48},{64,72... | collective-permute-start | bytes 196616 | tf_op jit(solution)/shard_map/ppermute | solution.py:177
  115.9 28.0 %all-to-all-start.2 = ((bf16[128,8,128]{2,1,0:T(8,128)(2,1)}), bf16[128,8,128]{2,1,0:T(8,128)(2,1)S(1)}, u32[]{:S(2)}, u32[]{:S(2)}) async-start(bf16[128,8,128]{2,1,0:T(8,128)(2,1)} %bitcast.8), calls=%async_computation.2 | async-start | bytes 524288 | tf_op jit(solution)/shard_map/all_to_all | solution.py:184

commit v6 on v3

--- a/solution.py
+++ b/solution.py
@@ -22,7 +22,10 @@
     return pl.CostEstimate(flops=flops, bytes_accessed=moved, transcendentals=0)
 
 
-def panel_kernel(grad_hbm, mask_hbm, weight_hbm, panel_ref, grad, mask, weight, arrived):
+def panel_kernel(
+    grad_hbm, mask_hbm, weight_hbm, panel_ref, after_ref, grad, mask, weight, arrived
+):
+    after_ref[...] = jnp.zeros_like(after_ref)
     copies = [
         pltpu.make_async_copy(mask_hbm, mask, arrived.at[0]),
         pltpu.make_async_copy(grad_hbm, grad, arrived.at[1]),
@@ -39,7 +42,7 @@
 
 
 def weight_kernel(
-    grad_hbm, mask_hbm, aggregated_hbm, after_ref, out_ref, grad, mask, aggregated, arrived
+    grad_hbm, mask_hbm, aggregated_hbm, before_ref, out_ref, after_ref, grad, mask, aggregated, arrived
 ):
     copies = [
         pltpu.make_async_copy(mask_hbm, mask, arrived.at[0]),
@@ -50,6 +53,7 @@
         copy.start()
     for copy in copies:
         copy.wait()
+    after_ref[...] = jnp.zeros_like(after_ref)
     flipped = aggregated[...].T
     feats = flipped.shape[0]
     for j in range(grad.shape[1] // LANES):
@@ -59,6 +63,12 @@
         out_ref[j * feats : (j + 1) * feats, :] = term.astype(jnp.bfloat16)
 
 
+def pack_kernel(after_ref, near, four, packed_ref):
+    nodes = near.shape[0]
+    packed_ref[0:nodes, :] = near[...]
+    packed_ref[nodes : 2 * nodes, :] = four[...]
+
+
 def sum_kernel(after_ref, spread_ref, out_ref):
     acc = spread_ref[0].astype(jnp.float32)
     for c in range(1, spread_ref.shape[0]):
@@ -66,9 +76,17 @@
     out_ref[...] = acc.astype(jnp.bfloat16)
 
 
+def quarter_kernel(sent_in, own, row_1, row_2, row_3, sent_out, out_ref):
+    f32 = jnp.float32
+    total = (own[...].astype(f32) + row_1[...].astype(f32)) + (
+        row_2[...].astype(f32) + row_3[...].astype(f32)
+    )
+    out_ref[...] = total.astype(jnp.bfloat16)
+
+
 def tiles_kernel(
-    live_ref, row_ref, col_ref, tiles_hbm, near, four, got_1, got_2, got_3, out_ref,
-    tiles, panel, total, arrived,
+    live_ref, row_ref, col_ref, tiles_hbm, near, four, got_1, got_2, got_3, out_hbm,
+    tiles, panel, total, done, arrived, written,
 ):
     slots, size = tiles.shape[0], tiles.shape[1]
     copies = []
@@ -102,12 +120,17 @@
         copies[k].wait()
         last = jnp.minimum((k + 1) * CHUNK, live)
         lax.fori_loop(k * CHUNK // GROUP, (last + GROUP - 1) // GROUP, group, 0)
-    owners, height = out_ref.shape[0], out_ref.shape[1]
+    owners, height = done.shape[0], done.shape[1]
+    results = []
     for c in range(owners):
         for k in range(height // size):
-            out_ref[c, k * size : (k + 1) * size, :] = total[c * (height // size) + k].astype(
+            done[c, k * size : (k + 1) * size, :] = total[c * (height // size) + k].astype(
                 jnp.bfloat16
             )
+        results.append(pltpu.make_async_copy(done.at[c], out_hbm.at[c], written.at[c]))
+        results[-1].start()
+    for result in results:
+        result.wait()
 
 
 def halves_kernel(half_ref, got_ref, keep_ref, send_ref, total):
@@ -161,6 +184,7 @@
     per_owner = nodes // size
     bf, f32 = jnp.bfloat16, jnp.float32
     shape = jax.ShapeDtypeStruct
+    token = shape((8, LANES), f32)
 
     def swap(value, mask):
         return lax.ppermute(value, "row", [(i, i ^ mask) for i in range(n_row)])
@@ -176,11 +200,11 @@
     def line_all_to_all(value):
         return lax.all_to_all(value, "col", 0, 0, axis_index_groups=lines, tiled=True)
 
-    near = pl.pallas_call(
+    near, first = pl.pallas_call(
         panel_kernel,
-        out_shape=shape((nodes, feats), bf),
+        out_shape=(shape((nodes, feats), bf), token),
         in_specs=[HBM] * 3,
-        out_specs=VMEM,
+        out_specs=(VMEM, VMEM),
         scratch_shapes=[
             pltpu.VMEM((nodes, width), bf),
             pltpu.VMEM((nodes, width), jnp.int32),
@@ -193,24 +217,41 @@
 
     four = swap(near, 4)
 
-    term = pl.pallas_call(
+    term, ready = pl.pallas_call(
         weight_kernel,
-        out_shape=shape((width // LANES * feats, LANES), bf),
-        in_specs=[HBM] * 4,
-        out_specs=VMEM,
+        out_shape=(shape((width // LANES * feats, LANES), bf), token),
+        in_specs=[HBM] * 3 + [VMEM],
+        out_specs=(VMEM, VMEM),
         scratch_shapes=[
             pltpu.VMEM((nodes, width), bf),
             pltpu.VMEM((nodes, width), jnp.int32),
             pltpu.VMEM((nodes, feats), bf),
             pltpu.SemaphoreType.DMA((3,)),
         ],
-        compiler_params=params(54),
+        compiler_params=params(53.75),
         cost_estimate=cost(2 * 10**10, nodes * width * 4),
-    )(grad_out, relu_mask, aggregated, four)
+    )(grad_out, relu_mask, aggregated, first)
     spread = line_all_to_all(term.reshape(n_y, term.shape[0] // n_y, LANES))
     extra = spread.shape[1]
-    packed = jnp.concatenate([near, four])
+    packed = pl.pallas_call(
+        pack_kernel,
+        out_shape=shape((2 * nodes, feats), bf),
+        in_specs=[VMEM] * 3,
+        out_specs=VMEM,
+        compiler_params=params(16),
+        cost_estimate=cost(2 * 10**10, nodes * feats * 8),
+    )(ready, near, four)
     got_1, got_2, got_3 = swap(packed, 1), swap(packed, 2), swap(packed, 3)
+
+    share = pl.pallas_call(
+        sum_kernel,
+        out_shape=shape((extra, LANES), bf),
+        in_specs=[HBM, VMEM],
+        out_specs=VMEM,
+        compiler_params=params(16),
+        cost_estimate=cost(n_y * extra * LANES, n_y * extra * LANES * 2),
+    )(packed, spread)
+    row_1, row_2, row_3 = swap(share, 1), swap(share, 2), swap(share, 3)
 
     live = tile_count[0, 0]
     away = (tile_col[0, 0] * size // nodes) ^ lax.axis_index("row")
@@ -222,28 +263,28 @@
         tiles_kernel,
         out_shape=shape((n_y, PAIR * nodes, feats), bf),
         in_specs=[SMEM] * 3 + [HBM] + [VMEM] * 5,
-        out_specs=VMEM,
+        out_specs=HBM,
         scratch_shapes=[
             pltpu.VMEM((slots, size, size), bf),
             pltpu.VMEM((n_row * per_owner, size, feats), bf),
             pltpu.VMEM((block_tiles + 1, size, feats), f32),
+            pltpu.VMEM((n_y, PAIR * nodes, feats), bf),
             pltpu.SemaphoreType.DMA((slots // CHUNK,)),
+            pltpu.SemaphoreType.DMA((n_y,)),
         ],
         compiler_params=params(50),
         cost_estimate=cost(2 * 10**10, slots * size * size * 2),
     )(live.reshape(1), row_at, col_at, tile_data, near, four, got_1, got_2, got_3)
+    sent, share = pl.pallas_call(
+        quarter_kernel,
+        out_shape=(shape(sent.shape, bf), shape((extra, LANES), bf)),
+        in_specs=[HBM] + [VMEM] * 4,
+        out_specs=(HBM, VMEM),
+        input_output_aliases={0: 0},
+        compiler_params=params(16),
+        cost_estimate=cost(4 * extra * LANES, 4 * extra * LANES * 2),
+    )(sent, share, row_1, row_2, row_3)
     got = line_all_to_all(sent)
-
-    share = pl.pallas_call(
-        sum_kernel,
-        out_shape=shape((extra, LANES), bf),
-        in_specs=[HBM, VMEM],
-        out_specs=VMEM,
-        compiler_params=params(16),
-        cost_estimate=cost(n_y * extra * LANES, n_y * extra * LANES * 2),
-    )(sent, spread)
-    row_1, row_2, row_3 = swap(share, 1), swap(share, 2), swap(share, 3)
-    share = ((share.astype(f32) + row_1.astype(f32)) + (row_2.astype(f32) + row_3.astype(f32))).astype(bf)
     far_4, far_pair, far_both = swap(share, 4), swap_pair(share), swap_pair(share, 4)
 
     half = (lax.axis_index("col") & (PAIR - 1)).astype(jnp.int32).reshape(1)
@@ -268,7 +309,7 @@
     shares = line_all_to_all(whole)
     features, after = pl.pallas_call(
         features_kernel,
-        out_shape=(shape((nodes, feats), bf), shape((8, LANES), f32)),
+        out_shape=(shape((nodes, feats), bf), token),
         in_specs=[VMEM] * 2,
         out_specs=(VMEM, VMEM),
         compiler_params=params(16),

time: 119 us -> 116 us (0.975)
  the two profiles are of different devices: /device:TPU:6 before, /device:TPU:64 now
where the time goes in v6:
time: 116 us; the launch traced here: 115 us
  starting transfers between devices  84 us (72%)
  waiting for transfers between devices  17.7 us (15%)
  Pallas kernels  10.8 us (9%)
  between operations  1.57 us (1%)
    ppermute x8, starting transfers between devices, swap(): return lax.ppermute(value, 'row', [(i, i ^ mask) for i in range(n_row)])  35.6 us
    ppermute x2, starting transfers between devices, swap_pair(): return lax.ppermute(value, 'col', [(i, i ^ 1) for i in range(n_col)])  21.6 us
    all_to_all x3, starting transfers between devices, line_all_to_all(): lax.all_to_all(value, 'col', 0, 0, axis_index_groups=lines, tiled=True)  18.1 us
    all_to_all x3, waiting for transfers between devices, line_all_to_all(): lax.all_to_all(value, 'col', 0, 0, axis_index_groups=lines, tiled=True)  17.7 us
    ppermute x1, starting transfers between devices, swap_pair(): lax.ppermute(value, ('row', 'col'), [(i, i ^ mask * n_col + 1) for i in r...  8.75 us
    pallas_call x1, Pallas kernels, shards(): pl.pallas_call(tiles_kernel, out_shape=shape((n_y, PAIR * nodes, feats),...  4.2 us
    pallas_call x1, Pallas kernels, shards(): pl.pallas_call(weight_kernel, out_shape=(shape((width // LANES * feats, L...  2.42 us
  transfers between devices with their start and end apart: 14, of which 2 were waited for; matrix products, arithmetic and copies ran while one was open for 0% of the time, Pallas kernels for 7%

profile of v6, /device:TPU:64, one launch (start us, length us, event | category | flops | bytes accessed | tf_op | source)
XLA Modules:
  0.0 114.9 jit_solution(4561038222292949292)
XLA Ops:
  0.6 1.8 %shard_map.95 = (bf16[256,128]{1,0:T(8,128)(2,1)S(1)}, f32[8,128]{1,0:T(8,128)S(1)}) custom-call(bf16[256,1024]{1,0:T(8,128)(2,1)} %grad_hbm.3, s32[256,1024]{1,0:T(8,128)} %mask_hbm.3, bf16[128,1024]{1,0:T(8,128)(2,1)} %weight_hbm.1), custom_call_target="tpu_custom_call" | custom-call | flops 67108864 | bytes 2097152 | tf_op jit(solution)/shard_map/pallas_call | solution.py:203
  2.4 10.9 %collective-permute-start = (bf16[256,128]{1,0:T(8,128)(2,1)S(1)}, bf16[256,128]{1,0:T(8,128)(2,1)S(1)}, u32[]{:S(2)}, u32[]{:S(2)}) collective-permute-start(bf16[256,128]{1,0:T(8,128)(2,1)S(1)} %get-tuple-element.12.near), channel_id=1, source_target_pairs={{0,512},{128,640},{256,768},{384,896},{512,0},{640,128},{768,256},... | collective-permute-start | bytes 196616 | tf_op jit(solution)/shard_map/ppermute | solution.py:190
  13.3 0.0 copy-start
  13.3 0.8 copy-done
  14.2 2.4 %shard_map.96 = (bf16[1024,128]{1,0:T(8,128)(2,1)}, f32[8,128]{1,0:T(8,128)S(1)}) custom-call(bf16[256,1024]{1,0:T(8,128)(2,1)} %grad_hbm.3, s32[256,1024]{1,0:T(8,128)} %mask_hbm.3, bf16[256,128]{1,0:T(8,128)(2,1)S(1)} %copy-done, f32[8,128]{1,0:T(8,128)S(1)} %get-tuple-element.13.before_ref), custom_call_target="tpu_custom_call" | custom-call | flops 20000000000 | bytes 1048576 | tf_op jit(solution)/shard_map/pallas_call | solution.py:220
  16.6 7.1 %all-to-all-start = ((bf16[8,128,128]{2,1,0:T(8,128)(2,1)}), bf16[8,128,128]{2,1,0:T(8,128)(2,1)S(1)}, u32[]{:S(2)}, u32[]{:S(2)}) async-start(bf16[8,128,128]{2,1,0:T(8,128)(2,1)} %bitcast.9), calls=%async_computation | async-start | bytes 524288 | tf_op jit(solution)/shard_map/all_to_all | solution.py:201
  24.4 0.0 collective-permute-done.four
  24.4 0.0 copy-start.1
  24.4 0.0 copy-start.2
  24.4 4.3 %collective-permute-start.3 = (bf16[512,128]{1,0:T(8,128)(2,1)S(1)}, bf16[512,128]{1,0:T(8,128)(2,1)S(1)}, u32[]{:S(2)}, u32[]{:S(2)}) collective-permute-start(bf16[512,128]{1,0:T(8,128)(2,1)S(1)} %shard_map.97.after_ref), channel_id=1, source_target_pairs={{0,384},{128,256},{256,128},{384,0},{512,896},{640,768},{768,640},... | collective-permute-start | bytes 393224 | tf_op jit(solution)/shard_map/ppermute | solution.py:190
  28.7 3.7 %collective-permute-start.2 = (bf16[512,128]{1,0:T(8,128)(2,1)S(1)}, bf16[512,128]{1,0:T(8,128)(2,1)S(1)}, u32[]{:S(2)}, u32[]{:S(2)}) collective-permute-start(bf16[512,128]{1,0:T(8,128)(2,1)S(1)} %shard_map.97.after_ref), channel_id=1, source_target_pairs={{0,256},{128,384},{256,0},{384,128},{512,768},{640,896},{768,512},... | collective-permute-start | bytes 393224 | tf_op jit(solution)/shard_map/ppermute | solution.py:190
  32.4 3.4 %collective-permute-start.1 = (bf16[512,128]{1,0:T(8,128)(2,1)S(1)}, bf16[512,128]{1,0:T(8,128)(2,1)S(1)}, u32[]{:S(2)}, u32[]{:S(2)}) collective-permute-start(bf16[512,128]{1,0:T(8,128)(2,1)S(1)} %shard_map.97.after_ref), channel_id=1, source_target_pairs={{0,128},{128,0},{256,384},{384,256},{512,640},{640,512},{768,896},... | collective-permute-start | bytes 393224 | tf_op jit(solution)/shard_map/ppermute | solution.py:190
  35.9 3.7 %collective-permute-start.6 = (bf16[128,128]{1,0:T(8,128)(2,1)S(1)}, bf16[128,128]{1,0:T(8,128)(2,1)S(1)}, u32[]{:S(2)}, u32[]{:S(2)}) collective-permute-start(bf16[128,128]{1,0:T(8,128)(2,1)S(1)} %shard_map.99.own), channel_id=1, source_target_pairs={{0,384},{128,256},{256,128},{384,0},{512,896},{640,768},{768,640},... | collective-permute-start | bytes 98312 | tf_op jit(solution)/shard_map/ppermute | solution.py:190
  39.6 3.7 %collective-permute-start.5 = (bf16[128,128]{1,0:T(8,128)(2,1)S(1)}, bf16[128,128]{1,0:T(8,128)(2,1)S(1)}, u32[]{:S(2)}, u32[]{:S(2)}) collective-permute-start(bf16[128,128]{1,0:T(8,128)(2,1)S(1)} %shard_map.99.own), channel_id=1, source_target_pairs={{0,256},{128,384},{256,0},{384,128},{512,768},{640,896},{768,512},... | collective-permute-start | bytes 98312 | tf_op jit(solution)/shard_map/ppermute | solution.py:190
  43.4 0.0 collective-permute-done.3.got_3
  43.4 3.4 %collective-permute-start.4 = (bf16[128,128]{1,0:T(8,128)(2,1)S(1)}, bf16[128,128]{1,0:T(8,128)(2,1)S(1)}, u32[]{:S(2)}, u32[]{:S(2)}) collective-permute-start(bf16[128,128]{1,0:T(8,128)(2,1)S(1)} %shard_map.99.own), channel_id=1, source_target_pairs={{0,128},{128,0},{256,384},{384,256},{512,640},{640,512},{768,896},... | collective-permute-start | bytes 98312 | tf_op jit(solution)/shard_map/ppermute | solution.py:190
  46.8 0.0 collective-permute-done.2.got_2
  46.8 4.2 %shard_map.98.sent_in = bf16[8,512,128]{2,1,0:T(8,128)(2,1)} custom-call(s32[1]{0:T(128)} %bitcast.7.live_ref, s32[160]{0:T(256)S(1)} %get-tuple-element.22.row_ref, s32[160]{0:T(256)S(1)} %get-tuple-element.23.col_ref, bf16[160,128,128]{2,1,0:T(8,128)(2,1)} %bitcast.12, bf16[256,128]{1,0:T(8,128)(2,1)S(1)} %get-tuple-element.12.near, ...), custom_call_target="tpu_custom_call" | custom-call | flops 20000000000 | bytes 5242880 | tf_op jit(solution)/shard_map/pallas_call | solution.py:262
  51.0 0.0 collective-permute-done.6.row_3
  51.0 0.0 collective-permute-done.4.row_1
  51.1 7.5 %all-to-all-start.1 = ((bf16[8,512,128]{2,1,0:T(8,128)(2,1)}), bf16[8,512,128]{2,1,0:T(8,128)(2,1)S(1)}, u32[]{:S(2)}, u32[]{:S(2)}) async-start(bf16[8,512,128]{2,1,0:T(8,128)(2,1)} %get-tuple-element.16), calls=%async_computation.1 | async-start | bytes 2097152 | tf_op jit(solution)/shard_map/all_to_all | solution.py:201
  58.6 8.7 %collective-permute-start.10 = (bf16[128,128]{1,0:T(8,128)(2,1)S(1)}, bf16[128,128]{1,0:T(8,128)(2,1)S(1)}, u32[]{:S(2)}, u32[]{:S(2)}) collective-permute-start(bf16[128,128]{1,0:T(8,128)(2,1)S(1)} %get-tuple-element.21.own), channel_id=1, source_target_pairs={{0,520},{8,512},{16,536},{24,528},{32,552},{40,544},{48,568},{56,5... | collective-permute-start | bytes 98312 | tf_op jit(solution)/shard_map/ppermute | solution.py:196
  67.4 7.4 %collective-permute-start.9 = (bf16[128,128]{1,0:T(8,128)(2,1)S(1)}, bf16[128,128]{1,0:T(8,128)(2,1)S(1)}, u32[]{:S(2)}, u32[]{:S(2)}) collective-permute-start(bf16[128,128]{1,0:T(8,128)(2,1)S(1)} %get-tuple-element.21.own), channel_id=1, source_target_pairs={{0,8},{8,0},{16,24},{24,16},{32,40},{40,32},{48,56},{56,48},{64,72... | collective-permute-start | bytes 98312 | tf_op jit(solution)/shard_map/ppermute | solution.py:194
  74.7 2.5 %collective-permute-start.8 = (bf16[128,128]{1,0:T(8,128)(2,1)S(1)}, bf16[128,128]{1,0:T(8,128)(2,1)S(1)}, u32[]{:S(2)}, u32[]{:S(2)}) collective-permute-start(bf16[128,128]{1,0:T(8,128)(2,1)S(1)} %get-tuple-element.21.own), channel_id=1, source_target_pairs={{0,512},{128,640},{256,768},{384,896},{512,0},{640,128},{768,256},... | collective-permute-start | bytes 98312 | tf_op jit(solution)/shard_map/ppermute | solution.py:190
  77.2 7.9 %all-to-all-done.1.got_ref = bf16[8,512,128]{2,1,0:T(8,128)(2,1)S(1)} async-done(((bf16[8,512,128]{2,1,0:T(8,128)(2,1)}), bf16[8,512,128]{2,1,0:T(8,128)(2,1)S(1)}, u32[]{:S(2)}, u32[]{:S(2)}) %all-to-all-start.1) | async-done | bytes 1048608 | tf_op jit(solution)/shard_map/all_to_all | solution.py:201
  85.1 0.1 shard_map.101
  85.3 14.2 %collective-permute-start.7 = (bf16[256,128]{1,0:T(8,128)(2,1)S(1)}, bf16[256,128]{1,0:T(8,128)(2,1)S(1)}, u32[]{:S(2)}, u32[]{:S(2)}) collective-permute-start(bf16[256,128]{1,0:T(8,128)(2,1)S(1)} %get-tuple-element.18.after_ref), channel_id=1, source_target_pairs={{0,8},{8,0},{16,24},{24,16},{32,40},{40,32},{48,56},{56,48},{64,72... | collective-permute-start | bytes 196616 | tf_op jit(solution)/shard_map/ppermute | solution.py:194
  99.5 0.7 shard_map.103
  100.3 3.4 %all-to-all-start.2 = ((bf16[8,128,128]{2,1,0:T(8,128)(2,1)}), bf16[8,128,128]{2,1,0:T(8,128)(2,1)S(1)}, u32[]{:S(2)}, u32[]{:S(2)}) async-start(bf16[8,128,128]{2,1,0:T(8,128)(2,1)} %shard_map.103), calls=%async_computation.2 | async-start | bytes 524288 | tf_op jit(solution)/shard_map/all_to_all | solution.py:201
  103.7 0.6 shard_map.102
  104.3 9.7 %all-to-all-done.2.shares_ref = bf16[8,128,128]{2,1,0:T(8,128)(2,1)S(1)} async-done(((bf16[8,128,128]{2,1,0:T(8,128)(2,1)}), bf16[8,128,128]{2,1,0:T(8,128)(2,1)S(1)}, u32[]{:S(2)}, u32[]{:S(2)}) %all-to-all-start.2) | async-done | bytes 262176 | tf_op jit(solution)/shard_map/all_to_all | solution.py:201
  114.1 0.8 shard_map.104
  (13 shorter events, 0.1 us)
Async XLA Ops:
  2.4 22.0 %collective-permute-start = (bf16[256,128]{1,0:T(8,128)(2,1)S(1)}, bf16[256,128]{1,0:T(8,128)(2,1)S(1)}, u32[]{:S(2)}, u32[]{:S(2)}) collective-permute-start(bf16[256,128]{1,0:T(8,128)(2,1)S(1)} %get-tuple-element.12.near), channel_id=1, source_target_pairs={{0,512},{128,640},{256,768},{384,896},{512,0},{640,128},{768,256},... | collective-permute-start | bytes 196616 | tf_op jit(solution)/shard_map/ppermute | solution.py:190
  13.3 0.8 copy-start
  16.6 19.3 %all-to-all-start = ((bf16[8,128,128]{2,1,0:T(8,128)(2,1)}), bf16[8,128,128]{2,1,0:T(8,128)(2,1)S(1)}, u32[]{:S(2)}, u32[]{:S(2)}) async-start(bf16[8,128,128]{2,1,0:T(8,128)(2,1)} %bitcast.9), calls=%async_computation | async-start | bytes 524288 | tf_op jit(solution)/shard_map/all_to_all | solution.py:201
  24.4 11.4 %copy-start.1 = (s32[1,1,160]{2,1,0:T(1,128)S(1)}, s32[1,1,160]{2,1,0:T(1,128)}, u32[]{:S(2)}) copy-start(s32[1,1,160]{2,1,0:T(1,128)} %param.13) | copy-start | bytes 1924
  24.4 11.4 %copy-start.2 = (s32[1,1,160]{2,1,0:T(1,128)S(1)}, s32[1,1,160]{2,1,0:T(1,128)}, u32[]{:S(2)}) copy-start(s32[1,1,160]{2,1,0:T(1,128)} %param.14) | copy-start | bytes 1924
  24.4 19.0 %collective-permute-start.3 = (bf16[512,128]{1,0:T(8,128)(2,1)S(1)}, bf16[512,128]{1,0:T(8,128)(2,1)S(1)}, u32[]{:S(2)}, u32[]{:S(2)}) collective-permute-start(bf16[512,128]{1,0:T(8,128)(2,1)S(1)} %shard_map.97.after_ref), channel_id=1, source_target_pairs={{0,384},{128,256},{256,128},{384,0},{512,896},{640,768},{768,640},... | collective-permute-start | bytes 393224 | tf_op jit(solution)/shard_map/ppermute | solution.py:190
  28.7 18.1 %collective-permute-start.2 = (bf16[512,128]{1,0:T(8,128)(2,1)S(1)}, bf16[512,128]{1,0:T(8,128)(2,1)S(1)}, u32[]{:S(2)}, u32[]{:S(2)}) collective-permute-start(bf16[512,128]{1,0:T(8,128)(2,1)S(1)} %shard_map.97.after_ref), channel_id=1, source_target_pairs={{0,256},{128,384},{256,0},{384,128},{512,768},{640,896},{768,512},... | collective-permute-start | bytes 393224 | tf_op jit(solution)/shard_map/ppermute | solution.py:190
  32.4 14.3 %collective-permute-start.1 = (bf16[512,128]{1,0:T(8,128)(2,1)S(1)}, bf16[512,128]{1,0:T(8,128)(2,1)S(1)}, u32[]{:S(2)}, u32[]{:S(2)}) collective-permute-start(bf16[512,128]{1,0:T(8,128)(2,1)S(1)} %shard_map.97.after_ref), channel_id=1, source_target_pairs={{0,128},{128,0},{256,384},{384,256},{512,640},{640,512},{768,896},... | collective-permute-start | bytes 393224 | tf_op jit(solution)/shard_map/ppermute | solution.py:190
  35.9 15.1 %collective-permute-start.6 = (bf16[128,128]{1,0:T(8,128)(2,1)S(1)}, bf16[128,128]{1,0:T(8,128)(2,1)S(1)}, u32[]{:S(2)}, u32[]{:S(2)}) collective-permute-start(bf16[128,128]{1,0:T(8,128)(2,1)S(1)} %shard_map.99.own), channel_id=1, source_target_pairs={{0,384},{128,256},{256,128},{384,0},{512,896},{640,768},{768,640},... | collective-permute-start | bytes 98312 | tf_op jit(solution)/shard_map/ppermute | solution.py:190
  39.6 11.4 %collective-permute-start.5 = (bf16[128,128]{1,0:T(8,128)(2,1)S(1)}, bf16[128,128]{1,0:T(8,128)(2,1)S(1)}, u32[]{:S(2)}, u32[]{:S(2)}) collective-permute-start(bf16[128,128]{1,0:T(8,128)(2,1)S(1)} %shard_map.99.own), channel_id=1, source_target_pairs={{0,256},{128,384},{256,0},{384,128},{512,768},{640,896},{768,512},... | collective-permute-start | bytes 98312 | tf_op jit(solution)/shard_map/ppermute | solution.py:190
  43.4 7.6 %collective-permute-start.4 = (bf16[128,128]{1,0:T(8,128)(2,1)S(1)}, bf16[128,128]{1,0:T(8,128)(2,1)S(1)}, u32[]{:S(2)}, u32[]{:S(2)}) collective-permute-start(bf16[128,128]{1,0:T(8,128)(2,1)S(1)} %shard_map.99.own), channel_id=1, source_target_pairs={{0,128},{128,0},{256,384},{384,256},{512,640},{640,512},{768,896},... | collective-permute-start | bytes 98312 | tf_op jit(solution)/shard_map/ppermute | solution.py:190
  51.1 34.1 %all-to-all-start.1 = ((bf16[8,512,128]{2,1,0:T(8,128)(2,1)}), bf16[8,512,128]{2,1,0:T(8,128)(2,1)S(1)}, u32[]{:S(2)}, u32[]{:S(2)}) async-start(bf16[8,512,128]{2,1,0:T(8,128)(2,1)} %get-tuple-element.16), calls=%async_computation.1 | async-start | bytes 2097152 | tf_op jit(solution)/shard_map/all_to_all | solution.py:201
  58.6 40.9 %collective-permute-start.10 = (bf16[128,128]{1,0:T(8,128)(2,1)S(1)}, bf16[128,128]{1,0:T(8,128)(2,1)S(1)}, u32[]{:S(2)}, u32[]{:S(2)}) collective-permute-start(bf16[128,128]{1,0:T(8,128)(2,1)S(1)} %get-tuple-element.21.own), channel_id=1, source_target_pairs={{0,520},{8,512},{16,536},{24,528},{32,552},{40,544},{48,568},{56,5... | collective-permute-start | bytes 98312 | tf_op jit(solution)/shard_map/ppermute | solution.py:196
  67.4 32.2 %collective-permute-start.9 = (bf16[128,128]{1,0:T(8,128)(2,1)S(1)}, bf16[128,128]{1,0:T(8,128)(2,1)S(1)}, u32[]{:S(2)}, u32[]{:S(2)}) collective-permute-start(bf16[128,128]{1,0:T(8,128)(2,1)S(1)} %get-tuple-element.21.own), channel_id=1, source_target_pairs={{0,8},{8,0},{16,24},{24,16},{32,40},{40,32},{48,56},{56,48},{64,72... | collective-permute-start | bytes 98312 | tf_op jit(solution)/shard_map/ppermute | solution.py:194
  74.7 24.8 %collective-permute-start.8 = (bf16[128,128]{1,0:T(8,128)(2,1)S(1)}, bf16[128,128]{1,0:T(8,128)(2,1)S(1)}, u32[]{:S(2)}, u32[]{:S(2)}) collective-permute-start(bf16[128,128]{1,0:T(8,128)(2,1)S(1)} %get-tuple-element.21.own), channel_id=1, source_target_pairs={{0,512},{128,640},{256,768},{384,896},{512,0},{640,128},{768,256},... | collective-permute-start | bytes 98312 | tf_op jit(solution)/shard_map/ppermute | solution.py:190
  85.3 18.4 %collective-permute-start.7 = (bf16[256,128]{1,0:T(8,128)(2,1)S(1)}, bf16[256,128]{1,0:T(8,128)(2,1)S(1)}, u32[]{:S(2)}, u32[]{:S(2)}) collective-permute-start(bf16[256,128]{1,0:T(8,128)(2,1)S(1)} %get-tuple-element.18.after_ref), channel_id=1, source_target_pairs={{0,8},{8,0},{16,24},{24,16},{32,40},{40,32},{48,56},{56,48},{64,72... | collective-permute-start | bytes 196616 | tf_op jit(solution)/shard_map/ppermute | solution.py:194
  100.3 13.8 %all-to-all-start.2 = ((bf16[8,128,128]{2,1,0:T(8,128)(2,1)}), bf16[8,128,128]{2,1,0:T(8,128)(2,1)S(1)}, u32[]{:S(2)}, u32[]{:S(2)}) async-start(bf16[8,128,128]{2,1,0:T(8,128)(2,1)} %shard_map.103), calls=%async_computation.2 | async-start | bytes 524288 | tf_op jit(solution)/shard_map/all_to_all | solution.py:201

commit v7 on v6

--- a/solution.py
+++ b/solution.py
@@ -76,11 +76,8 @@
     out_ref[...] = acc.astype(jnp.bfloat16)
 
 
-def quarter_kernel(sent_in, own, row_1, row_2, row_3, sent_out, out_ref):
-    f32 = jnp.float32
-    total = (own[...].astype(f32) + row_1[...].astype(f32)) + (
-        row_2[...].astype(f32) + row_3[...].astype(f32)
-    )
+def pair_kernel(sent_in, own, other, sent_out, out_ref):
+    total = own[...].astype(jnp.float32) + other[...].astype(jnp.float32)
     out_ref[...] = total.astype(jnp.bfloat16)
 
 
@@ -147,11 +144,8 @@
     send_ref[...] = total[pl.ds(pl.multiple_of((1 - half) * own, own), own), :].astype(jnp.bfloat16)
 
 
-def share_kernel(after_ref, own, got_4, got_pair, got_both, out_ref):
-    f32 = jnp.float32
-    total = (own[...].astype(f32) + got_4[...].astype(f32)) + (
-        got_pair[...].astype(f32) + got_both[...].astype(f32)
-    )
+def share_kernel(after_ref, own, other, out_ref):
+    total = own[...].astype(jnp.float32) + other[...].astype(jnp.float32)
     total = total.astype(jnp.bfloat16)
     for c in range(out_ref.shape[0]):
         out_ref[c] = total
@@ -189,13 +183,8 @@
     def swap(value, mask):
         return lax.ppermute(value, "row", [(i, i ^ mask) for i in range(n_row)])
 
-    def swap_pair(value, mask=0):
-        if mask == 0:
-            return lax.ppermute(value, "col", [(i, i ^ 1) for i in range(n_col)])
-        count = n_row * n_col
-        return lax.ppermute(
-            value, ("row", "col"), [(i, i ^ (mask * n_col + 1)) for i in range(count)]
-        )
+    def swap_pair(value):
+        return lax.ppermute(value, "col", [(i, i ^ 1) for i in range(n_col)])
 
     def line_all_to_all(value):
         return lax.all_to_all(value, "col", 0, 0, axis_index_groups=lines, tiled=True)
@@ -228,7 +217,7 @@
             pltpu.VMEM((nodes, feats), bf),
             pltpu.SemaphoreType.DMA((3,)),
         ],
-        compiler_params=params(53.75),
+        compiler_params=params(53.9),
         cost_estimate=cost(2 * 10**10, nodes * width * 4),
     )(grad_out, relu_mask, aggregated, first)
     spread = line_all_to_all(term.reshape(n_y, term.shape[0] // n_y, LANES))
@@ -249,9 +238,9 @@
         in_specs=[HBM, VMEM],
         out_specs=VMEM,
         compiler_params=params(16),
-        cost_estimate=cost(n_y * extra * LANES, n_y * extra * LANES * 2),
+        cost_estimate=cost(2 * 10**10, n_y * extra * LANES * 2),
     )(packed, spread)
-    row_1, row_2, row_3 = swap(share, 1), swap(share, 2), swap(share, 3)
+    row_1 = swap(share, 1)
 
     live = tile_count[0, 0]
     away = (tile_col[0, 0] * size // nodes) ^ lax.axis_index("row")
@@ -276,16 +265,18 @@
         cost_estimate=cost(2 * 10**10, slots * size * size * 2),
     )(live.reshape(1), row_at, col_at, tile_data, near, four, got_1, got_2, got_3)
     sent, share = pl.pallas_call(
-        quarter_kernel,
+        pair_kernel,
         out_shape=(shape(sent.shape, bf), shape((extra, LANES), bf)),
-        in_specs=[HBM] + [VMEM] * 4,
+        in_specs=[HBM] + [VMEM] * 2,
         out_specs=(HBM, VMEM),
         input_output_aliases={0: 0},
         compiler_params=params(16),
         cost_estimate=cost(4 * extra * LANES, 4 * extra * LANES * 2),
-    )(sent, share, row_1, row_2, row_3)
+    )(sent, share, row_1)
     got = line_all_to_all(sent)
-    far_4, far_pair, far_both = swap(share, 4), swap_pair(share), swap_pair(share, 4)
+    for mask in (2, 4):
+        share = (share.astype(f32) + swap(share, mask).astype(f32)).astype(bf)
+    far = swap_pair(share)
 
     half = (lax.axis_index("col") & (PAIR - 1)).astype(jnp.int32).reshape(1)
     keep, send = pl.pallas_call(
@@ -301,11 +292,11 @@
     whole = pl.pallas_call(
         share_kernel,
         out_shape=shape((n_y, extra, LANES), bf),
-        in_specs=[HBM] + [VMEM] * 4,
+        in_specs=[HBM] + [VMEM] * 2,
         out_specs=VMEM,
         compiler_params=params(16),
         cost_estimate=cost(2 * 10**10, n_y * extra * LANES * 2),
-    )(send, share, far_4, far_pair, far_both)
+    )(send, share, far)
     shares = line_all_to_all(whole)
     features, after = pl.pallas_call(
         features_kernel,

time: 116 us -> 111 us (0.957)
  the two profiles are of different devices: /device:TPU:64 before, /device:TPU:6 now
where the time goes in v7:
time: 111 us; the launch traced here: 110 us
  starting transfers between devices  72.2 us (65%)
  waiting for transfers between devices  25.2 us (23%)
  Pallas kernels  10.8 us (10%)
  between operations  1.51 us (1%)
    ppermute x7, starting transfers between devices, swap(): return lax.ppermute(value, 'row', [(i, i ^ mask) for i in range(n_row)])  31.2 us
    ppermute x2, starting transfers between devices, swap_pair(): return lax.ppermute(value, 'col', [(i, i ^ 1) for i in range(n_col)])  22.8 us
    all_to_all x3, starting transfers between devices, line_all_to_all(): lax.all_to_all(value, 'col', 0, 0, axis_index_groups=lines, tiled=True)  18.3 us
    ppermute x7, waiting for transfers between devices, swap(): return lax.ppermute(value, 'row', [(i, i ^ mask) for i in range(n_row)])  15.5 us
    all_to_all x3, waiting for transfers between devices, line_all_to_all(): lax.all_to_all(value, 'col', 0, 0, axis_index_groups=lines, tiled=True)  9.46 us
    pallas_call x1, Pallas kernels, shards(): pl.pallas_call(tiles_kernel, out_shape=shape((n_y, PAIR * nodes, feats),...  4.19 us
    pallas_call x1, Pallas kernels, shards(): pl.pallas_call(weight_kernel, out_shape=(shape((width // LANES * feats, L...  2.43 us
  transfers between devices with their start and end apart: 12, of which 6 were waited for; matrix products, arithmetic and copies ran while one was open for 0% of the time, Pallas kernels for 7%

profile of v7, /device:TPU:6, one launch (start us, length us, event | category | flops | bytes accessed | tf_op | source)
XLA Modules:
  0.0 109.9 jit_solution(10944796626739545524)
XLA Ops:
  0.6 1.8 %shard_map.95 = (bf16[256,128]{1,0:T(8,128)(2,1)S(1)}, f32[8,128]{1,0:T(8,128)S(1)}) custom-call(bf16[256,1024]{1,0:T(8,128)(2,1)} %grad_hbm.3, s32[256,1024]{1,0:T(8,128)} %mask_hbm.3, bf16[128,1024]{1,0:T(8,128)(2,1)} %weight_hbm.1), custom_call_target="tpu_custom_call" | custom-call | flops 67108864 | bytes 2097152 | tf_op jit(solution)/shard_map/pallas_call | solution.py:192
  2.4 10.9 %collective-permute-start = (bf16[256,128]{1,0:T(8,128)(2,1)S(1)}, bf16[256,128]{1,0:T(8,128)(2,1)S(1)}, u32[]{:S(2)}, u32[]{:S(2)}) collective-permute-start(bf16[256,128]{1,0:T(8,128)(2,1)S(1)} %get-tuple-element.12.near), channel_id=1, source_target_pairs={{0,512},{128,640},{256,768},{384,896},{512,0},{640,128},{768,256},... | collective-permute-start | bytes 196616 | tf_op jit(solution)/shard_map/ppermute | solution.py:184
  13.3 0.0 copy-start
  13.3 0.0 copy-start.1
  13.4 2.4 %shard_map.96 = (bf16[1024,128]{1,0:T(8,128)(2,1)}, f32[8,128]{1,0:T(8,128)S(1)}) custom-call(bf16[256,1024]{1,0:T(8,128)(2,1)} %grad_hbm.3, s32[256,1024]{1,0:T(8,128)} %mask_hbm.3, bf16[256,128]{1,0:T(8,128)(2,1)} %aggregated_hbm.1, f32[8,128]{1,0:T(8,128)S(1)} %get-tuple-element.13.before_ref), custom_call_target="tpu_custom_call" | custom-call | flops 20000000000 | bytes 1048576 | tf_op jit(solution)/shard_map/pallas_call | solution.py:209
  15.8 7.1 %all-to-all-start = ((bf16[8,128,128]{2,1,0:T(8,128)(2,1)}), bf16[8,128,128]{2,1,0:T(8,128)(2,1)S(1)}, u32[]{:S(2)}, u32[]{:S(2)}) async-start(bf16[8,128,128]{2,1,0:T(8,128)(2,1)} %bitcast.9), calls=%async_computation | async-start | bytes 524288 | tf_op jit(solution)/shard_map/all_to_all | solution.py:190
  23.6 0.0 collective-permute-done.four
  23.6 7.9 %collective-permute-start.3 = (bf16[512,128]{1,0:T(8,128)(2,1)S(1)}, bf16[512,128]{1,0:T(8,128)(2,1)S(1)}, u32[]{:S(2)}, u32[]{:S(2)}) collective-permute-start(bf16[512,128]{1,0:T(8,128)(2,1)S(1)} %shard_map.97.after_ref), channel_id=1, source_target_pairs={{0,384},{128,256},{256,128},{384,0},{512,896},{640,768},{768,640},... | collective-permute-start | bytes 393224 | tf_op jit(solution)/shard_map/ppermute | solution.py:184
  31.5 1.9 %collective-permute-start.2 = (bf16[512,128]{1,0:T(8,128)(2,1)S(1)}, bf16[512,128]{1,0:T(8,128)(2,1)S(1)}, u32[]{:S(2)}, u32[]{:S(2)}) collective-permute-start(bf16[512,128]{1,0:T(8,128)(2,1)S(1)} %shard_map.97.after_ref), channel_id=1, source_target_pairs={{0,256},{128,384},{256,0},{384,128},{512,768},{640,896},{768,512},... | collective-permute-start | bytes 393224 | tf_op jit(solution)/shard_map/ppermute | solution.py:184
  33.5 2.5 %collective-permute-start.1 = (bf16[512,128]{1,0:T(8,128)(2,1)S(1)}, bf16[512,128]{1,0:T(8,128)(2,1)S(1)}, u32[]{:S(2)}, u32[]{:S(2)}) collective-permute-start(bf16[512,128]{1,0:T(8,128)(2,1)S(1)} %shard_map.97.after_ref), channel_id=1, source_target_pairs={{0,128},{128,0},{256,384},{384,256},{512,640},{640,512},{768,896},... | collective-permute-start | bytes 393224 | tf_op jit(solution)/shard_map/ppermute | solution.py:184
  35.9 0.0 all-to-all-done.spread_ref
  36.0 3.4 %collective-permute-start.4 = (bf16[128,128]{1,0:T(8,128)(2,1)S(1)}, bf16[128,128]{1,0:T(8,128)(2,1)S(1)}, u32[]{:S(2)}, u32[]{:S(2)}) collective-permute-start(bf16[128,128]{1,0:T(8,128)(2,1)S(1)} %shard_map.99.own), channel_id=1, source_target_pairs={{0,128},{128,0},{256,384},{384,256},{512,640},{640,512},{768,896},... | collective-permute-start | bytes 98312 | tf_op jit(solution)/shard_map/ppermute | solution.py:184
  39.4 0.0 collective-permute-done.3.got_3
  39.4 1.8 %collective-permute-done.2.got_2 = bf16[512,128]{1,0:T(8,128)(2,1)S(1)} collective-permute-done((bf16[512,128]{1,0:T(8,128)(2,1)S(1)}, bf16[512,128]{1,0:T(8,128)(2,1)S(1)}, u32[]{:S(2)}, u32[]{:S(2)}) %collective-permute-start.2) | collective-permute-done | bytes 131104 | tf_op jit(solution)/shard_map/ppermute | solution.py:184
  41.2 1.7 %collective-permute-done.1.got_1 = bf16[512,128]{1,0:T(8,128)(2,1)S(1)} collective-permute-done((bf16[512,128]{1,0:T(8,128)(2,1)S(1)}, bf16[512,128]{1,0:T(8,128)(2,1)S(1)}, u32[]{:S(2)}, u32[]{:S(2)}) %collective-permute-start.1) | collective-permute-done | bytes 131104 | tf_op jit(solution)/shard_map/ppermute | solution.py:184
  42.9 4.2 %shard_map.98.sent_in = bf16[8,512,128]{2,1,0:T(8,128)(2,1)} custom-call(s32[1]{0:T(128)} %bitcast.7.live_ref, s32[160]{0:T(256)S(1)} %get-tuple-element.22.row_ref, s32[160]{0:T(256)S(1)} %get-tuple-element.23.col_ref, bf16[160,128,128]{2,1,0:T(8,128)(2,1)} %bitcast.12, bf16[256,128]{1,0:T(8,128)(2,1)S(1)} %get-tuple-element.12.near, ...), custom_call_target="tpu_custom_call" | custom-call | flops 20000000000 | bytes 5242880 | tf_op jit(solution)/shard_map/pallas_call | solution.py:251
  47.1 0.0 collective-permute-done.4.other
  47.1 7.7 %all-to-all-start.1 = ((bf16[8,512,128]{2,1,0:T(8,128)(2,1)}), bf16[8,512,128]{2,1,0:T(8,128)(2,1)S(1)}, u32[]{:S(2)}, u32[]{:S(2)}) async-start(bf16[8,512,128]{2,1,0:T(8,128)(2,1)} %get-tuple-element.16), calls=%async_computation.1 | async-start | bytes 2097152 | tf_op jit(solution)/shard_map/all_to_all | solution.py:190
  54.9 1.9 %collective-permute-start.6 = (bf16[128,128]{1,0:T(8,128)(2,1)S(1)}, bf16[128,128]{1,0:T(8,128)(2,1)S(1)}, u32[]{:S(2)}, u32[]{:S(2)}) collective-permute-start(bf16[128,128]{1,0:T(8,128)(2,1)S(1)} %get-tuple-element.21), channel_id=1, source_target_pairs={{0,256},{128,384},{256,0},{384,128},{512,768},{640,896},{768,512},... | collective-permute-start | bytes 98312 | tf_op jit(solution)/shard_map/ppermute | solution.py:184
  56.8 4.8 %collective-permute-done.6 = bf16[128,128]{1,0:T(8,128)(2,1)S(1)} collective-permute-done((bf16[128,128]{1,0:T(8,128)(2,1)S(1)}, bf16[128,128]{1,0:T(8,128)(2,1)S(1)}, u32[]{:S(2)}, u32[]{:S(2)}) %collective-permute-start.6) | collective-permute-done | bytes 32800 | tf_op jit(solution)/shard_map/ppermute | solution.py:184
  61.6 2.7 %collective-permute-start.7 = (bf16[128,128]{1,0:T(8,128)(2,1)S(1)}, bf16[128,128]{1,0:T(8,128)(2,1)S(1)}, u32[]{:S(2)}, u32[]{:S(2)}) collective-permute-start(bf16[128,128]{1,0:T(8,128)(2,1)S(1)} %add_convert_fusion.1), channel_id=1, source_target_pairs={{0,512},{128,640},{256,768},{384,896},{512,0},{640,128},{768,256},... | collective-permute-start | bytes 98312 | tf_op jit(solution)/shard_map/ppermute | solution.py:184
  64.2 7.2 %collective-permute-done.7 = bf16[128,128]{1,0:T(8,128)(2,1)S(1)} collective-permute-done((bf16[128,128]{1,0:T(8,128)(2,1)S(1)}, bf16[128,128]{1,0:T(8,128)(2,1)S(1)}, u32[]{:S(2)}, u32[]{:S(2)}) %collective-permute-start.7) | collective-permute-done | bytes 32800 | tf_op jit(solution)/shard_map/ppermute | solution.py:184
  71.4 12.4 %collective-permute-start.8 = (bf16[128,128]{1,0:T(8,128)(2,1)S(1)}, bf16[128,128]{1,0:T(8,128)(2,1)S(1)}, u32[]{:S(2)}, u32[]{:S(2)}) collective-permute-start(bf16[128,128]{1,0:T(8,128)(2,1)S(1)} %add_convert_fusion.own), channel_id=1, source_target_pairs={{0,8},{8,0},{16,24},{24,16},{32,40},{40,32},{48,56},{56,48},{64,72... | collective-permute-start | bytes 98312 | tf_op jit(solution)/shard_map/ppermute | solution.py:187
  83.9 0.1 shard_map.101
  84.0 10.4 %collective-permute-start.5 = (bf16[256,128]{1,0:T(8,128)(2,1)S(1)}, bf16[256,128]{1,0:T(8,128)(2,1)S(1)}, u32[]{:S(2)}, u32[]{:S(2)}) collective-permute-start(bf16[256,128]{1,0:T(8,128)(2,1)S(1)} %get-tuple-element.18.after_ref), channel_id=1, source_target_pairs={{0,8},{8,0},{16,24},{24,16},{32,40},{40,32},{48,56},{56,48},{64,72... | collective-permute-start | bytes 196616 | tf_op jit(solution)/shard_map/ppermute | solution.py:187
  94.5 0.0 collective-permute-done.8.other
  94.5 0.7 shard_map.103
  95.2 3.4 %all-to-all-start.2 = ((bf16[8,128,128]{2,1,0:T(8,128)(2,1)}), bf16[8,128,128]{2,1,0:T(8,128)(2,1)S(1)}, u32[]{:S(2)}, u32[]{:S(2)}) async-start(bf16[8,128,128]{2,1,0:T(8,128)(2,1)} %shard_map.103), calls=%async_computation.2 | async-start | bytes 524288 | tf_op jit(solution)/shard_map/all_to_all | solution.py:190
  98.6 0.3 collective-permute-done.5.got_ref
  98.9 0.6 shard_map.102
  99.6 9.5 %all-to-all-done.2.shares_ref = bf16[8,128,128]{2,1,0:T(8,128)(2,1)S(1)} async-done(((bf16[8,128,128]{2,1,0:T(8,128)(2,1)}), bf16[8,128,128]{2,1,0:T(8,128)(2,1)S(1)}, u32[]{:S(2)}, u32[]{:S(2)}) %all-to-all-start.2) | async-done | bytes 262176 | tf_op jit(solution)/shard_map/all_to_all | solution.py:190
  109.0 0.8 shard_map.104
  (9 shorter events, 0.1 us)
Async XLA Ops:
  2.4 21.2 %collective-permute-start = (bf16[256,128]{1,0:T(8,128)(2,1)S(1)}, bf16[256,128]{1,0:T(8,128)(2,1)S(1)}, u32[]{:S(2)}, u32[]{:S(2)}) collective-permute-start(bf16[256,128]{1,0:T(8,128)(2,1)S(1)} %get-tuple-element.12.near), channel_id=1, source_target_pairs={{0,512},{128,640},{256,768},{384,896},{512,0},{640,128},{768,256},... | collective-permute-start | bytes 196616 | tf_op jit(solution)/shard_map/ppermute | solution.py:184
  13.3 10.2 %copy-start = (s32[1,1,160]{2,1,0:T(1,128)S(1)}, s32[1,1,160]{2,1,0:T(1,128)}, u32[]{:S(2)}) copy-start(s32[1,1,160]{2,1,0:T(1,128)} %param.13) | copy-start | bytes 1924
  13.3 10.2 %copy-start.1 = (s32[1,1,160]{2,1,0:T(1,128)S(1)}, s32[1,1,160]{2,1,0:T(1,128)}, u32[]{:S(2)}) copy-start(s32[1,1,160]{2,1,0:T(1,128)} %param.14) | copy-start | bytes 1924
  15.8 20.2 %all-to-all-start = ((bf16[8,128,128]{2,1,0:T(8,128)(2,1)}), bf16[8,128,128]{2,1,0:T(8,128)(2,1)S(1)}, u32[]{:S(2)}, u32[]{:S(2)}) async-start(bf16[8,128,128]{2,1,0:T(8,128)(2,1)} %bitcast.9), calls=%async_computation | async-start | bytes 524288 | tf_op jit(solution)/shard_map/all_to_all | solution.py:190
  23.6 15.8 %collective-permute-start.3 = (bf16[512,128]{1,0:T(8,128)(2,1)S(1)}, bf16[512,128]{1,0:T(8,128)(2,1)S(1)}, u32[]{:S(2)}, u32[]{:S(2)}) collective-permute-start(bf16[512,128]{1,0:T(8,128)(2,1)S(1)} %shard_map.97.after_ref), channel_id=1, source_target_pairs={{0,384},{128,256},{256,128},{384,0},{512,896},{640,768},{768,640},... | collective-permute-start | bytes 393224 | tf_op jit(solution)/shard_map/ppermute | solution.py:184
  31.5 9.7 %collective-permute-start.2 = (bf16[512,128]{1,0:T(8,128)(2,1)S(1)}, bf16[512,128]{1,0:T(8,128)(2,1)S(1)}, u32[]{:S(2)}, u32[]{:S(2)}) collective-permute-start(bf16[512,128]{1,0:T(8,128)(2,1)S(1)} %shard_map.97.after_ref), channel_id=1, source_target_pairs={{0,256},{128,384},{256,0},{384,128},{512,768},{640,896},{768,512},... | collective-permute-start | bytes 393224 | tf_op jit(solution)/shard_map/ppermute | solution.py:184
  33.5 9.4 %collective-permute-start.1 = (bf16[512,128]{1,0:T(8,128)(2,1)S(1)}, bf16[512,128]{1,0:T(8,128)(2,1)S(1)}, u32[]{:S(2)}, u32[]{:S(2)}) collective-permute-start(bf16[512,128]{1,0:T(8,128)(2,1)S(1)} %shard_map.97.after_ref), channel_id=1, source_target_pairs={{0,128},{128,0},{256,384},{384,256},{512,640},{640,512},{768,896},... | collective-permute-start | bytes 393224 | tf_op jit(solution)/shard_map/ppermute | solution.py:184
  36.0 11.1 %collective-permute-start.4 = (bf16[128,128]{1,0:T(8,128)(2,1)S(1)}, bf16[128,128]{1,0:T(8,128)(2,1)S(1)}, u32[]{:S(2)}, u32[]{:S(2)}) collective-permute-start(bf16[128,128]{1,0:T(8,128)(2,1)S(1)} %shard_map.99.own), channel_id=1, source_target_pairs={{0,128},{128,0},{256,384},{384,256},{512,640},{640,512},{768,896},... | collective-permute-start | bytes 98312 | tf_op jit(solution)/shard_map/ppermute | solution.py:184
  47.1 36.8 %all-to-all-start.1 = ((bf16[8,512,128]{2,1,0:T(8,128)(2,1)}), bf16[8,512,128]{2,1,0:T(8,128)(2,1)S(1)}, u32[]{:S(2)}, u32[]{:S(2)}) async-start(bf16[8,512,128]{2,1,0:T(8,128)(2,1)} %get-tuple-element.16), calls=%async_computation.1 | async-start | bytes 2097152 | tf_op jit(solution)/shard_map/all_to_all | solution.py:190
  54.9 6.7 %collective-permute-start.6 = (bf16[128,128]{1,0:T(8,128)(2,1)S(1)}, bf16[128,128]{1,0:T(8,128)(2,1)S(1)}, u32[]{:S(2)}, u32[]{:S(2)}) collective-permute-start(bf16[128,128]{1,0:T(8,128)(2,1)S(1)} %get-tuple-element.21), channel_id=1, source_target_pairs={{0,256},{128,384},{256,0},{384,128},{512,768},{640,896},{768,512},... | collective-permute-start | bytes 98312 | tf_op jit(solution)/shard_map/ppermute | solution.py:184
  61.6 9.9 %collective-permute-start.7 = (bf16[128,128]{1,0:T(8,128)(2,1)S(1)}, bf16[128,128]{1,0:T(8,128)(2,1)S(1)}, u32[]{:S(2)}, u32[]{:S(2)}) collective-permute-start(bf16[128,128]{1,0:T(8,128)(2,1)S(1)} %add_convert_fusion.1), channel_id=1, source_target_pairs={{0,512},{128,640},{256,768},{384,896},{512,0},{640,128},{768,256},... | collective-permute-start | bytes 98312 | tf_op jit(solution)/shard_map/ppermute | solution.py:184
  71.4 23.0 %collective-permute-start.8 = (bf16[128,128]{1,0:T(8,128)(2,1)S(1)}, bf16[128,128]{1,0:T(8,128)(2,1)S(1)}, u32[]{:S(2)}, u32[]{:S(2)}) collective-permute-start(bf16[128,128]{1,0:T(8,128)(2,1)S(1)} %add_convert_fusion.own), channel_id=1, source_target_pairs={{0,8},{8,0},{16,24},{24,16},{32,40},{40,32},{48,56},{56,48},{64,72... | collective-permute-start | bytes 98312 | tf_op jit(solution)/shard_map/ppermute | solution.py:187
  84.0 14.9 %collective-permute-start.5 = (bf16[256,128]{1,0:T(8,128)(2,1)S(1)}, bf16[256,128]{1,0:T(8,128)(2,1)S(1)}, u32[]{:S(2)}, u32[]{:S(2)}) collective-permute-start(bf16[256,128]{1,0:T(8,128)(2,1)S(1)} %get-tuple-element.18.after_ref), channel_id=1, source_target_pairs={{0,8},{8,0},{16,24},{24,16},{32,40},{40,32},{48,56},{56,48},{64,72... | collective-permute-start | bytes 196616 | tf_op jit(solution)/shard_map/ppermute | solution.py:187
  95.2 13.8 %all-to-all-start.2 = ((bf16[8,128,128]{2,1,0:T(8,128)(2,1)}), bf16[8,128,128]{2,1,0:T(8,128)(2,1)S(1)}, u32[]{:S(2)}, u32[]{:S(2)}) async-start(bf16[8,128,128]{2,1,0:T(8,128)(2,1)} %shard_map.103), calls=%async_computation.2 | async-start | bytes 524288 | tf_op jit(solution)/shard_map/all_to_all | solution.py:190

commit v8 on v7

--- a/solution.py
+++ b/solution.py
@@ -1,3 +1,5 @@
+import functools
+
 import jax
 import jax.numpy as jnp
 from jax import lax
@@ -6,7 +8,7 @@
 from jax.sharding import PartitionSpec as P
 
 LANES = 128
-GROUP = 8
+GROUP = 4
 CHUNK = 16
 PAIR = 2
 VMEM = pl.BlockSpec(memory_space=pltpu.VMEM)
@@ -81,42 +83,77 @@
     out_ref[...] = total.astype(jnp.bfloat16)
 
 
+def prepare_kernel(
+    blank, live_ref, row_ref, col_ref, after_ref,
+    pairs_ref, order_ref, col_at_ref, row_at_ref, counts, places,
+):
+    block_rows = counts.shape[0]
+    live = live_ref[0]
+    for r in range(block_rows):
+        counts[r] = 0
+    for i in range(order_ref.shape[0]):
+        order_ref[i] = 0
+        col_at_ref[i] = blank
+    for i in range(row_at_ref.shape[0]):
+        row_at_ref[i] = block_rows
+
+    def count(s, carry):
+        r = row_ref[s]
+        counts[r] = counts[r] + 1
+        return carry
+
+    lax.fori_loop(0, live, count, 0)
+    used = 0
+    for r in range(block_rows):
+        places[r] = used
+        used = used + ((counts[r] + 1) & -2)
+    pairs_ref[0] = used >> 1
+
+    def place(s, carry):
+        r = row_ref[s]
+        at = places[r]
+        places[r] = at + 1
+        order_ref[at] = s
+        col_at_ref[at] = col_ref[s]
+        row_at_ref[at >> 1] = r
+        return carry
+
+    lax.fori_loop(0, live, place, 0)
+
+
 def tiles_kernel(
-    live_ref, row_ref, col_ref, tiles_hbm, near, four, got_1, got_2, got_3, out_hbm,
-    tiles, panel, total, done, arrived, written,
+    live_ref, pairs_ref, order_ref, col_ref, row_ref, tiles_hbm, near, four, got_1, got_2, got_3,
+    out_hbm, tiles, panel, total, done, arrived, written,
 ):
     slots, size = tiles.shape[0], tiles.shape[1]
     copies = []
     for k in range(slots // CHUNK):
         part = pl.ds(k * CHUNK, CHUNK)
         copies.append(pltpu.make_async_copy(tiles_hbm.at[part], tiles.at[part], arrived.at[k]))
-        copies[-1].start()
+        pl.when(k * CHUNK < live_ref[0])(copies[-1].start)
     total[...] = jnp.zeros_like(total)
     place = 0
     for part in (near, four, got_1, got_2, got_3):
         for k in range(part.shape[0] // size):
             panel[place] = part[k * size : (k + 1) * size, :]
             place += 1
-    live = live_ref[0]
+    panel[place] = jnp.zeros(panel.shape[1:], jnp.bfloat16)
+    for k in range(slots // CHUNK):
+        pl.when(k * CHUNK < live_ref[0])(copies[k].wait)
 
     def group(g, carry):
-        first = g * GROUP
         terms = []
         for u in range(GROUP):
-            terms.append(
-                jnp.dot(
-                    tiles[first + u], panel[col_ref[first + u]], preferred_element_type=jnp.float32
-                )
-            )
+            at = 2 * (g * GROUP + u)
+            left = jnp.concatenate([tiles[order_ref[at]], tiles[order_ref[at + 1]]], axis=1)
+            right = jnp.concatenate([panel[col_ref[at]], panel[col_ref[at + 1]]], axis=0)
+            terms.append(jnp.dot(left, right, preferred_element_type=jnp.float32))
         for u in range(GROUP):
-            r = row_ref[first + u]
+            r = row_ref[g * GROUP + u]
             total[r] = total[r] + terms[u]
         return carry
 
-    for k in range(slots // CHUNK):
-        copies[k].wait()
-        last = jnp.minimum((k + 1) * CHUNK, live)
-        lax.fori_loop(k * CHUNK // GROUP, (last + GROUP - 1) // GROUP, group, 0)
+    lax.fori_loop(0, (pairs_ref[0] + GROUP - 1) // GROUP, group, 0)
     owners, height = done.shape[0], done.shape[1]
     results = []
     for c in range(owners):
@@ -246,16 +283,33 @@
     away = (tile_col[0, 0] * size // nodes) ^ lax.axis_index("row")
     chunk = (away & 3) * 2 + (away >> 2)
     col_at = chunk * per_owner + tile_col[0, 0] % per_owner
-    row_at = jnp.where(jnp.arange(slots, dtype=jnp.int32) < live, tile_row[0, 0], block_tiles)
+    room = -(-(slots + block_tiles) // (2 * GROUP)) * GROUP
+    pairs, order, cols, rows = pl.pallas_call(
+        functools.partial(prepare_kernel, n_row * per_owner),
+        out_shape=(
+            shape((1,), jnp.int32),
+            shape((2 * room,), jnp.int32),
+            shape((2 * room,), jnp.int32),
+            shape((room,), jnp.int32),
+        ),
+        in_specs=[SMEM] * 3 + [HBM],
+        out_specs=(SMEM,) * 4,
+        scratch_shapes=[
+            pltpu.SMEM((block_tiles,), jnp.int32),
+            pltpu.SMEM((block_tiles,), jnp.int32),
+        ],
+        compiler_params=params(16),
+        cost_estimate=cost(2 * 10**10, slots * 8),
+    )(live.reshape(1), tile_row[0, 0], col_at, packed)
 
     sent = pl.pallas_call(
         tiles_kernel,
         out_shape=shape((n_y, PAIR * nodes, feats), bf),
-        in_specs=[SMEM] * 3 + [HBM] + [VMEM] * 5,
+        in_specs=[SMEM] * 5 + [HBM] + [VMEM] * 5,
         out_specs=HBM,
         scratch_shapes=[
             pltpu.VMEM((slots, size, size), bf),
-            pltpu.VMEM((n_row * per_owner, size, feats), bf),
+            pltpu.VMEM((n_row * per_owner + 1, size, feats), bf),
             pltpu.VMEM((block_tiles + 1, size, feats), f32),
             pltpu.VMEM((n_y, PAIR * nodes, feats), bf),
             pltpu.SemaphoreType.DMA((slots // CHUNK,)),
@@ -263,7 +317,7 @@
         ],
         compiler_params=params(50),
         cost_estimate=cost(2 * 10**10, slots * size * size * 2),
-    )(live.reshape(1), row_at, col_at, tile_data, near, four, got_1, got_2, got_3)
+    )(live.reshape(1), pairs, order, cols, rows, tile_data, near, four, got_1, got_2, got_3)
     sent, share = pl.pallas_call(
         pair_kernel,
         out_shape=(shape(sent.shape, bf), shape((extra, LANES), bf)),

time: 111 us -> 116 us (1.045)
  starting transfers between devices: 72.2 us -> 79.7 us
  waiting for transfers between devices: 25.2 us -> 20.7 us
  Pallas kernels: 10.8 us -> 13.1 us
    ppermute x7, waiting for transfers between devices: 15.5 us -> 10.9 us  [swap(): return lax.ppermute(value, 'row', [(i, i ^ mask) for i in range(n_row)])]
    ppermute x7, starting transfers between devices: 31.2 us -> 34.9 us  [swap(): return lax.ppermute(value, 'row', [(i, i ^ mask) for i in range(n_row)])]
    all_to_all x3, starting transfers between devices: 18.3 us -> 21.3 us  [line_all_to_all(): lax.all_to_all(value, 'col', 0, 0, axis_index_groups=lines, tiled=True)]
    pallas_call x0 -> x1, Pallas kernels: none -> 1.93 us  [shards(): pl.pallas_call(functools.partial(prepare_kernel, n_row * per_owner), out_...]
  transfers between devices with their start and end apart: 12 -> 12, of which waited for: 6 -> 5; matrix products, arithmetic and copies ran while one was open for 0% -> 0% of each run, Pallas kernels for 7% -> 9%
where the time goes in v8:
time: 116 us; the launch traced here: 115 us
  starting transfers between devices  79.7 us (69%)
  waiting for transfers between devices  20.7 us (18%)
  Pallas kernels  13.1 us (11%)
  between operations  1.52 us (1%)
    ppermute x7, starting transfers between devices, swap(): return lax.ppermute(value, 'row', [(i, i ^ mask) for i in range(n_row)])  34.9 us
    ppermute x2, starting transfers between devices, swap_pair(): return lax.ppermute(value, 'col', [(i, i ^ 1) for i in range(n_col)])  23.5 us
    all_to_all x3, starting transfers between devices, line_all_to_all(): lax.all_to_all(value, 'col', 0, 0, axis_index_groups=lines, tiled=True)  21.3 us
    ppermute x7, waiting for transfers between devices, swap(): return lax.ppermute(value, 'row', [(i, i ^ mask) for i in range(n_row)])  10.9 us
    all_to_all x3, waiting for transfers between devices, line_all_to_all(): lax.all_to_all(value, 'col', 0, 0, axis_index_groups=lines, tiled=True)  9.63 us
    pallas_call x1, Pallas kernels, shards(): pl.pallas_call(tiles_kernel, out_shape=shape((n_y, PAIR * nodes, feats),...  4.52 us
    pallas_call x1, Pallas kernels, shards(): pl.pallas_call(weight_kernel, out_shape=(shape((width // LANES * feats, L...  2.43 us
  transfers between devices with their start and end apart: 12, of which 5 were waited for; matrix products, arithmetic and copies ran while one was open for 0% of the time, Pallas kernels for 9%

profile of v8, /device:TPU:6, one launch (start us, length us, event | category | flops | bytes accessed | tf_op | source)
XLA Modules:
  0.0 115.0 jit_solution(1765223547431512852)
XLA Ops:
  0.6 1.8 %shard_map.95 = (bf16[256,128]{1,0:T(8,128)(2,1)S(1)}, f32[8,128]{1,0:T(8,128)S(1)}) custom-call(bf16[256,1024]{1,0:T(8,128)(2,1)} %grad_hbm.3, s32[256,1024]{1,0:T(8,128)} %mask_hbm.3, bf16[128,1024]{1,0:T(8,128)(2,1)} %weight_hbm.1), custom_call_target="tpu_custom_call" | custom-call | flops 67108864 | bytes 2097152 | tf_op jit(solution)/shard_map/pallas_call | solution.py:229
  2.4 10.9 %collective-permute-start = (bf16[256,128]{1,0:T(8,128)(2,1)S(1)}, bf16[256,128]{1,0:T(8,128)(2,1)S(1)}, u32[]{:S(2)}, u32[]{:S(2)}) collective-permute-start(bf16[256,128]{1,0:T(8,128)(2,1)S(1)} %get-tuple-element.18.near), channel_id=1, source_target_pairs={{0,512},{128,640},{256,768},{384,896},{512,0},{640,128},{768,256},... | collective-permute-start | bytes 196616 | tf_op jit(solution)/shard_map/ppermute | solution.py:221
  13.3 0.0 copy-start.1
  13.3 2.4 %shard_map.96 = (bf16[1024,128]{1,0:T(8,128)(2,1)}, f32[8,128]{1,0:T(8,128)S(1)}) custom-call(bf16[256,1024]{1,0:T(8,128)(2,1)} %grad_hbm.3, s32[256,1024]{1,0:T(8,128)} %mask_hbm.3, bf16[256,128]{1,0:T(8,128)(2,1)} %aggregated_hbm.1, f32[8,128]{1,0:T(8,128)S(1)} %get-tuple-element.16.before_ref), custom_call_target="tpu_custom_call" | custom-call | flops 20000000000 | bytes 1048576 | tf_op jit(solution)/shard_map/pallas_call | solution.py:246
  15.8 7.1 %all-to-all-start = ((bf16[8,128,128]{2,1,0:T(8,128)(2,1)}), bf16[8,128,128]{2,1,0:T(8,128)(2,1)S(1)}, u32[]{:S(2)}, u32[]{:S(2)}) async-start(bf16[8,128,128]{2,1,0:T(8,128)(2,1)} %bitcast.9), calls=%async_computation | async-start | bytes 524288 | tf_op jit(solution)/shard_map/all_to_all | solution.py:227
  23.6 0.0 collective-permute-done.four
  23.6 0.0 copy-start
  23.6 7.9 %collective-permute-start.3 = (bf16[512,128]{1,0:T(8,128)(2,1)S(1)}, bf16[512,128]{1,0:T(8,128)(2,1)S(1)}, u32[]{:S(2)}, u32[]{:S(2)}) collective-permute-start(bf16[512,128]{1,0:T(8,128)(2,1)S(1)} %shard_map.97.after_ref), channel_id=1, source_target_pairs={{0,384},{128,256},{256,128},{384,0},{512,896},{640,768},{768,640},... | collective-permute-start | bytes 393224 | tf_op jit(solution)/shard_map/ppermute | solution.py:221
  31.5 1.9 %collective-permute-start.2 = (bf16[512,128]{1,0:T(8,128)(2,1)S(1)}, bf16[512,128]{1,0:T(8,128)(2,1)S(1)}, u32[]{:S(2)}, u32[]{:S(2)}) collective-permute-start(bf16[512,128]{1,0:T(8,128)(2,1)S(1)} %shard_map.97.after_ref), channel_id=1, source_target_pairs={{0,256},{128,384},{256,0},{384,128},{512,768},{640,896},{768,512},... | collective-permute-start | bytes 393224 | tf_op jit(solution)/shard_map/ppermute | solution.py:221
  33.4 2.5 %collective-permute-start.1 = (bf16[512,128]{1,0:T(8,128)(2,1)S(1)}, bf16[512,128]{1,0:T(8,128)(2,1)S(1)}, u32[]{:S(2)}, u32[]{:S(2)}) collective-permute-start(bf16[512,128]{1,0:T(8,128)(2,1)S(1)} %shard_map.97.after_ref), channel_id=1, source_target_pairs={{0,128},{128,0},{256,384},{384,256},{512,640},{640,512},{768,896},... | collective-permute-start | bytes 393224 | tf_op jit(solution)/shard_map/ppermute | solution.py:221
  35.9 1.9 %shard_map.98 = (s32[1]{0:T(128)}, s32[192]{0:T(256)S(1)}, s32[192]{0:T(256)S(1)}, s32[96]{0:T(128)S(1)}) custom-call(s32[1]{0:T(128)} %bitcast.6.live_ref, s32[160]{0:T(256)S(1)} %bitcast.8, s32[160]{0:T(256)S(1)} %fusion.col_ref, bf16[512,128]{1,0:T(8,128)(2,1)S(1)} %shard_map.97.after_ref), custom_call_target="tpu_custom_call" | custom-call | flops 20000000000 | bytes 1280 | tf_op jit(solution)/shard_map/pallas_call | solution.py:287
  37.9 3.4 %collective-permute-start.4 = (bf16[128,128]{1,0:T(8,128)(2,1)S(1)}, bf16[128,128]{1,0:T(8,128)(2,1)S(1)}, u32[]{:S(2)}, u32[]{:S(2)}) collective-permute-start(bf16[128,128]{1,0:T(8,128)(2,1)S(1)} %shard_map.100.own), channel_id=1, source_target_pairs={{0,128},{128,0},{256,384},{384,256},{512,640},{640,512},{768,896},... | collective-permute-start | bytes 98312 | tf_op jit(solution)/shard_map/ppermute | solution.py:221
  41.3 0.0 collective-permute-done.3.got_3
  41.3 0.0 collective-permute-done.2.got_2
  41.3 1.5 %collective-permute-done.1.got_1 = bf16[512,128]{1,0:T(8,128)(2,1)S(1)} collective-permute-done((bf16[512,128]{1,0:T(8,128)(2,1)S(1)}, bf16[512,128]{1,0:T(8,128)(2,1)S(1)}, u32[]{:S(2)}, u32[]{:S(2)}) %collective-permute-start.1) | collective-permute-done | bytes 131104 | tf_op jit(solution)/shard_map/ppermute | solution.py:221
  42.9 4.5 %shard_map.99.sent_in = bf16[8,512,128]{2,1,0:T(8,128)(2,1)} custom-call(s32[1]{0:T(128)} %bitcast.7.live_ref, s32[1]{0:T(128)} %get-tuple-element.19.pairs_ref, s32[192]{0:T(256)S(1)} %get-tuple-element.20.order_ref, s32[192]{0:T(256)S(1)} %get-tuple-element.21.col_ref, s32[96]{0:T(128)S(1)} %get-tuple-element.22.row_ref, bf16[160,128,128]{2,1,0:T(8,128)(2,1)} %bitcast.11, ...), custom_call_target="tpu_custom_call" | custom-call | flops 20000000000 | bytes 5242880 | tf_op jit(solution)/shard_map/pallas_call | solution.py:305
  47.4 0.0 collective-permute-done.4.other
  47.4 10.7 %all-to-all-start.1 = ((bf16[8,512,128]{2,1,0:T(8,128)(2,1)}), bf16[8,512,128]{2,1,0:T(8,128)(2,1)S(1)}, u32[]{:S(2)}, u32[]{:S(2)}) async-start(bf16[8,512,128]{2,1,0:T(8,128)(2,1)} %get-tuple-element.24), calls=%async_computation.1 | async-start | bytes 2097152 | tf_op jit(solution)/shard_map/all_to_all | solution.py:227
  58.2 6.1 %collective-permute-start.6 = (bf16[128,128]{1,0:T(8,128)(2,1)S(1)}, bf16[128,128]{1,0:T(8,128)(2,1)S(1)}, u32[]{:S(2)}, u32[]{:S(2)}) collective-permute-start(bf16[128,128]{1,0:T(8,128)(2,1)S(1)} %get-tuple-element.29), channel_id=1, source_target_pairs={{0,256},{128,384},{256,0},{384,128},{512,768},{640,896},{768,512},... | collective-permute-start | bytes 98312 | tf_op jit(solution)/shard_map/ppermute | solution.py:221
  64.2 1.9 %collective-permute-done.6 = bf16[128,128]{1,0:T(8,128)(2,1)S(1)} collective-permute-done((bf16[128,128]{1,0:T(8,128)(2,1)S(1)}, bf16[128,128]{1,0:T(8,128)(2,1)S(1)}, u32[]{:S(2)}, u32[]{:S(2)}) %collective-permute-start.6) | collective-permute-done | bytes 32800 | tf_op jit(solution)/shard_map/ppermute | solution.py:221
  66.1 2.2 %collective-permute-start.7 = (bf16[128,128]{1,0:T(8,128)(2,1)S(1)}, bf16[128,128]{1,0:T(8,128)(2,1)S(1)}, u32[]{:S(2)}, u32[]{:S(2)}) collective-permute-start(bf16[128,128]{1,0:T(8,128)(2,1)S(1)} %add_convert_fusion.1), channel_id=1, source_target_pairs={{0,512},{128,640},{256,768},{384,896},{512,0},{640,128},{768,256},... | collective-permute-start | bytes 98312 | tf_op jit(solution)/shard_map/ppermute | solution.py:221
  68.4 7.5 %collective-permute-done.7 = bf16[128,128]{1,0:T(8,128)(2,1)S(1)} collective-permute-done((bf16[128,128]{1,0:T(8,128)(2,1)S(1)}, bf16[128,128]{1,0:T(8,128)(2,1)S(1)}, u32[]{:S(2)}, u32[]{:S(2)}) %collective-permute-start.7) | collective-permute-done | bytes 32800 | tf_op jit(solution)/shard_map/ppermute | solution.py:221
  75.9 13.0 %collective-permute-start.8 = (bf16[128,128]{1,0:T(8,128)(2,1)S(1)}, bf16[128,128]{1,0:T(8,128)(2,1)S(1)}, u32[]{:S(2)}, u32[]{:S(2)}) collective-permute-start(bf16[128,128]{1,0:T(8,128)(2,1)S(1)} %add_convert_fusion.own), channel_id=1, source_target_pairs={{0,8},{8,0},{16,24},{24,16},{32,40},{40,32},{48,56},{56,48},{64,72... | collective-permute-start | bytes 98312 | tf_op jit(solution)/shard_map/ppermute | solution.py:224
  88.8 0.0 all-to-all-done.1.got_ref
  88.8 0.1 shard_map.102
  89.0 10.6 %collective-permute-start.5 = (bf16[256,128]{1,0:T(8,128)(2,1)S(1)}, bf16[256,128]{1,0:T(8,128)(2,1)S(1)}, u32[]{:S(2)}, u32[]{:S(2)}) collective-permute-start(bf16[256,128]{1,0:T(8,128)(2,1)S(1)} %get-tuple-element.26.after_ref), channel_id=1, source_target_pairs={{0,8},{8,0},{16,24},{24,16},{32,40},{40,32},{48,56},{56,48},{64,72... | collective-permute-start | bytes 196616 | tf_op jit(solution)/shard_map/ppermute | solution.py:224
  99.6 0.7 shard_map.104
  100.3 3.4 %all-to-all-start.2 = ((bf16[8,128,128]{2,1,0:T(8,128)(2,1)}), bf16[8,128,128]{2,1,0:T(8,128)(2,1)S(1)}, u32[]{:S(2)}, u32[]{:S(2)}) async-start(bf16[8,128,128]{2,1,0:T(8,128)(2,1)} %shard_map.104), calls=%async_computation.2 | async-start | bytes 524288 | tf_op jit(solution)/shard_map/all_to_all | solution.py:227
  103.7 0.1 collective-permute-done.5.got_ref
  103.9 0.6 shard_map.103
  104.5 9.6 %all-to-all-done.2.shares_ref = bf16[8,128,128]{2,1,0:T(8,128)(2,1)S(1)} async-done(((bf16[8,128,128]{2,1,0:T(8,128)(2,1)}), bf16[8,128,128]{2,1,0:T(8,128)(2,1)S(1)}, u32[]{:S(2)}, u32[]{:S(2)}) %all-to-all-start.2) | async-done | bytes 262176 | tf_op jit(solution)/shard_map/all_to_all | solution.py:227
  114.1 0.8 shard_map.105
  (10 shorter events, 0.1 us)
Async XLA Ops:
  2.4 21.2 %collective-permute-start = (bf16[256,128]{1,0:T(8,128)(2,1)S(1)}, bf16[256,128]{1,0:T(8,128)(2,1)S(1)}, u32[]{:S(2)}, u32[]{:S(2)}) collective-permute-start(bf16[256,128]{1,0:T(8,128)(2,1)S(1)} %get-tuple-element.18.near), channel_id=1, source_target_pairs={{0,512},{128,640},{256,768},{384,896},{512,0},{640,128},{768,256},... | collective-permute-start | bytes 196616 | tf_op jit(solution)/shard_map/ppermute | solution.py:221
  13.3 9.6 %copy-start.1 = (s32[1,1,160]{2,1,0:T(1,128)S(1)}, s32[1,1,160]{2,1,0:T(1,128)}, u32[]{:S(2)}) copy-start(s32[1,1,160]{2,1,0:T(1,128)} %param.14) | copy-start | bytes 1924
  15.8 22.1 %all-to-all-start = ((bf16[8,128,128]{2,1,0:T(8,128)(2,1)}), bf16[8,128,128]{2,1,0:T(8,128)(2,1)S(1)}, u32[]{:S(2)}, u32[]{:S(2)}) async-start(bf16[8,128,128]{2,1,0:T(8,128)(2,1)} %bitcast.9), calls=%async_computation | async-start | bytes 524288 | tf_op jit(solution)/shard_map/all_to_all | solution.py:227
  23.6 12.3 %copy-start = (s32[1,1,160]{2,1,0:T(1,128)S(1)}, s32[1,1,160]{2,1,0:T(1,128)}, u32[]{:S(2)}) copy-start(s32[1,1,160]{2,1,0:T(1,128)} %param.13) | copy-start | bytes 1924
  23.6 17.7 %collective-permute-start.3 = (bf16[512,128]{1,0:T(8,128)(2,1)S(1)}, bf16[512,128]{1,0:T(8,128)(2,1)S(1)}, u32[]{:S(2)}, u32[]{:S(2)}) collective-permute-start(bf16[512,128]{1,0:T(8,128)(2,1)S(1)} %shard_map.97.after_ref), channel_id=1, source_target_pairs={{0,384},{128,256},{256,128},{384,0},{512,896},{640,768},{768,640},... | collective-permute-start | bytes 393224 | tf_op jit(solution)/shard_map/ppermute | solution.py:221
  31.5 9.8 %collective-permute-start.2 = (bf16[512,128]{1,0:T(8,128)(2,1)S(1)}, bf16[512,128]{1,0:T(8,128)(2,1)S(1)}, u32[]{:S(2)}, u32[]{:S(2)}) collective-permute-start(bf16[512,128]{1,0:T(8,128)(2,1)S(1)} %shard_map.97.after_ref), channel_id=1, source_target_pairs={{0,256},{128,384},{256,0},{384,128},{512,768},{640,896},{768,512},... | collective-permute-start | bytes 393224 | tf_op jit(solution)/shard_map/ppermute | solution.py:221
  33.4 9.4 %collective-permute-start.1 = (bf16[512,128]{1,0:T(8,128)(2,1)S(1)}, bf16[512,128]{1,0:T(8,128)(2,1)S(1)}, u32[]{:S(2)}, u32[]{:S(2)}) collective-permute-start(bf16[512,128]{1,0:T(8,128)(2,1)S(1)} %shard_map.97.after_ref), channel_id=1, source_target_pairs={{0,128},{128,0},{256,384},{384,256},{512,640},{640,512},{768,896},... | collective-permute-start | bytes 393224 | tf_op jit(solution)/shard_map/ppermute | solution.py:221
  37.9 9.5 %collective-permute-start.4 = (bf16[128,128]{1,0:T(8,128)(2,1)S(1)}, bf16[128,128]{1,0:T(8,128)(2,1)S(1)}, u32[]{:S(2)}, u32[]{:S(2)}) collective-permute-start(bf16[128,128]{1,0:T(8,128)(2,1)S(1)} %shard_map.100.own), channel_id=1, source_target_pairs={{0,128},{128,0},{256,384},{384,256},{512,640},{640,512},{768,896},... | collective-permute-start | bytes 98312 | tf_op jit(solution)/shard_map/ppermute | solution.py:221
  47.4 41.4 %all-to-all-start.1 = ((bf16[8,512,128]{2,1,0:T(8,128)(2,1)}), bf16[8,512,128]{2,1,0:T(8,128)(2,1)S(1)}, u32[]{:S(2)}, u32[]{:S(2)}) async-start(bf16[8,512,128]{2,1,0:T(8,128)(2,1)} %get-tuple-element.24), calls=%async_computation.1 | async-start | bytes 2097152 | tf_op jit(solution)/shard_map/all_to_all | solution.py:227
  58.2 8.0 %collective-permute-start.6 = (bf16[128,128]{1,0:T(8,128)(2,1)S(1)}, bf16[128,128]{1,0:T(8,128)(2,1)S(1)}, u32[]{:S(2)}, u32[]{:S(2)}) collective-permute-start(bf16[128,128]{1,0:T(8,128)(2,1)S(1)} %get-tuple-element.29), channel_id=1, source_target_pairs={{0,256},{128,384},{256,0},{384,128},{512,768},{640,896},{768,512},... | collective-permute-start | bytes 98312 | tf_op jit(solution)/shard_map/ppermute | solution.py:221
  66.1 9.7 %collective-permute-start.7 = (bf16[128,128]{1,0:T(8,128)(2,1)S(1)}, bf16[128,128]{1,0:T(8,128)(2,1)S(1)}, u32[]{:S(2)}, u32[]{:S(2)}) collective-permute-start(bf16[128,128]{1,0:T(8,128)(2,1)S(1)} %add_convert_fusion.1), channel_id=1, source_target_pairs={{0,512},{128,640},{256,768},{384,896},{512,0},{640,128},{768,256},... | collective-permute-start | bytes 98312 | tf_op jit(solution)/shard_map/ppermute | solution.py:221
  75.9 23.7 %collective-permute-start.8 = (bf16[128,128]{1,0:T(8,128)(2,1)S(1)}, bf16[128,128]{1,0:T(8,128)(2,1)S(1)}, u32[]{:S(2)}, u32[]{:S(2)}) collective-permute-start(bf16[128,128]{1,0:T(8,128)(2,1)S(1)} %add_convert_fusion.own), channel_id=1, source_target_pairs={{0,8},{8,0},{16,24},{24,16},{32,40},{40,32},{48,56},{56,48},{64,72... | collective-permute-start | bytes 98312 | tf_op jit(solution)/shard_map/ppermute | solution.py:224
  89.0 14.9 %collective-permute-start.5 = (bf16[256,128]{1,0:T(8,128)(2,1)S(1)}, bf16[256,128]{1,0:T(8,128)(2,1)S(1)}, u32[]{:S(2)}, u32[]{:S(2)}) collective-permute-start(bf16[256,128]{1,0:T(8,128)(2,1)S(1)} %get-tuple-element.26.after_ref), channel_id=1, source_target_pairs={{0,8},{8,0},{16,24},{24,16},{32,40},{40,32},{48,56},{56,48},{64,72... | collective-permute-start | bytes 196616 | tf_op jit(solution)/shard_map/ppermute | solution.py:224
  100.3 13.8 %all-to-all-start.2 = ((bf16[8,128,128]{2,1,0:T(8,128)(2,1)}), bf16[8,128,128]{2,1,0:T(8,128)(2,1)S(1)}, u32[]{:S(2)}, u32[]{:S(2)}) async-start(bf16[8,128,128]{2,1,0:T(8,128)(2,1)} %shard_map.104), calls=%async_computation.2 | async-start | bytes 524288 | tf_op jit(solution)/shard_map/all_to_all | solution.py:227

commit v9 on v7

--- a/solution.py
+++ b/solution.py
@@ -6,8 +6,7 @@
 from jax.sharding import PartitionSpec as P
 
 LANES = 128
-GROUP = 8
-CHUNK = 16
+GROUP = 32
 PAIR = 2
 VMEM = pl.BlockSpec(memory_space=pltpu.VMEM)
 SMEM = pl.BlockSpec(memory_space=pltpu.SMEM)
@@ -85,21 +84,24 @@
     live_ref, row_ref, col_ref, tiles_hbm, near, four, got_1, got_2, got_3, out_hbm,
     tiles, panel, total, done, arrived, written,
 ):
-    slots, size = tiles.shape[0], tiles.shape[1]
-    copies = []
-    for k in range(slots // CHUNK):
-        part = pl.ds(k * CHUNK, CHUNK)
-        copies.append(pltpu.make_async_copy(tiles_hbm.at[part], tiles.at[part], arrived.at[k]))
-        copies[-1].start()
+    size = tiles.shape[1]
+    groups = (live_ref[0] + GROUP - 1) // GROUP
+
+    def fetch(g):
+        part = pl.ds(g * GROUP, GROUP)
+        return pltpu.make_async_copy(tiles_hbm.at[part], tiles.at[part], arrived.at[g])
+
+    for g in range(tiles.shape[0] // GROUP):
+        pl.when(g < groups)(fetch(g).start)
     total[...] = jnp.zeros_like(total)
     place = 0
     for part in (near, four, got_1, got_2, got_3):
         for k in range(part.shape[0] // size):
             panel[place] = part[k * size : (k + 1) * size, :]
             place += 1
-    live = live_ref[0]
 
     def group(g, carry):
+        fetch(g).wait()
         first = g * GROUP
         terms = []
         for u in range(GROUP):
@@ -113,10 +115,7 @@
             total[r] = total[r] + terms[u]
         return carry
 
-    for k in range(slots // CHUNK):
-        copies[k].wait()
-        last = jnp.minimum((k + 1) * CHUNK, live)
-        lax.fori_loop(k * CHUNK // GROUP, (last + GROUP - 1) // GROUP, group, 0)
+    lax.fori_loop(0, groups, group, 0)
     owners, height = done.shape[0], done.shape[1]
     results = []
     for c in range(owners):
@@ -258,7 +257,7 @@
             pltpu.VMEM((n_row * per_owner, size, feats), bf),
             pltpu.VMEM((block_tiles + 1, size, feats), f32),
             pltpu.VMEM((n_y, PAIR * nodes, feats), bf),
-            pltpu.SemaphoreType.DMA((slots // CHUNK,)),
+            pltpu.SemaphoreType.DMA((slots // GROUP,)),
             pltpu.SemaphoreType.DMA((n_y,)),
         ],
         compiler_params=params(50),

time: 111 us -> 110 us (level)
    all_to_all x3, waiting for transfers between devices: 9.46 us -> 7.26 us  [line_all_to_all(): lax.all_to_all(value, 'col', 0, 0, axis_index_groups=lines, tiled=True)]
    ppermute x2, waiting for transfers between devices: 0.3 us -> 2.51 us  [swap_pair(): return lax.ppermute(value, 'col', [(i, i ^ 1) for i in range(n_col)])]
  transfers between devices with their start and end apart: 12 -> 12, of which waited for: 6 -> 6; matrix products, arithmetic and copies ran while one was open for 0% -> 0% of each run, Pallas kernels for 7% -> 8%
where the time goes in v9:
time: 110 us; the launch traced here: 109 us
  starting transfers between devices  72.1 us (66%)
  waiting for transfers between devices  24.4 us (22%)
  Pallas kernels  11 us (10%)
  between operations  1.51 us (1%)
    ppermute x7, starting transfers between devices, swap(): return lax.ppermute(value, 'row', [(i, i ^ mask) for i in range(n_row)])  31.9 us
    ppermute x2, starting transfers between devices, swap_pair(): return lax.ppermute(value, 'col', [(i, i ^ 1) for i in range(n_col)])  22.7 us
    all_to_all x3, starting transfers between devices, line_all_to_all(): lax.all_to_all(value, 'col', 0, 0, axis_index_groups=lines, tiled=True)  17.6 us
    ppermute x7, waiting for transfers between devices, swap(): return lax.ppermute(value, 'row', [(i, i ^ mask) for i in range(n_row)])  14.6 us
    all_to_all x3, waiting for transfers between devices, line_all_to_all(): lax.all_to_all(value, 'col', 0, 0, axis_index_groups=lines, tiled=True)  7.26 us
    pallas_call x1, Pallas kernels, shards(): pl.pallas_call(tiles_kernel, out_shape=shape((n_y, PAIR * nodes, feats),...  4.36 us
    ppermute x2, waiting for transfers between devices, swap_pair(): return lax.ppermute(value, 'col', [(i, i ^ 1) for i in range(n_col)])  2.51 us
    pallas_call x1, Pallas kernels, shards(): pl.pallas_call(weight_kernel, out_shape=(shape((width // LANES * feats, L...  2.43 us
  transfers between devices with their start and end apart: 12, of which 6 were waited for; matrix products, arithmetic and copies ran while one was open for 0% of the time, Pallas kernels for 8%

profile of v9, /device:TPU:6, one launch (start us, length us, event | category | flops | bytes accessed | tf_op | source)
XLA Modules:
  0.0 109.1 jit_solution(5347103339130054650)
XLA Ops:
  0.6 1.8 %shard_map.95 = (bf16[256,128]{1,0:T(8,128)(2,1)S(1)}, f32[8,128]{1,0:T(8,128)S(1)}) custom-call(bf16[256,1024]{1,0:T(8,128)(2,1)} %grad_hbm.3, s32[256,1024]{1,0:T(8,128)} %mask_hbm.3, bf16[128,1024]{1,0:T(8,128)(2,1)} %weight_hbm.1), custom_call_target="tpu_custom_call" | custom-call | flops 67108864 | bytes 2097152 | tf_op jit(solution)/shard_map/pallas_call | solution.py:191
  2.4 10.9 %collective-permute-start = (bf16[256,128]{1,0:T(8,128)(2,1)S(1)}, bf16[256,128]{1,0:T(8,128)(2,1)S(1)}, u32[]{:S(2)}, u32[]{:S(2)}) collective-permute-start(bf16[256,128]{1,0:T(8,128)(2,1)S(1)} %get-tuple-element.12.near), channel_id=1, source_target_pairs={{0,512},{128,640},{256,768},{384,896},{512,0},{640,128},{768,256},... | collective-permute-start | bytes 196616 | tf_op jit(solution)/shard_map/ppermute | solution.py:183
  13.3 0.0 copy-start
  13.3 0.0 copy-start.1
  13.4 2.4 %shard_map.96 = (bf16[1024,128]{1,0:T(8,128)(2,1)}, f32[8,128]{1,0:T(8,128)S(1)}) custom-call(bf16[256,1024]{1,0:T(8,128)(2,1)} %grad_hbm.3, s32[256,1024]{1,0:T(8,128)} %mask_hbm.3, bf16[256,128]{1,0:T(8,128)(2,1)} %aggregated_hbm.1, f32[8,128]{1,0:T(8,128)S(1)} %get-tuple-element.13.before_ref), custom_call_target="tpu_custom_call" | custom-call | flops 20000000000 | bytes 1048576 | tf_op jit(solution)/shard_map/pallas_call | solution.py:208
  15.8 7.1 %all-to-all-start = ((bf16[8,128,128]{2,1,0:T(8,128)(2,1)}), bf16[8,128,128]{2,1,0:T(8,128)(2,1)S(1)}, u32[]{:S(2)}, u32[]{:S(2)}) async-start(bf16[8,128,128]{2,1,0:T(8,128)(2,1)} %bitcast.9), calls=%async_computation | async-start | bytes 524288 | tf_op jit(solution)/shard_map/all_to_all | solution.py:189
  23.6 0.0 collective-permute-done.four
  23.6 7.9 %collective-permute-start.3 = (bf16[512,128]{1,0:T(8,128)(2,1)S(1)}, bf16[512,128]{1,0:T(8,128)(2,1)S(1)}, u32[]{:S(2)}, u32[]{:S(2)}) collective-permute-start(bf16[512,128]{1,0:T(8,128)(2,1)S(1)} %shard_map.97.after_ref), channel_id=1, source_target_pairs={{0,384},{128,256},{256,128},{384,0},{512,896},{640,768},{768,640},... | collective-permute-start | bytes 393224 | tf_op jit(solution)/shard_map/ppermute | solution.py:183
  31.5 1.9 %collective-permute-start.2 = (bf16[512,128]{1,0:T(8,128)(2,1)S(1)}, bf16[512,128]{1,0:T(8,128)(2,1)S(1)}, u32[]{:S(2)}, u32[]{:S(2)}) collective-permute-start(bf16[512,128]{1,0:T(8,128)(2,1)S(1)} %shard_map.97.after_ref), channel_id=1, source_target_pairs={{0,256},{128,384},{256,0},{384,128},{512,768},{640,896},{768,512},... | collective-permute-start | bytes 393224 | tf_op jit(solution)/shard_map/ppermute | solution.py:183
  33.5 2.5 %collective-permute-start.1 = (bf16[512,128]{1,0:T(8,128)(2,1)S(1)}, bf16[512,128]{1,0:T(8,128)(2,1)S(1)}, u32[]{:S(2)}, u32[]{:S(2)}) collective-permute-start(bf16[512,128]{1,0:T(8,128)(2,1)S(1)} %shard_map.97.after_ref), channel_id=1, source_target_pairs={{0,128},{128,0},{256,384},{384,256},{512,640},{640,512},{768,896},... | collective-permute-start | bytes 393224 | tf_op jit(solution)/shard_map/ppermute | solution.py:183
  35.9 0.0 all-to-all-done.spread_ref
  36.0 3.4 %collective-permute-start.4 = (bf16[128,128]{1,0:T(8,128)(2,1)S(1)}, bf16[128,128]{1,0:T(8,128)(2,1)S(1)}, u32[]{:S(2)}, u32[]{:S(2)}) collective-permute-start(bf16[128,128]{1,0:T(8,128)(2,1)S(1)} %shard_map.99.own), channel_id=1, source_target_pairs={{0,128},{128,0},{256,384},{384,256},{512,640},{640,512},{768,896},... | collective-permute-start | bytes 98312 | tf_op jit(solution)/shard_map/ppermute | solution.py:183
  39.4 0.0 collective-permute-done.3.got_3
  39.4 1.8 %collective-permute-done.2.got_2 = bf16[512,128]{1,0:T(8,128)(2,1)S(1)} collective-permute-done((bf16[512,128]{1,0:T(8,128)(2,1)S(1)}, bf16[512,128]{1,0:T(8,128)(2,1)S(1)}, u32[]{:S(2)}, u32[]{:S(2)}) %collective-permute-start.2) | collective-permute-done | bytes 131104 | tf_op jit(solution)/shard_map/ppermute | solution.py:183
  41.2 1.7 %collective-permute-done.1.got_1 = bf16[512,128]{1,0:T(8,128)(2,1)S(1)} collective-permute-done((bf16[512,128]{1,0:T(8,128)(2,1)S(1)}, bf16[512,128]{1,0:T(8,128)(2,1)S(1)}, u32[]{:S(2)}, u32[]{:S(2)}) %collective-permute-start.1) | collective-permute-done | bytes 131104 | tf_op jit(solution)/shard_map/ppermute | solution.py:183
  42.9 4.4 %shard_map.98.sent_in = bf16[8,512,128]{2,1,0:T(8,128)(2,1)} custom-call(s32[1]{0:T(128)} %bitcast.7.live_ref, s32[160]{0:T(256)S(1)} %get-tuple-element.22.row_ref, s32[160]{0:T(256)S(1)} %get-tuple-element.23.col_ref, bf16[160,128,128]{2,1,0:T(8,128)(2,1)} %bitcast.12, bf16[256,128]{1,0:T(8,128)(2,1)S(1)} %get-tuple-element.12.near, ...), custom_call_target="tpu_custom_call" | custom-call | flops 20000000000 | bytes 5242880 | tf_op jit(solution)/shard_map/pallas_call | solution.py:250
  47.3 0.0 collective-permute-done.4.other
  47.3 7.1 %all-to-all-start.1 = ((bf16[8,512,128]{2,1,0:T(8,128)(2,1)}), bf16[8,512,128]{2,1,0:T(8,128)(2,1)S(1)}, u32[]{:S(2)}, u32[]{:S(2)}) async-start(bf16[8,512,128]{2,1,0:T(8,128)(2,1)} %get-tuple-element.16), calls=%async_computation.1 | async-start | bytes 2097152 | tf_op jit(solution)/shard_map/all_to_all | solution.py:189
  54.3 3.4 %collective-permute-start.6 = (bf16[128,128]{1,0:T(8,128)(2,1)S(1)}, bf16[128,128]{1,0:T(8,128)(2,1)S(1)}, u32[]{:S(2)}, u32[]{:S(2)}) collective-permute-start(bf16[128,128]{1,0:T(8,128)(2,1)S(1)} %get-tuple-element.21), channel_id=1, source_target_pairs={{0,256},{128,384},{256,0},{384,128},{512,768},{640,896},{768,512},... | collective-permute-start | bytes 98312 | tf_op jit(solution)/shard_map/ppermute | solution.py:183
  57.7 3.3 %collective-permute-done.6 = bf16[128,128]{1,0:T(8,128)(2,1)S(1)} collective-permute-done((bf16[128,128]{1,0:T(8,128)(2,1)S(1)}, bf16[128,128]{1,0:T(8,128)(2,1)S(1)}, u32[]{:S(2)}, u32[]{:S(2)}) %collective-permute-start.6) | collective-permute-done | bytes 32800 | tf_op jit(solution)/shard_map/ppermute | solution.py:183
  61.1 1.9 %collective-permute-start.7 = (bf16[128,128]{1,0:T(8,128)(2,1)S(1)}, bf16[128,128]{1,0:T(8,128)(2,1)S(1)}, u32[]{:S(2)}, u32[]{:S(2)}) collective-permute-start(bf16[128,128]{1,0:T(8,128)(2,1)S(1)} %add_convert_fusion.1), channel_id=1, source_target_pairs={{0,512},{128,640},{256,768},{384,896},{512,0},{640,128},{768,256},... | collective-permute-start | bytes 98312 | tf_op jit(solution)/shard_map/ppermute | solution.py:183
  63.0 7.8 %collective-permute-done.7 = bf16[128,128]{1,0:T(8,128)(2,1)S(1)} collective-permute-done((bf16[128,128]{1,0:T(8,128)(2,1)S(1)}, bf16[128,128]{1,0:T(8,128)(2,1)S(1)}, u32[]{:S(2)}, u32[]{:S(2)}) %collective-permute-start.7) | collective-permute-done | bytes 32800 | tf_op jit(solution)/shard_map/ppermute | solution.py:183
  70.8 12.4 %collective-permute-start.8 = (bf16[128,128]{1,0:T(8,128)(2,1)S(1)}, bf16[128,128]{1,0:T(8,128)(2,1)S(1)}, u32[]{:S(2)}, u32[]{:S(2)}) collective-permute-start(bf16[128,128]{1,0:T(8,128)(2,1)S(1)} %add_convert_fusion.own), channel_id=1, source_target_pairs={{0,8},{8,0},{16,24},{24,16},{32,40},{40,32},{48,56},{56,48},{64,72... | collective-permute-start | bytes 98312 | tf_op jit(solution)/shard_map/ppermute | solution.py:186
  83.2 0.0 all-to-all-done.1.got_ref
  83.2 0.1 shard_map.101
  83.3 10.3 %collective-permute-start.5 = (bf16[256,128]{1,0:T(8,128)(2,1)S(1)}, bf16[256,128]{1,0:T(8,128)(2,1)S(1)}, u32[]{:S(2)}, u32[]{:S(2)}) collective-permute-start(bf16[256,128]{1,0:T(8,128)(2,1)S(1)} %get-tuple-element.18.after_ref), channel_id=1, source_target_pairs={{0,8},{8,0},{16,24},{24,16},{32,40},{40,32},{48,56},{56,48},{64,72... | collective-permute-start | bytes 196616 | tf_op jit(solution)/shard_map/ppermute | solution.py:186
  93.7 0.7 shard_map.103
  94.4 3.4 %all-to-all-start.2 = ((bf16[8,128,128]{2,1,0:T(8,128)(2,1)}), bf16[8,128,128]{2,1,0:T(8,128)(2,1)S(1)}, u32[]{:S(2)}, u32[]{:S(2)}) async-start(bf16[8,128,128]{2,1,0:T(8,128)(2,1)} %shard_map.103), calls=%async_computation.2 | async-start | bytes 524288 | tf_op jit(solution)/shard_map/all_to_all | solution.py:189
  97.8 2.5 %collective-permute-done.5.got_ref = bf16[256,128]{1,0:T(8,128)(2,1)S(1)} collective-permute-done((bf16[256,128]{1,0:T(8,128)(2,1)S(1)}, bf16[256,128]{1,0:T(8,128)(2,1)S(1)}, u32[]{:S(2)}, u32[]{:S(2)}) %collective-permute-start.5) | collective-permute-done | bytes 65568 | tf_op jit(solution)/shard_map/ppermute | solution.py:186
  100.3 0.6 shard_map.102
  101.0 7.3 %all-to-all-done.2.shares_ref = bf16[8,128,128]{2,1,0:T(8,128)(2,1)S(1)} async-done(((bf16[8,128,128]{2,1,0:T(8,128)(2,1)}), bf16[8,128,128]{2,1,0:T(8,128)(2,1)S(1)}, u32[]{:S(2)}, u32[]{:S(2)}) %all-to-all-start.2) | async-done | bytes 262176 | tf_op jit(solution)/shard_map/all_to_all | solution.py:189
  108.2 0.8 shard_map.104
  (9 shorter events, 0.1 us)
Async XLA Ops:
  2.4 21.2 %collective-permute-start = (bf16[256,128]{1,0:T(8,128)(2,1)S(1)}, bf16[256,128]{1,0:T(8,128)(2,1)S(1)}, u32[]{:S(2)}, u32[]{:S(2)}) collective-permute-start(bf16[256,128]{1,0:T(8,128)(2,1)S(1)} %get-tuple-element.12.near), channel_id=1, source_target_pairs={{0,512},{128,640},{256,768},{384,896},{512,0},{640,128},{768,256},... | collective-permute-start | bytes 196616 | tf_op jit(solution)/shard_map/ppermute | solution.py:183
  13.3 10.2 %copy-start = (s32[1,1,160]{2,1,0:T(1,128)S(1)}, s32[1,1,160]{2,1,0:T(1,128)}, u32[]{:S(2)}) copy-start(s32[1,1,160]{2,1,0:T(1,128)} %param.13) | copy-start | bytes 1924
  13.3 10.2 %copy-start.1 = (s32[1,1,160]{2,1,0:T(1,128)S(1)}, s32[1,1,160]{2,1,0:T(1,128)}, u32[]{:S(2)}) copy-start(s32[1,1,160]{2,1,0:T(1,128)} %param.14) | copy-start | bytes 1924
  15.8 20.2 %all-to-all-start = ((bf16[8,128,128]{2,1,0:T(8,128)(2,1)}), bf16[8,128,128]{2,1,0:T(8,128)(2,1)S(1)}, u32[]{:S(2)}, u32[]{:S(2)}) async-start(bf16[8,128,128]{2,1,0:T(8,128)(2,1)} %bitcast.9), calls=%async_computation | async-start | bytes 524288 | tf_op jit(solution)/shard_map/all_to_all | solution.py:189
  23.6 15.8 %collective-permute-start.3 = (bf16[512,128]{1,0:T(8,128)(2,1)S(1)}, bf16[512,128]{1,0:T(8,128)(2,1)S(1)}, u32[]{:S(2)}, u32[]{:S(2)}) collective-permute-start(bf16[512,128]{1,0:T(8,128)(2,1)S(1)} %shard_map.97.after_ref), channel_id=1, source_target_pairs={{0,384},{128,256},{256,128},{384,0},{512,896},{640,768},{768,640},... | collective-permute-start | bytes 393224 | tf_op jit(solution)/shard_map/ppermute | solution.py:183
  31.5 9.7 %collective-permute-start.2 = (bf16[512,128]{1,0:T(8,128)(2,1)S(1)}, bf16[512,128]{1,0:T(8,128)(2,1)S(1)}, u32[]{:S(2)}, u32[]{:S(2)}) collective-permute-start(bf16[512,128]{1,0:T(8,128)(2,1)S(1)} %shard_map.97.after_ref), channel_id=1, source_target_pairs={{0,256},{128,384},{256,0},{384,128},{512,768},{640,896},{768,512},... | collective-permute-start | bytes 393224 | tf_op jit(solution)/shard_map/ppermute | solution.py:183
  33.5 9.4 %collective-permute-start.1 = (bf16[512,128]{1,0:T(8,128)(2,1)S(1)}, bf16[512,128]{1,0:T(8,128)(2,1)S(1)}, u32[]{:S(2)}, u32[]{:S(2)}) collective-permute-start(bf16[512,128]{1,0:T(8,128)(2,1)S(1)} %shard_map.97.after_ref), channel_id=1, source_target_pairs={{0,128},{128,0},{256,384},{384,256},{512,640},{640,512},{768,896},... | collective-permute-start | bytes 393224 | tf_op jit(solution)/shard_map/ppermute | solution.py:183
  36.0 11.3 %collective-permute-start.4 = (bf16[128,128]{1,0:T(8,128)(2,1)S(1)}, bf16[128,128]{1,0:T(8,128)(2,1)S(1)}, u32[]{:S(2)}, u32[]{:S(2)}) collective-permute-start(bf16[128,128]{1,0:T(8,128)(2,1)S(1)} %shard_map.99.own), channel_id=1, source_target_pairs={{0,128},{128,0},{256,384},{384,256},{512,640},{640,512},{768,896},... | collective-permute-start | bytes 98312 | tf_op jit(solution)/shard_map/ppermute | solution.py:183
  47.3 35.9 %all-to-all-start.1 = ((bf16[8,512,128]{2,1,0:T(8,128)(2,1)}), bf16[8,512,128]{2,1,0:T(8,128)(2,1)S(1)}, u32[]{:S(2)}, u32[]{:S(2)}) async-start(bf16[8,512,128]{2,1,0:T(8,128)(2,1)} %get-tuple-element.16), calls=%async_computation.1 | async-start | bytes 2097152 | tf_op jit(solution)/shard_map/all_to_all | solution.py:189
  54.3 6.7 %collective-permute-start.6 = (bf16[128,128]{1,0:T(8,128)(2,1)S(1)}, bf16[128,128]{1,0:T(8,128)(2,1)S(1)}, u32[]{:S(2)}, u32[]{:S(2)}) collective-permute-start(bf16[128,128]{1,0:T(8,128)(2,1)S(1)} %get-tuple-element.21), channel_id=1, source_target_pairs={{0,256},{128,384},{256,0},{384,128},{512,768},{640,896},{768,512},... | collective-permute-start | bytes 98312 | tf_op jit(solution)/shard_map/ppermute | solution.py:183
  61.1 9.7 %collective-permute-start.7 = (bf16[128,128]{1,0:T(8,128)(2,1)S(1)}, bf16[128,128]{1,0:T(8,128)(2,1)S(1)}, u32[]{:S(2)}, u32[]{:S(2)}) collective-permute-start(bf16[128,128]{1,0:T(8,128)(2,1)S(1)} %add_convert_fusion.1), channel_id=1, source_target_pairs={{0,512},{128,640},{256,768},{384,896},{512,0},{640,128},{768,256},... | collective-permute-start | bytes 98312 | tf_op jit(solution)/shard_map/ppermute | solution.py:183
  70.8 22.9 %collective-permute-start.8 = (bf16[128,128]{1,0:T(8,128)(2,1)S(1)}, bf16[128,128]{1,0:T(8,128)(2,1)S(1)}, u32[]{:S(2)}, u32[]{:S(2)}) collective-permute-start(bf16[128,128]{1,0:T(8,128)(2,1)S(1)} %add_convert_fusion.own), channel_id=1, source_target_pairs={{0,8},{8,0},{16,24},{24,16},{32,40},{40,32},{48,56},{56,48},{64,72... | collective-permute-start | bytes 98312 | tf_op jit(solution)/shard_map/ppermute | solution.py:186
  83.3 17.0 %collective-permute-start.5 = (bf16[256,128]{1,0:T(8,128)(2,1)S(1)}, bf16[256,128]{1,0:T(8,128)(2,1)S(1)}, u32[]{:S(2)}, u32[]{:S(2)}) collective-permute-start(bf16[256,128]{1,0:T(8,128)(2,1)S(1)} %get-tuple-element.18.after_ref), channel_id=1, source_target_pairs={{0,8},{8,0},{16,24},{24,16},{32,40},{40,32},{48,56},{56,48},{64,72... | collective-permute-start | bytes 196616 | tf_op jit(solution)/shard_map/ppermute | solution.py:186
  94.4 13.8 %all-to-all-start.2 = ((bf16[8,128,128]{2,1,0:T(8,128)(2,1)}), bf16[8,128,128]{2,1,0:T(8,128)(2,1)S(1)}, u32[]{:S(2)}, u32[]{:S(2)}) async-start(bf16[8,128,128]{2,1,0:T(8,128)(2,1)} %shard_map.103), calls=%async_computation.2 | async-start | bytes 524288 | tf_op jit(solution)/shard_map/all_to_all | solution.py:189

commit v10 on v9

--- a/solution.py
+++ b/solution.py
@@ -273,9 +273,9 @@
         cost_estimate=cost(4 * extra * LANES, 4 * extra * LANES * 2),
     )(sent, share, row_1)
     got = line_all_to_all(sent)
-    for mask in (2, 4):
-        share = (share.astype(f32) + swap(share, mask).astype(f32)).astype(bf)
-    far = swap_pair(share)
+    share = (share.astype(f32) + swap_pair(share).astype(f32)).astype(bf)
+    share = (share.astype(f32) + swap(share, 2).astype(f32)).astype(bf)
+    far = swap(share, 4)
 
     half = (lax.axis_index("col") & (PAIR - 1)).astype(jnp.int32).reshape(1)
     keep, send = pl.pallas_call(

time: 110 us -> 112 us (1.018)
  starting transfers between devices: 72.1 us -> 76.7 us
  waiting for transfers between devices: 24.4 us -> 22.2 us
    ppermute x7, waiting for transfers between devices: 14.6 us -> 8.26 us  [swap(): return lax.ppermute(value, 'row', [(i, i ^ mask) for i in range(n_row)])]
    all_to_all x3, waiting for transfers between devices: 7.26 us -> 11.1 us  [line_all_to_all(): lax.all_to_all(value, 'col', 0, 0, axis_index_groups=lines, tiled=True)]
    all_to_all x3, starting transfers between devices: 17.6 us -> 20.4 us  [line_all_to_all(): lax.all_to_all(value, 'col', 0, 0, axis_index_groups=lines, tiled=True)]
  transfers between devices with their start and end apart: 12 -> 12, of which waited for: 6 -> 6; matrix products, arithmetic and copies ran while one was open for 0% -> 0% of each run, Pallas kernels for 8% -> 7%
where the time goes in v10:
time: 112 us; the launch traced here: 111 us
  starting transfers between devices  76.7 us (68%)
  waiting for transfers between devices  22.2 us (20%)
  Pallas kernels  10.5 us (9%)
  between operations  1.5 us (1%)
    ppermute x7, starting transfers between devices, swap(): return lax.ppermute(value, 'row', [(i, i ^ mask) for i in range(n_row)])  32.5 us
    ppermute x2, starting transfers between devices, swap_pair(): return lax.ppermute(value, 'col', [(i, i ^ 1) for i in range(n_col)])  23.7 us
    all_to_all x3, starting transfers between devices, line_all_to_all(): lax.all_to_all(value, 'col', 0, 0, axis_index_groups=lines, tiled=True)  20.4 us
    all_to_all x3, waiting for transfers between devices, line_all_to_all(): lax.all_to_all(value, 'col', 0, 0, axis_index_groups=lines, tiled=True)  11.1 us
    ppermute x7, waiting for transfers between devices, swap(): return lax.ppermute(value, 'row', [(i, i ^ mask) for i in range(n_row)])  8.26 us
    pallas_call x1, Pallas kernels, shards(): pl.pallas_call(tiles_kernel, out_shape=shape((n_y, PAIR * nodes, feats),...  3.88 us
    ppermute x2, waiting for transfers between devices, swap_pair(): return lax.ppermute(value, 'col', [(i, i ^ 1) for i in range(n_col)])  2.79 us
    pallas_call x1, Pallas kernels, shards(): pl.pallas_call(weight_kernel, out_shape=(shape((width // LANES * feats, L...  2.43 us
  transfers between devices with their start and end apart: 12, of which 6 were waited for; matrix products, arithmetic and copies ran while one was open for 0% of the time, Pallas kernels for 7%

profile of v10, /device:TPU:6, one launch (start us, length us, event | category | flops | bytes accessed | tf_op | source)
XLA Modules:
  0.0 111.0 jit_solution(11012169080453401173)
XLA Ops:
  0.6 1.8 %shard_map.95 = (bf16[256,128]{1,0:T(8,128)(2,1)S(1)}, f32[8,128]{1,0:T(8,128)S(1)}) custom-call(bf16[256,1024]{1,0:T(8,128)(2,1)} %grad_hbm.3, s32[256,1024]{1,0:T(8,128)} %mask_hbm.3, bf16[128,1024]{1,0:T(8,128)(2,1)} %weight_hbm.1), custom_call_target="tpu_custom_call" | custom-call | flops 67108864 | bytes 2097152 | tf_op jit(solution)/shard_map/pallas_call | solution.py:191
  2.4 10.9 %collective-permute-start = (bf16[256,128]{1,0:T(8,128)(2,1)S(1)}, bf16[256,128]{1,0:T(8,128)(2,1)S(1)}, u32[]{:S(2)}, u32[]{:S(2)}) collective-permute-start(bf16[256,128]{1,0:T(8,128)(2,1)S(1)} %get-tuple-element.12.near), channel_id=1, source_target_pairs={{0,512},{128,640},{256,768},{384,896},{512,0},{640,128},{768,256},... | collective-permute-start | bytes 196616 | tf_op jit(solution)/shard_map/ppermute | solution.py:183
  13.3 0.0 copy-start
  13.3 0.0 copy-start.1
  13.4 2.4 %shard_map.96 = (bf16[1024,128]{1,0:T(8,128)(2,1)}, f32[8,128]{1,0:T(8,128)S(1)}) custom-call(bf16[256,1024]{1,0:T(8,128)(2,1)} %grad_hbm.3, s32[256,1024]{1,0:T(8,128)} %mask_hbm.3, bf16[256,128]{1,0:T(8,128)(2,1)} %aggregated_hbm.1, f32[8,128]{1,0:T(8,128)S(1)} %get-tuple-element.13.before_ref), custom_call_target="tpu_custom_call" | custom-call | flops 20000000000 | bytes 1048576 | tf_op jit(solution)/shard_map/pallas_call | solution.py:208
  15.8 7.1 %all-to-all-start = ((bf16[8,128,128]{2,1,0:T(8,128)(2,1)}), bf16[8,128,128]{2,1,0:T(8,128)(2,1)S(1)}, u32[]{:S(2)}, u32[]{:S(2)}) async-start(bf16[8,128,128]{2,1,0:T(8,128)(2,1)} %bitcast.9), calls=%async_computation | async-start | bytes 524288 | tf_op jit(solution)/shard_map/all_to_all | solution.py:189
  23.6 0.0 collective-permute-done.four
  23.6 7.9 %collective-permute-start.3 = (bf16[512,128]{1,0:T(8,128)(2,1)S(1)}, bf16[512,128]{1,0:T(8,128)(2,1)S(1)}, u32[]{:S(2)}, u32[]{:S(2)}) collective-permute-start(bf16[512,128]{1,0:T(8,128)(2,1)S(1)} %shard_map.97.after_ref), channel_id=1, source_target_pairs={{0,384},{128,256},{256,128},{384,0},{512,896},{640,768},{768,640},... | collective-permute-start | bytes 393224 | tf_op jit(solution)/shard_map/ppermute | solution.py:183
  31.5 1.9 %collective-permute-start.2 = (bf16[512,128]{1,0:T(8,128)(2,1)S(1)}, bf16[512,128]{1,0:T(8,128)(2,1)S(1)}, u32[]{:S(2)}, u32[]{:S(2)}) collective-permute-start(bf16[512,128]{1,0:T(8,128)(2,1)S(1)} %shard_map.97.after_ref), channel_id=1, source_target_pairs={{0,256},{128,384},{256,0},{384,128},{512,768},{640,896},{768,512},... | collective-permute-start | bytes 393224 | tf_op jit(solution)/shard_map/ppermute | solution.py:183
  33.5 2.5 %collective-permute-start.1 = (bf16[512,128]{1,0:T(8,128)(2,1)S(1)}, bf16[512,128]{1,0:T(8,128)(2,1)S(1)}, u32[]{:S(2)}, u32[]{:S(2)}) collective-permute-start(bf16[512,128]{1,0:T(8,128)(2,1)S(1)} %shard_map.97.after_ref), channel_id=1, source_target_pairs={{0,128},{128,0},{256,384},{384,256},{512,640},{640,512},{768,896},... | collective-permute-start | bytes 393224 | tf_op jit(solution)/shard_map/ppermute | solution.py:183
  35.9 0.0 all-to-all-done.spread_ref
  36.0 3.4 %collective-permute-start.4 = (bf16[128,128]{1,0:T(8,128)(2,1)S(1)}, bf16[128,128]{1,0:T(8,128)(2,1)S(1)}, u32[]{:S(2)}, u32[]{:S(2)}) collective-permute-start(bf16[128,128]{1,0:T(8,128)(2,1)S(1)} %shard_map.99.own), channel_id=1, source_target_pairs={{0,128},{128,0},{256,384},{384,256},{512,640},{640,512},{768,896},... | collective-permute-start | bytes 98312 | tf_op jit(solution)/shard_map/ppermute | solution.py:183
  39.4 0.0 collective-permute-done.3.got_3
  39.4 1.8 %collective-permute-done.2.got_2 = bf16[512,128]{1,0:T(8,128)(2,1)S(1)} collective-permute-done((bf16[512,128]{1,0:T(8,128)(2,1)S(1)}, bf16[512,128]{1,0:T(8,128)(2,1)S(1)}, u32[]{:S(2)}, u32[]{:S(2)}) %collective-permute-start.2) | collective-permute-done | bytes 131104 | tf_op jit(solution)/shard_map/ppermute | solution.py:183
  41.2 1.7 %collective-permute-done.1.got_1 = bf16[512,128]{1,0:T(8,128)(2,1)S(1)} collective-permute-done((bf16[512,128]{1,0:T(8,128)(2,1)S(1)}, bf16[512,128]{1,0:T(8,128)(2,1)S(1)}, u32[]{:S(2)}, u32[]{:S(2)}) %collective-permute-start.1) | collective-permute-done | bytes 131104 | tf_op jit(solution)/shard_map/ppermute | solution.py:183
  42.9 3.9 %shard_map.98.sent_in = bf16[8,512,128]{2,1,0:T(8,128)(2,1)} custom-call(s32[1]{0:T(128)} %bitcast.7.live_ref, s32[160]{0:T(256)S(1)} %get-tuple-element.22.row_ref, s32[160]{0:T(256)S(1)} %get-tuple-element.23.col_ref, bf16[160,128,128]{2,1,0:T(8,128)(2,1)} %bitcast.12, bf16[256,128]{1,0:T(8,128)(2,1)S(1)} %get-tuple-element.12.near, ...), custom_call_target="tpu_custom_call" | custom-call | flops 20000000000 | bytes 5242880 | tf_op jit(solution)/shard_map/pallas_call | solution.py:250
  46.8 0.0 collective-permute-done.4.other
  46.8 7.1 %all-to-all-start.1 = ((bf16[8,512,128]{2,1,0:T(8,128)(2,1)}), bf16[8,512,128]{2,1,0:T(8,128)(2,1)S(1)}, u32[]{:S(2)}, u32[]{:S(2)}) async-start(bf16[8,512,128]{2,1,0:T(8,128)(2,1)} %get-tuple-element.16), calls=%async_computation.1 | async-start | bytes 2097152 | tf_op jit(solution)/shard_map/all_to_all | solution.py:189
  53.9 11.7 %collective-permute-start.6 = (bf16[128,128]{1,0:T(8,128)(2,1)S(1)}, bf16[128,128]{1,0:T(8,128)(2,1)S(1)}, u32[]{:S(2)}, u32[]{:S(2)}) collective-permute-start(bf16[128,128]{1,0:T(8,128)(2,1)S(1)} %get-tuple-element.21), channel_id=1, source_target_pairs={{0,8},{8,0},{16,24},{24,16},{32,40},{40,32},{48,56},{56,48},{64,72... | collective-permute-start | bytes 98312 | tf_op jit(solution)/shard_map/ppermute | solution.py:186
  65.6 2.8 %collective-permute-done.6 = bf16[128,128]{1,0:T(8,128)(2,1)S(1)} collective-permute-done((bf16[128,128]{1,0:T(8,128)(2,1)S(1)}, bf16[128,128]{1,0:T(8,128)(2,1)S(1)}, u32[]{:S(2)}, u32[]{:S(2)}) %collective-permute-start.6) | collective-permute-done | bytes 32800 | tf_op jit(solution)/shard_map/ppermute | solution.py:186
  68.4 1.9 %collective-permute-start.7 = (bf16[128,128]{1,0:T(8,128)(2,1)S(1)}, bf16[128,128]{1,0:T(8,128)(2,1)S(1)}, u32[]{:S(2)}, u32[]{:S(2)}) collective-permute-start(bf16[128,128]{1,0:T(8,128)(2,1)S(1)} %add_convert_fusion.1), channel_id=1, source_target_pairs={{0,256},{128,384},{256,0},{384,128},{512,768},{640,896},{768,512},... | collective-permute-start | bytes 98312 | tf_op jit(solution)/shard_map/ppermute | solution.py:183
  70.3 4.8 %collective-permute-done.7 = bf16[128,128]{1,0:T(8,128)(2,1)S(1)} collective-permute-done((bf16[128,128]{1,0:T(8,128)(2,1)S(1)}, bf16[128,128]{1,0:T(8,128)(2,1)S(1)}, u32[]{:S(2)}, u32[]{:S(2)}) %collective-permute-start.7) | collective-permute-done | bytes 32800 | tf_op jit(solution)/shard_map/ppermute | solution.py:183
  75.1 4.0 %collective-permute-start.8 = (bf16[128,128]{1,0:T(8,128)(2,1)S(1)}, bf16[128,128]{1,0:T(8,128)(2,1)S(1)}, u32[]{:S(2)}, u32[]{:S(2)}) collective-permute-start(bf16[128,128]{1,0:T(8,128)(2,1)S(1)} %add_convert_fusion.own), channel_id=1, source_target_pairs={{0,512},{128,640},{256,768},{384,896},{512,0},{640,128},{768,256},... | collective-permute-start | bytes 98312 | tf_op jit(solution)/shard_map/ppermute | solution.py:183
  79.1 1.3 %all-to-all-done.1.got_ref = bf16[8,512,128]{2,1,0:T(8,128)(2,1)S(1)} async-done(((bf16[8,512,128]{2,1,0:T(8,128)(2,1)}), bf16[8,512,128]{2,1,0:T(8,128)(2,1)S(1)}, u32[]{:S(2)}, u32[]{:S(2)}) %all-to-all-start.1) | async-done | bytes 1048608 | tf_op jit(solution)/shard_map/all_to_all | solution.py:189
  80.4 0.1 shard_map.101
  80.6 12.0 %collective-permute-start.5 = (bf16[256,128]{1,0:T(8,128)(2,1)S(1)}, bf16[256,128]{1,0:T(8,128)(2,1)S(1)}, u32[]{:S(2)}, u32[]{:S(2)}) collective-permute-start(bf16[256,128]{1,0:T(8,128)(2,1)S(1)} %get-tuple-element.18.after_ref), channel_id=1, source_target_pairs={{0,8},{8,0},{16,24},{24,16},{32,40},{40,32},{48,56},{56,48},{64,72... | collective-permute-start | bytes 196616 | tf_op jit(solution)/shard_map/ppermute | solution.py:186
  92.6 0.0 collective-permute-done.8.other
  92.6 0.7 shard_map.103
  93.4 6.3 %all-to-all-start.2 = ((bf16[8,128,128]{2,1,0:T(8,128)(2,1)}), bf16[8,128,128]{2,1,0:T(8,128)(2,1)S(1)}, u32[]{:S(2)}, u32[]{:S(2)}) async-start(bf16[8,128,128]{2,1,0:T(8,128)(2,1)} %shard_map.103), calls=%async_computation.2 | async-start | bytes 524288 | tf_op jit(solution)/shard_map/all_to_all | solution.py:189
  99.6 0.6 shard_map.102
  100.3 9.8 %all-to-all-done.2.shares_ref = bf16[8,128,128]{2,1,0:T(8,128)(2,1)S(1)} async-done(((bf16[8,128,128]{2,1,0:T(8,128)(2,1)}), bf16[8,128,128]{2,1,0:T(8,128)(2,1)S(1)}, u32[]{:S(2)}, u32[]{:S(2)}) %all-to-all-start.2) | async-done | bytes 262176 | tf_op jit(solution)/shard_map/all_to_all | solution.py:189
  110.1 0.8 shard_map.104
  (9 shorter events, 0.1 us)
Async XLA Ops:
  2.4 21.2 %collective-permute-start = (bf16[256,128]{1,0:T(8,128)(2,1)S(1)}, bf16[256,128]{1,0:T(8,128)(2,1)S(1)}, u32[]{:S(2)}, u32[]{:S(2)}) collective-permute-start(bf16[256,128]{1,0:T(8,128)(2,1)S(1)} %get-tuple-element.12.near), channel_id=1, source_target_pairs={{0,512},{128,640},{256,768},{384,896},{512,0},{640,128},{768,256},... | collective-permute-start | bytes 196616 | tf_op jit(solution)/shard_map/ppermute | solution.py:183
  13.3 10.2 %copy-start = (s32[1,1,160]{2,1,0:T(1,128)S(1)}, s32[1,1,160]{2,1,0:T(1,128)}, u32[]{:S(2)}) copy-start(s32[1,1,160]{2,1,0:T(1,128)} %param.13) | copy-start | bytes 1924
  13.3 10.2 %copy-start.1 = (s32[1,1,160]{2,1,0:T(1,128)S(1)}, s32[1,1,160]{2,1,0:T(1,128)}, u32[]{:S(2)}) copy-start(s32[1,1,160]{2,1,0:T(1,128)} %param.14) | copy-start | bytes 1924
  15.8 20.2 %all-to-all-start = ((bf16[8,128,128]{2,1,0:T(8,128)(2,1)}), bf16[8,128,128]{2,1,0:T(8,128)(2,1)S(1)}, u32[]{:S(2)}, u32[]{:S(2)}) async-start(bf16[8,128,128]{2,1,0:T(8,128)(2,1)} %bitcast.9), calls=%async_computation | async-start | bytes 524288 | tf_op jit(solution)/shard_map/all_to_all | solution.py:189
  23.6 15.8 %collective-permute-start.3 = (bf16[512,128]{1,0:T(8,128)(2,1)S(1)}, bf16[512,128]{1,0:T(8,128)(2,1)S(1)}, u32[]{:S(2)}, u32[]{:S(2)}) collective-permute-start(bf16[512,128]{1,0:T(8,128)(2,1)S(1)} %shard_map.97.after_ref), channel_id=1, source_target_pairs={{0,384},{128,256},{256,128},{384,0},{512,896},{640,768},{768,640},... | collective-permute-start | bytes 393224 | tf_op jit(solution)/shard_map/ppermute | solution.py:183
  31.5 9.7 %collective-permute-start.2 = (bf16[512,128]{1,0:T(8,128)(2,1)S(1)}, bf16[512,128]{1,0:T(8,128)(2,1)S(1)}, u32[]{:S(2)}, u32[]{:S(2)}) collective-permute-start(bf16[512,128]{1,0:T(8,128)(2,1)S(1)} %shard_map.97.after_ref), channel_id=1, source_target_pairs={{0,256},{128,384},{256,0},{384,128},{512,768},{640,896},{768,512},... | collective-permute-start | bytes 393224 | tf_op jit(solution)/shard_map/ppermute | solution.py:183
  33.5 9.4 %collective-permute-start.1 = (bf16[512,128]{1,0:T(8,128)(2,1)S(1)}, bf16[512,128]{1,0:T(8,128)(2,1)S(1)}, u32[]{:S(2)}, u32[]{:S(2)}) collective-permute-start(bf16[512,128]{1,0:T(8,128)(2,1)S(1)} %shard_map.97.after_ref), channel_id=1, source_target_pairs={{0,128},{128,0},{256,384},{384,256},{512,640},{640,512},{768,896},... | collective-permute-start | bytes 393224 | tf_op jit(solution)/shard_map/ppermute | solution.py:183
  36.0 10.8 %collective-permute-start.4 = (bf16[128,128]{1,0:T(8,128)(2,1)S(1)}, bf16[128,128]{1,0:T(8,128)(2,1)S(1)}, u32[]{:S(2)}, u32[]{:S(2)}) collective-permute-start(bf16[128,128]{1,0:T(8,128)(2,1)S(1)} %shard_map.99.own), channel_id=1, source_target_pairs={{0,128},{128,0},{256,384},{384,256},{512,640},{640,512},{768,896},... | collective-permute-start | bytes 98312 | tf_op jit(solution)/shard_map/ppermute | solution.py:183
  46.8 33.6 %all-to-all-start.1 = ((bf16[8,512,128]{2,1,0:T(8,128)(2,1)}), bf16[8,512,128]{2,1,0:T(8,128)(2,1)S(1)}, u32[]{:S(2)}, u32[]{:S(2)}) async-start(bf16[8,512,128]{2,1,0:T(8,128)(2,1)} %get-tuple-element.16), calls=%async_computation.1 | async-start | bytes 2097152 | tf_op jit(solution)/shard_map/all_to_all | solution.py:189
  53.9 14.5 %collective-permute-start.6 = (bf16[128,128]{1,0:T(8,128)(2,1)S(1)}, bf16[128,128]{1,0:T(8,128)(2,1)S(1)}, u32[]{:S(2)}, u32[]{:S(2)}) collective-permute-start(bf16[128,128]{1,0:T(8,128)(2,1)S(1)} %get-tuple-element.21), channel_id=1, source_target_pairs={{0,8},{8,0},{16,24},{24,16},{32,40},{40,32},{48,56},{56,48},{64,72... | collective-permute-start | bytes 98312 | tf_op jit(solution)/shard_map/ppermute | solution.py:186
  68.4 6.7 %collective-permute-start.7 = (bf16[128,128]{1,0:T(8,128)(2,1)S(1)}, bf16[128,128]{1,0:T(8,128)(2,1)S(1)}, u32[]{:S(2)}, u32[]{:S(2)}) collective-permute-start(bf16[128,128]{1,0:T(8,128)(2,1)S(1)} %add_convert_fusion.1), channel_id=1, source_target_pairs={{0,256},{128,384},{256,0},{384,128},{512,768},{640,896},{768,512},... | collective-permute-start | bytes 98312 | tf_op jit(solution)/shard_map/ppermute | solution.py:183
  75.1 17.5 %collective-permute-start.8 = (bf16[128,128]{1,0:T(8,128)(2,1)S(1)}, bf16[128,128]{1,0:T(8,128)(2,1)S(1)}, u32[]{:S(2)}, u32[]{:S(2)}) collective-permute-start(bf16[128,128]{1,0:T(8,128)(2,1)S(1)} %add_convert_fusion.own), channel_id=1, source_target_pairs={{0,512},{128,640},{256,768},{384,896},{512,0},{640,128},{768,256},... | collective-permute-start | bytes 98312 | tf_op jit(solution)/shard_map/ppermute | solution.py:183
  80.6 19.0 %collective-permute-start.5 = (bf16[256,128]{1,0:T(8,128)(2,1)S(1)}, bf16[256,128]{1,0:T(8,128)(2,1)S(1)}, u32[]{:S(2)}, u32[]{:S(2)}) collective-permute-start(bf16[256,128]{1,0:T(8,128)(2,1)S(1)} %get-tuple-element.18.after_ref), channel_id=1, source_target_pairs={{0,8},{8,0},{16,24},{24,16},{32,40},{40,32},{48,56},{56,48},{64,72... | collective-permute-start | bytes 196616 | tf_op jit(solution)/shard_map/ppermute | solution.py:186
  93.4 16.7 %all-to-all-start.2 = ((bf16[8,128,128]{2,1,0:T(8,128)(2,1)}), bf16[8,128,128]{2,1,0:T(8,128)(2,1)S(1)}, u32[]{:S(2)}, u32[]{:S(2)}) async-start(bf16[8,128,128]{2,1,0:T(8,128)(2,1)} %shard_map.103), calls=%async_computation.2 | async-start | bytes 524288 | tf_op jit(solution)/shard_map/all_to_all | solution.py:189

commit v11 on v9

--- a/solution.py
+++ b/solution.py
@@ -129,7 +129,7 @@
         result.wait()
 
 
-def halves_kernel(half_ref, got_ref, keep_ref, send_ref, total):
+def halves_kernel(half_ref, after_ref, got_ref, keep_ref, send_ref, total):
     owners, height = got_ref.shape[0], got_ref.shape[1]
     for k in range(height // LANES):
         rows = slice(k * LANES, (k + 1) * LANES)
@@ -143,19 +143,20 @@
     send_ref[...] = total[pl.ds(pl.multiple_of((1 - half) * own, own), own), :].astype(jnp.bfloat16)
 
 
-def share_kernel(after_ref, own, other, out_ref):
+def share_kernel(own, other, out_ref, after_ref):
+    after_ref[...] = jnp.zeros_like(after_ref)
     total = own[...].astype(jnp.float32) + other[...].astype(jnp.float32)
     total = total.astype(jnp.bfloat16)
     for c in range(out_ref.shape[0]):
         out_ref[c] = total
 
 
-def features_kernel(keep_ref, got_ref, features_ref, after_ref):
+def features_kernel(before_ref, keep_ref, got_ref, features_ref):
+    features_ref[...] = (keep_ref[...] + got_ref[...].astype(jnp.float32)).astype(jnp.bfloat16)
+
+
+def spread_kernel(shares_ref, weight_ref, after_ref):
     after_ref[...] = jnp.zeros_like(after_ref)
-    features_ref[...] = (keep_ref[...] + got_ref[...].astype(jnp.float32)).astype(jnp.bfloat16)
-
-
-def spread_kernel(after_ref, shares_ref, weight_ref):
     owners, rows = shares_ref.shape[0], shares_ref.shape[1]
     feats = weight_ref.shape[0]
     for g in range(owners * rows // feats):
@@ -277,42 +278,42 @@
         share = (share.astype(f32) + swap(share, mask).astype(f32)).astype(bf)
     far = swap_pair(share)
 
+    whole, ready = pl.pallas_call(
+        share_kernel,
+        out_shape=(shape((n_y, extra, LANES), bf), token),
+        in_specs=[VMEM] * 2,
+        out_specs=(VMEM, VMEM),
+        compiler_params=params(16),
+        cost_estimate=cost(n_y * extra * LANES, n_y * extra * LANES * 2),
+    )(share, far)
+    shares = line_all_to_all(whole)
     half = (lax.axis_index("col") & (PAIR - 1)).astype(jnp.int32).reshape(1)
     keep, send = pl.pallas_call(
         halves_kernel,
         out_shape=(shape((nodes, feats), f32), shape((nodes, feats), bf)),
-        in_specs=[SMEM, VMEM],
+        in_specs=[SMEM, HBM, VMEM],
         out_specs=(VMEM, VMEM),
         scratch_shapes=[pltpu.VMEM((PAIR * nodes, feats), f32)],
         compiler_params=params(16),
         cost_estimate=cost(nodes * feats * n_col, nodes * feats * n_col * 2),
-    )(half, got)
+    )(half, ready, got)
     other = swap_pair(send)
-    whole = pl.pallas_call(
-        share_kernel,
-        out_shape=shape((n_y, extra, LANES), bf),
+    grad_weight, after = pl.pallas_call(
+        spread_kernel,
+        out_shape=(shape((feats, width), f32), token),
+        in_specs=[VMEM],
+        out_specs=(VMEM, VMEM),
+        compiler_params=params(16),
+        cost_estimate=cost(feats * width, feats * width * 6),
+    )(shares)
+    features = pl.pallas_call(
+        features_kernel,
+        out_shape=shape((nodes, feats), bf),
         in_specs=[HBM] + [VMEM] * 2,
         out_specs=VMEM,
         compiler_params=params(16),
-        cost_estimate=cost(2 * 10**10, n_y * extra * LANES * 2),
-    )(send, share, far)
-    shares = line_all_to_all(whole)
-    features, after = pl.pallas_call(
-        features_kernel,
-        out_shape=(shape((nodes, feats), bf), token),
-        in_specs=[VMEM] * 2,
-        out_specs=(VMEM, VMEM),
-        compiler_params=params(16),
-        cost_estimate=cost(2 * 10**10, nodes * feats * 4),
-    )(keep, other)
-    grad_weight = pl.pallas_call(
-        spread_kernel,
-        out_shape=shape((feats, width), f32),
-        in_specs=[HBM, VMEM],
-        out_specs=VMEM,
-        compiler_params=params(16),
-        cost_estimate=cost(feats * width, feats * width * 6),
-    )(after, shares)
+        cost_estimate=cost(nodes * feats, nodes * feats * 4),
+    )(after, keep, other)
     return features, grad_weight
 
 

time: 110 us -> 112 us (1.018); the launches traced: 109 us -> 110 us
  waiting for transfers between devices: 24.4 us -> 20.2 us
  starting transfers between devices: 72.1 us -> 76.2 us
    all_to_all x3, waiting for transfers between devices: 7.26 us -> 0.01 us  [line_all_to_all(): lax.all_to_all(value, 'col', 0, 0, axis_index_groups=lines, tiled=True)]
    all_to_all x3, starting transfers between devices: 17.6 us -> 21.4 us  [line_all_to_all(): lax.all_to_all(value, 'col', 0, 0, axis_index_groups=lines, tiled=True)]
    ppermute x2, starting transfers between devices: 22.7 us -> 24.4 us  [swap_pair(): return lax.ppermute(value, 'col', [(i, i ^ 1) for i in range(n_col)])]
    ppermute x2, waiting for transfers between devices: 2.51 us -> 4.1 us  [swap_pair(): return lax.ppermute(value, 'col', [(i, i ^ 1) for i in range(n_col)])]
    ppermute x7, starting transfers between devices: 31.9 us -> 30.4 us  [swap(): return lax.ppermute(value, 'row', [(i, i ^ mask) for i in range(n_row)])]
    ppermute x7, waiting for transfers between devices: 14.6 us -> 16.1 us  [swap(): return lax.ppermute(value, 'row', [(i, i ^ mask) for i in range(n_row)])]
  transfers between devices with their start and end apart: 12 -> 12, of which waited for: 6 -> 6; matrix products, arithmetic and copies ran while one was open for 0% -> 0% of each run, Pallas kernels for 8% -> 9%
where the time goes in v11:
time: 112 us; the launch traced here: 110 us
  starting transfers between devices  76.2 us (68%)
  waiting for transfers between devices  20.2 us (18%)
  Pallas kernels  11.9 us (11%)
  between operations  1.49 us (1%)
    ppermute x7, starting transfers between devices, swap(): return lax.ppermute(value, 'row', [(i, i ^ mask) for i in range(n_row)])  30.4 us
    ppermute x2, starting transfers between devices, swap_pair(): return lax.ppermute(value, 'col', [(i, i ^ 1) for i in range(n_col)])  24.4 us
    all_to_all x3, starting transfers between devices, line_all_to_all(): lax.all_to_all(value, 'col', 0, 0, axis_index_groups=lines, tiled=True)  21.4 us
    ppermute x7, waiting for transfers between devices, swap(): return lax.ppermute(value, 'row', [(i, i ^ mask) for i in range(n_row)])  16.1 us
    pallas_call x1, Pallas kernels, shards(): pl.pallas_call(tiles_kernel, out_shape=shape((n_y, PAIR * nodes, feats),...  5.32 us
    ppermute x2, waiting for transfers between devices, swap_pair(): return lax.ppermute(value, 'col', [(i, i ^ 1) for i in range(n_col)])  4.1 us
    pallas_call x1, Pallas kernels, shards(): pl.pallas_call(weight_kernel, out_shape=(shape((width // LANES * feats, L...  2.43 us
  transfers between devices with their start and end apart: 12, of which 6 were waited for; matrix products, arithmetic and copies ran while one was open for 0% of the time, Pallas kernels for 9%

profile of v11, /device:TPU:6, one launch (start us, length us, event | category | flops | bytes accessed | tf_op | source)
XLA Modules:
  0.0 109.9 jit_solution(612700338756827865)
XLA Ops:
  0.6 1.8 %shard_map.95 = (bf16[256,128]{1,0:T(8,128)(2,1)S(1)}, f32[8,128]{1,0:T(8,128)S(1)}) custom-call(bf16[256,1024]{1,0:T(8,128)(2,1)} %grad_hbm.3, s32[256,1024]{1,0:T(8,128)} %mask_hbm.3, bf16[128,1024]{1,0:T(8,128)(2,1)} %weight_hbm.1), custom_call_target="tpu_custom_call" | custom-call | flops 67108864 | bytes 2097152 | tf_op jit(solution)/shard_map/pallas_call | solution.py:192
  2.4 10.9 %collective-permute-start = (bf16[256,128]{1,0:T(8,128)(2,1)S(1)}, bf16[256,128]{1,0:T(8,128)(2,1)S(1)}, u32[]{:S(2)}, u32[]{:S(2)}) collective-permute-start(bf16[256,128]{1,0:T(8,128)(2,1)S(1)} %get-tuple-element.14.near), channel_id=1, source_target_pairs={{0,512},{128,640},{256,768},{384,896},{512,0},{640,128},{768,256},... | collective-permute-start | bytes 196616 | tf_op jit(solution)/shard_map/ppermute | solution.py:184
  13.3 0.0 copy-start
  13.3 0.0 copy-start.1
  13.4 2.4 %shard_map.96 = (bf16[1024,128]{1,0:T(8,128)(2,1)}, f32[8,128]{1,0:T(8,128)S(1)}) custom-call(bf16[256,1024]{1,0:T(8,128)(2,1)} %grad_hbm.3, s32[256,1024]{1,0:T(8,128)} %mask_hbm.3, bf16[256,128]{1,0:T(8,128)(2,1)} %aggregated_hbm.1, f32[8,128]{1,0:T(8,128)S(1)} %get-tuple-element.15.before_ref), custom_call_target="tpu_custom_call" | custom-call | flops 20000000000 | bytes 1048576 | tf_op jit(solution)/shard_map/pallas_call | solution.py:209
  15.8 7.1 %all-to-all-start = ((bf16[8,128,128]{2,1,0:T(8,128)(2,1)}), bf16[8,128,128]{2,1,0:T(8,128)(2,1)S(1)}, u32[]{:S(2)}, u32[]{:S(2)}) async-start(bf16[8,128,128]{2,1,0:T(8,128)(2,1)} %bitcast.9), calls=%async_computation | async-start | bytes 524288 | tf_op jit(solution)/shard_map/all_to_all | solution.py:190
  23.6 0.0 collective-permute-done.four
  23.6 7.9 %collective-permute-start.3 = (bf16[512,128]{1,0:T(8,128)(2,1)S(1)}, bf16[512,128]{1,0:T(8,128)(2,1)S(1)}, u32[]{:S(2)}, u32[]{:S(2)}) collective-permute-start(bf16[512,128]{1,0:T(8,128)(2,1)S(1)} %shard_map.97.after_ref), channel_id=1, source_target_pairs={{0,384},{128,256},{256,128},{384,0},{512,896},{640,768},{768,640},... | collective-permute-start | bytes 393224 | tf_op jit(solution)/shard_map/ppermute | solution.py:184
  31.5 1.9 %collective-permute-start.2 = (bf16[512,128]{1,0:T(8,128)(2,1)S(1)}, bf16[512,128]{1,0:T(8,128)(2,1)S(1)}, u32[]{:S(2)}, u32[]{:S(2)}) collective-permute-start(bf16[512,128]{1,0:T(8,128)(2,1)S(1)} %shard_map.97.after_ref), channel_id=1, source_target_pairs={{0,256},{128,384},{256,0},{384,128},{512,768},{640,896},{768,512},... | collective-permute-start | bytes 393224 | tf_op jit(solution)/shard_map/ppermute | solution.py:184
  33.5 2.5 %collective-permute-start.1 = (bf16[512,128]{1,0:T(8,128)(2,1)S(1)}, bf16[512,128]{1,0:T(8,128)(2,1)S(1)}, u32[]{:S(2)}, u32[]{:S(2)}) collective-permute-start(bf16[512,128]{1,0:T(8,128)(2,1)S(1)} %shard_map.97.after_ref), channel_id=1, source_target_pairs={{0,128},{128,0},{256,384},{384,256},{512,640},{640,512},{768,896},... | collective-permute-start | bytes 393224 | tf_op jit(solution)/shard_map/ppermute | solution.py:184
  35.9 0.0 all-to-all-done.spread_ref
  36.0 3.4 %collective-permute-start.4 = (bf16[128,128]{1,0:T(8,128)(2,1)S(1)}, bf16[128,128]{1,0:T(8,128)(2,1)S(1)}, u32[]{:S(2)}, u32[]{:S(2)}) collective-permute-start(bf16[128,128]{1,0:T(8,128)(2,1)S(1)} %shard_map.99.own), channel_id=1, source_target_pairs={{0,128},{128,0},{256,384},{384,256},{512,640},{640,512},{768,896},... | collective-permute-start | bytes 98312 | tf_op jit(solution)/shard_map/ppermute | solution.py:184
  39.4 0.0 collective-permute-done.3.got_3
  39.4 1.8 %collective-permute-done.2.got_2 = bf16[512,128]{1,0:T(8,128)(2,1)S(1)} collective-permute-done((bf16[512,128]{1,0:T(8,128)(2,1)S(1)}, bf16[512,128]{1,0:T(8,128)(2,1)S(1)}, u32[]{:S(2)}, u32[]{:S(2)}) %collective-permute-start.2) | collective-permute-done | bytes 131104 | tf_op jit(solution)/shard_map/ppermute | solution.py:184
  41.2 1.7 %collective-permute-done.1.got_1 = bf16[512,128]{1,0:T(8,128)(2,1)S(1)} collective-permute-done((bf16[512,128]{1,0:T(8,128)(2,1)S(1)}, bf16[512,128]{1,0:T(8,128)(2,1)S(1)}, u32[]{:S(2)}, u32[]{:S(2)}) %collective-permute-start.1) | collective-permute-done | bytes 131104 | tf_op jit(solution)/shard_map/ppermute | solution.py:184
  42.9 5.3 %shard_map.98.sent_in = bf16[8,512,128]{2,1,0:T(8,128)(2,1)} custom-call(s32[1]{0:T(128)} %bitcast.7.live_ref, s32[160]{0:T(256)S(1)} %get-tuple-element.26.row_ref, s32[160]{0:T(256)S(1)} %get-tuple-element.27.col_ref, bf16[160,128,128]{2,1,0:T(8,128)(2,1)} %bitcast.12, bf16[256,128]{1,0:T(8,128)(2,1)S(1)} %get-tuple-element.14.near, ...), custom_call_target="tpu_custom_call" | custom-call | flops 20000000000 | bytes 5242880 | tf_op jit(solution)/shard_map/pallas_call | solution.py:251
  48.2 7.1 %all-to-all-start.2 = ((bf16[8,512,128]{2,1,0:T(8,128)(2,1)}), bf16[8,512,128]{2,1,0:T(8,128)(2,1)S(1)}, u32[]{:S(2)}, u32[]{:S(2)}) async-start(bf16[8,512,128]{2,1,0:T(8,128)(2,1)} %get-tuple-element.22), calls=%async_computation.2 | async-start | bytes 2097152 | tf_op jit(solution)/shard_map/all_to_all | solution.py:190
  55.3 1.9 %collective-permute-start.5 = (bf16[128,128]{1,0:T(8,128)(2,1)S(1)}, bf16[128,128]{1,0:T(8,128)(2,1)S(1)}, u32[]{:S(2)}, u32[]{:S(2)}) collective-permute-start(bf16[128,128]{1,0:T(8,128)(2,1)S(1)} %get-tuple-element.18), channel_id=1, source_target_pairs={{0,256},{128,384},{256,0},{384,128},{512,768},{640,896},{768,512},... | collective-permute-start | bytes 98312 | tf_op jit(solution)/shard_map/ppermute | solution.py:184
  57.2 4.8 %collective-permute-done.5 = bf16[128,128]{1,0:T(8,128)(2,1)S(1)} collective-permute-done((bf16[128,128]{1,0:T(8,128)(2,1)S(1)}, bf16[128,128]{1,0:T(8,128)(2,1)S(1)}, u32[]{:S(2)}, u32[]{:S(2)}) %collective-permute-start.5) | collective-permute-done | bytes 32800 | tf_op jit(solution)/shard_map/ppermute | solution.py:184
  62.0 1.9 %collective-permute-start.6 = (bf16[128,128]{1,0:T(8,128)(2,1)S(1)}, bf16[128,128]{1,0:T(8,128)(2,1)S(1)}, u32[]{:S(2)}, u32[]{:S(2)}) collective-permute-start(bf16[128,128]{1,0:T(8,128)(2,1)S(1)} %add_convert_fusion.1), channel_id=1, source_target_pairs={{0,512},{128,640},{256,768},{384,896},{512,0},{640,128},{768,256},... | collective-permute-start | bytes 98312 | tf_op jit(solution)/shard_map/ppermute | solution.py:184
  63.9 7.8 %collective-permute-done.6 = bf16[128,128]{1,0:T(8,128)(2,1)S(1)} collective-permute-done((bf16[128,128]{1,0:T(8,128)(2,1)S(1)}, bf16[128,128]{1,0:T(8,128)(2,1)S(1)}, u32[]{:S(2)}, u32[]{:S(2)}) %collective-permute-start.6) | collective-permute-done | bytes 32800 | tf_op jit(solution)/shard_map/ppermute | solution.py:184
  71.7 12.2 %collective-permute-start.7 = (bf16[128,128]{1,0:T(8,128)(2,1)S(1)}, bf16[128,128]{1,0:T(8,128)(2,1)S(1)}, u32[]{:S(2)}, u32[]{:S(2)}) collective-permute-start(bf16[128,128]{1,0:T(8,128)(2,1)S(1)} %add_convert_fusion.own), channel_id=1, source_target_pairs={{0,8},{8,0},{16,24},{24,16},{32,40},{40,32},{48,56},{56,48},{64,72... | collective-permute-start | bytes 98312 | tf_op jit(solution)/shard_map/ppermute | solution.py:187
  84.0 2.3 %collective-permute-done.7.other = bf16[128,128]{1,0:T(8,128)(2,1)S(1)} collective-permute-done((bf16[128,128]{1,0:T(8,128)(2,1)S(1)}, bf16[128,128]{1,0:T(8,128)(2,1)S(1)}, u32[]{:S(2)}, u32[]{:S(2)}) %collective-permute-start.7) | collective-permute-done | bytes 32800 | tf_op jit(solution)/shard_map/ppermute | solution.py:187
  86.3 0.7 shard_map.101
  87.0 0.0 all-to-all-done.2.got_ref
  87.0 7.2 %all-to-all-start.1 = ((bf16[8,128,128]{2,1,0:T(8,128)(2,1)}), bf16[8,128,128]{2,1,0:T(8,128)(2,1)S(1)}, u32[]{:S(2)}, u32[]{:S(2)}) async-start(bf16[8,128,128]{2,1,0:T(8,128)(2,1)} %get-tuple-element.19), calls=%async_computation.1 | async-start | bytes 524288 | tf_op jit(solution)/shard_map/all_to_all | solution.py:190
  94.2 0.1 shard_map.103
  94.4 12.2 %collective-permute-start.8 = (bf16[256,128]{1,0:T(8,128)(2,1)S(1)}, bf16[256,128]{1,0:T(8,128)(2,1)S(1)}, u32[]{:S(2)}, u32[]{:S(2)}) collective-permute-start(bf16[256,128]{1,0:T(8,128)(2,1)S(1)} %get-tuple-element.24), channel_id=1, source_target_pairs={{0,8},{8,0},{16,24},{24,16},{32,40},{40,32},{48,56},{56,48},{64,72... | collective-permute-start | bytes 196616 | tf_op jit(solution)/shard_map/ppermute | solution.py:187
  106.6 0.0 all-to-all-done.1.shares_ref
  106.6 0.8 shard_map.102
  107.4 1.8 %collective-permute-done.8.got_ref = bf16[256,128]{1,0:T(8,128)(2,1)S(1)} collective-permute-done((bf16[256,128]{1,0:T(8,128)(2,1)S(1)}, bf16[256,128]{1,0:T(8,128)(2,1)S(1)}, u32[]{:S(2)}, u32[]{:S(2)}) %collective-permute-start.8) | collective-permute-done | bytes 65568 | tf_op jit(solution)/shard_map/ppermute | solution.py:187
  109.2 0.6 shard_map.104
  (9 shorter events, 0.1 us)
Async XLA Ops:
  2.4 21.2 %collective-permute-start = (bf16[256,128]{1,0:T(8,128)(2,1)S(1)}, bf16[256,128]{1,0:T(8,128)(2,1)S(1)}, u32[]{:S(2)}, u32[]{:S(2)}) collective-permute-start(bf16[256,128]{1,0:T(8,128)(2,1)S(1)} %get-tuple-element.14.near), channel_id=1, source_target_pairs={{0,512},{128,640},{256,768},{384,896},{512,0},{640,128},{768,256},... | collective-permute-start | bytes 196616 | tf_op jit(solution)/shard_map/ppermute | solution.py:184
  13.3 10.2 %copy-start = (s32[1,1,160]{2,1,0:T(1,128)S(1)}, s32[1,1,160]{2,1,0:T(1,128)}, u32[]{:S(2)}) copy-start(s32[1,1,160]{2,1,0:T(1,128)} %param.13) | copy-start | bytes 1924
  13.3 10.2 %copy-start.1 = (s32[1,1,160]{2,1,0:T(1,128)S(1)}, s32[1,1,160]{2,1,0:T(1,128)}, u32[]{:S(2)}) copy-start(s32[1,1,160]{2,1,0:T(1,128)} %param.14) | copy-start | bytes 1924
  15.8 20.2 %all-to-all-start = ((bf16[8,128,128]{2,1,0:T(8,128)(2,1)}), bf16[8,128,128]{2,1,0:T(8,128)(2,1)S(1)}, u32[]{:S(2)}, u32[]{:S(2)}) async-start(bf16[8,128,128]{2,1,0:T(8,128)(2,1)} %bitcast.9), calls=%async_computation | async-start | bytes 524288 | tf_op jit(solution)/shard_map/all_to_all | solution.py:190
  23.6 15.8 %collective-permute-start.3 = (bf16[512,128]{1,0:T(8,128)(2,1)S(1)}, bf16[512,128]{1,0:T(8,128)(2,1)S(1)}, u32[]{:S(2)}, u32[]{:S(2)}) collective-permute-start(bf16[512,128]{1,0:T(8,128)(2,1)S(1)} %shard_map.97.after_ref), channel_id=1, source_target_pairs={{0,384},{128,256},{256,128},{384,0},{512,896},{640,768},{768,640},... | collective-permute-start | bytes 393224 | tf_op jit(solution)/shard_map/ppermute | solution.py:184
  31.5 9.7 %collective-permute-start.2 = (bf16[512,128]{1,0:T(8,128)(2,1)S(1)}, bf16[512,128]{1,0:T(8,128)(2,1)S(1)}, u32[]{:S(2)}, u32[]{:S(2)}) collective-permute-start(bf16[512,128]{1,0:T(8,128)(2,1)S(1)} %shard_map.97.after_ref), channel_id=1, source_target_pairs={{0,256},{128,384},{256,0},{384,128},{512,768},{640,896},{768,512},... | collective-permute-start | bytes 393224 | tf_op jit(solution)/shard_map/ppermute | solution.py:184
  33.5 9.4 %collective-permute-start.1 = (bf16[512,128]{1,0:T(8,128)(2,1)S(1)}, bf16[512,128]{1,0:T(8,128)(2,1)S(1)}, u32[]{:S(2)}, u32[]{:S(2)}) collective-permute-start(bf16[512,128]{1,0:T(8,128)(2,1)S(1)} %shard_map.97.after_ref), channel_id=1, source_target_pairs={{0,128},{128,0},{256,384},{384,256},{512,640},{640,512},{768,896},... | collective-permute-start | bytes 393224 | tf_op jit(solution)/shard_map/ppermute | solution.py:184
  36.0 12.2 %collective-permute-start.4 = (bf16[128,128]{1,0:T(8,128)(2,1)S(1)}, bf16[128,128]{1,0:T(8,128)(2,1)S(1)}, u32[]{:S(2)}, u32[]{:S(2)}) collective-permute-start(bf16[128,128]{1,0:T(8,128)(2,1)S(1)} %shard_map.99.own), channel_id=1, source_target_pairs={{0,128},{128,0},{256,384},{384,256},{512,640},{640,512},{768,896},... | collective-permute-start | bytes 98312 | tf_op jit(solution)/shard_map/ppermute | solution.py:184
  48.2 38.8 %all-to-all-start.2 = ((bf16[8,512,128]{2,1,0:T(8,128)(2,1)}), bf16[8,512,128]{2,1,0:T(8,128)(2,1)S(1)}, u32[]{:S(2)}, u32[]{:S(2)}) async-start(bf16[8,512,128]{2,1,0:T(8,128)(2,1)} %get-tuple-element.22), calls=%async_computation.2 | async-start | bytes 2097152 | tf_op jit(solution)/shard_map/all_to_all | solution.py:190
  55.3 6.7 %collective-permute-start.5 = (bf16[128,128]{1,0:T(8,128)(2,1)S(1)}, bf16[128,128]{1,0:T(8,128)(2,1)S(1)}, u32[]{:S(2)}, u32[]{:S(2)}) collective-permute-start(bf16[128,128]{1,0:T(8,128)(2,1)S(1)} %get-tuple-element.18), channel_id=1, source_target_pairs={{0,256},{128,384},{256,0},{384,128},{512,768},{640,896},{768,512},... | collective-permute-start | bytes 98312 | tf_op jit(solution)/shard_map/ppermute | solution.py:184
  62.0 9.7 %collective-permute-start.6 = (bf16[128,128]{1,0:T(8,128)(2,1)S(1)}, bf16[128,128]{1,0:T(8,128)(2,1)S(1)}, u32[]{:S(2)}, u32[]{:S(2)}) collective-permute-start(bf16[128,128]{1,0:T(8,128)(2,1)S(1)} %add_convert_fusion.1), channel_id=1, source_target_pairs={{0,512},{128,640},{256,768},{384,896},{512,0},{640,128},{768,256},... | collective-permute-start | bytes 98312 | tf_op jit(solution)/shard_map/ppermute | solution.py:184
  71.7 14.5 %collective-permute-start.7 = (bf16[128,128]{1,0:T(8,128)(2,1)S(1)}, bf16[128,128]{1,0:T(8,128)(2,1)S(1)}, u32[]{:S(2)}, u32[]{:S(2)}) collective-permute-start(bf16[128,128]{1,0:T(8,128)(2,1)S(1)} %add_convert_fusion.own), channel_id=1, source_target_pairs={{0,8},{8,0},{16,24},{24,16},{32,40},{40,32},{48,56},{56,48},{64,72... | collective-permute-start | bytes 98312 | tf_op jit(solution)/shard_map/ppermute | solution.py:187
  87.0 19.6 %all-to-all-start.1 = ((bf16[8,128,128]{2,1,0:T(8,128)(2,1)}), bf16[8,128,128]{2,1,0:T(8,128)(2,1)S(1)}, u32[]{:S(2)}, u32[]{:S(2)}) async-start(bf16[8,128,128]{2,1,0:T(8,128)(2,1)} %get-tuple-element.19), calls=%async_computation.1 | async-start | bytes 524288 | tf_op jit(solution)/shard_map/all_to_all | solution.py:190
  94.4 14.9 %collective-permute-start.8 = (bf16[256,128]{1,0:T(8,128)(2,1)S(1)}, bf16[256,128]{1,0:T(8,128)(2,1)S(1)}, u32[]{:S(2)}, u32[]{:S(2)}) collective-permute-start(bf16[256,128]{1,0:T(8,128)(2,1)S(1)} %get-tuple-element.24), channel_id=1, source_target_pairs={{0,8},{8,0},{16,24},{24,16},{32,40},{40,32},{48,56},{56,48},{64,72... | collective-permute-start | bytes 196616 | tf_op jit(solution)/shard_map/ppermute | solution.py:187

commit v12 on v11

--- a/solution.py
+++ b/solution.py
@@ -68,11 +68,20 @@
     packed_ref[nodes : 2 * nodes, :] = four[...]
 
 
-def sum_kernel(after_ref, spread_ref, out_ref):
+def sum_kernel(spread_ref, packed_in, packed_ref):
     acc = spread_ref[0].astype(jnp.float32)
     for c in range(1, spread_ref.shape[0]):
         acc = acc + spread_ref[c].astype(jnp.float32)
-    out_ref[...] = acc.astype(jnp.bfloat16)
+    rows = packed_in.shape[0]
+    packed_ref[0:rows, :] = packed_in[...]
+    packed_ref[rows:, :] = acc.astype(jnp.bfloat16)
+
+
+def panel_part_kernel(near, four, got_2, got_3, out_ref):
+    at = 0
+    for part in (near, four, got_2, got_3):
+        out_ref[at : at + part.shape[0], :] = part[...]
+        at += part.shape[0]
 
 
 def pair_kernel(sent_in, own, other, sent_out, out_ref):
@@ -81,7 +90,7 @@
 
 
 def tiles_kernel(
-    live_ref, row_ref, col_ref, tiles_hbm, near, four, got_1, got_2, got_3, out_hbm,
+    live_ref, row_ref, col_ref, tiles_hbm, parts, got_1, out_hbm,
     tiles, panel, total, done, arrived, written,
 ):
     size = tiles.shape[1]
@@ -95,8 +104,8 @@
         pl.when(g < groups)(fetch(g).start)
     total[...] = jnp.zeros_like(total)
     place = 0
-    for part in (near, four, got_1, got_2, got_3):
-        for k in range(part.shape[0] // size):
+    for part, count in ((parts, parts.shape[0]), (got_1, parts.shape[0] // 3)):
+        for k in range(count // size):
             panel[place] = part[k * size : (k + 1) * size, :]
             place += 1
 
@@ -230,28 +239,40 @@
         compiler_params=params(16),
         cost_estimate=cost(2 * 10**10, nodes * feats * 8),
     )(ready, near, four)
-    got_1, got_2, got_3 = swap(packed, 1), swap(packed, 2), swap(packed, 3)
-
-    share = pl.pallas_call(
+    got_2, got_3 = swap(packed, 2), swap(packed, 3)
+    loaded = pl.pallas_call(
         sum_kernel,
-        out_shape=shape((extra, LANES), bf),
-        in_specs=[HBM, VMEM],
+        out_shape=shape((2 * nodes + extra, LANES), bf),
+        in_specs=[VMEM] * 2,
         out_specs=VMEM,
         compiler_params=params(16),
         cost_estimate=cost(2 * 10**10, n_y * extra * LANES * 2),
-    )(packed, spread)
-    row_1 = swap(share, 1)
+    )(spread, packed)
+    got_1 = swap(loaded, 1)
+    parts = pl.pallas_call(
+        panel_part_kernel,
+        out_shape=shape((6 * nodes, feats), bf),
+        in_specs=[VMEM] * 4,
+        out_specs=VMEM,
+        compiler_params=params(16),
+        cost_estimate=cost(2 * 10**10, 12 * nodes * feats * 2),
+    )(near, four, got_2, got_3)
+    share = loaded[2 * nodes :].astype(f32) + got_1[2 * nodes :].astype(f32)
+    share = share.astype(bf)
+    row_2 = swap(share, 2)
 
     live = tile_count[0, 0]
     away = (tile_col[0, 0] * size // nodes) ^ lax.axis_index("row")
-    chunk = (away & 3) * 2 + (away >> 2)
+    low = away & 3
+    slot = jnp.where(low == 0, 0, jnp.where(low == 1, 3, low - 1))
+    chunk = slot * 2 + (away >> 2)
     col_at = chunk * per_owner + tile_col[0, 0] % per_owner
     row_at = jnp.where(jnp.arange(slots, dtype=jnp.int32) < live, tile_row[0, 0], block_tiles)
 
     sent = pl.pallas_call(
         tiles_kernel,
         out_shape=shape((n_y, PAIR * nodes, feats), bf),
-        in_specs=[SMEM] * 3 + [HBM] + [VMEM] * 5,
+        in_specs=[SMEM] * 3 + [HBM] + [VMEM] * 2,
         out_specs=HBM,
         scratch_shapes=[
             pltpu.VMEM((slots, size, size), bf),
@@ -263,7 +284,7 @@
         ],
         compiler_params=params(50),
         cost_estimate=cost(2 * 10**10, slots * size * size * 2),
-    )(live.reshape(1), row_at, col_at, tile_data, near, four, got_1, got_2, got_3)
+    )(live.reshape(1), row_at, col_at, tile_data, parts, got_1)
     sent, share = pl.pallas_call(
         pair_kernel,
         out_shape=(shape(sent.shape, bf), shape((extra, LANES), bf)),
@@ -272,10 +293,9 @@
         input_output_aliases={0: 0},
         compiler_params=params(16),
         cost_estimate=cost(4 * extra * LANES, 4 * extra * LANES * 2),
-    )(sent, share, row_1)
+    )(sent, share, row_2)
     got = line_all_to_all(sent)
-    for mask in (2, 4):
-        share = (share.astype(f32) + swap(share, mask).astype(f32)).astype(bf)
+    share = (share.astype(f32) + swap(share, 4).astype(f32)).astype(bf)
     far = swap_pair(share)
 
     whole, ready = pl.pallas_call(

time: 112 us -> 109 us (0.973)
  the two profiles are of different devices: /device:TPU:6 before, /device:TPU:72 now
where the time goes in v12:
time: 109 us; the launch traced here: 108 us
  starting transfers between devices  70.2 us (64%)
  waiting for transfers between devices  24.7 us (23%)
  Pallas kernels  12 us (11%)
  between operations  1.46 us (1%)
    ppermute x6, starting transfers between devices, swap(): return lax.ppermute(value, 'row', [(i, i ^ mask) for i in range(n_row)])  29.4 us
    all_to_all x3, starting transfers between devices, line_all_to_all(): lax.all_to_all(value, 'col', 0, 0, axis_index_groups=lines, tiled=True)  20.9 us
    ppermute x2, starting transfers between devices, swap_pair(): return lax.ppermute(value, 'col', [(i, i ^ 1) for i in range(n_col)])  19.9 us
    ppermute x6, waiting for transfers between devices, swap(): return lax.ppermute(value, 'row', [(i, i ^ mask) for i in range(n_row)])  12.8 us
    ppermute x2, waiting for transfers between devices, swap_pair(): return lax.ppermute(value, 'col', [(i, i ^ 1) for i in range(n_col)])  10.5 us
    pallas_call x1, Pallas kernels, shards(): pl.pallas_call(tiles_kernel, out_shape=shape((n_y, PAIR * nodes, feats),...  5.33 us
    pallas_call x1, Pallas kernels, shards(): pl.pallas_call(weight_kernel, out_shape=(shape((width // LANES * feats, L...  2.43 us
  transfers between devices with their start and end apart: 11, of which 7 were waited for; matrix products, arithmetic and copies ran while one was open for 0% of the time, Pallas kernels for 9%

profile of v12, /device:TPU:72, one launch (start us, length us, event | category | flops | bytes accessed | tf_op | source)
XLA Modules:
  0.0 108.4 jit_solution(660731015833300390)
XLA Ops:
  0.6 1.8 %shard_map.95 = (bf16[256,128]{1,0:T(8,128)(2,1)S(1)}, f32[8,128]{1,0:T(8,128)S(1)}) custom-call(bf16[256,1024]{1,0:T(8,128)(2,1)} %grad_hbm.3, s32[256,1024]{1,0:T(8,128)} %mask_hbm.3, bf16[128,1024]{1,0:T(8,128)(2,1)} %weight_hbm.1), custom_call_target="tpu_custom_call" | custom-call | flops 67108864 | bytes 2097152 | tf_op jit(solution)/shard_map/pallas_call | solution.py:201
  2.4 10.9 %collective-permute-start = (bf16[256,128]{1,0:T(8,128)(2,1)S(1)}, bf16[256,128]{1,0:T(8,128)(2,1)S(1)}, u32[]{:S(2)}, u32[]{:S(2)}) collective-permute-start(bf16[256,128]{1,0:T(8,128)(2,1)S(1)} %get-tuple-element.14.near), channel_id=1, source_target_pairs={{0,512},{128,640},{256,768},{384,896},{512,0},{640,128},{768,256},... | collective-permute-start | bytes 196616 | tf_op jit(solution)/shard_map/ppermute | solution.py:193
  13.3 0.0 copy-start
  13.3 0.0 copy-start.1
  13.4 2.4 %shard_map.96 = (bf16[1024,128]{1,0:T(8,128)(2,1)}, f32[8,128]{1,0:T(8,128)S(1)}) custom-call(bf16[256,1024]{1,0:T(8,128)(2,1)} %grad_hbm.3, s32[256,1024]{1,0:T(8,128)} %mask_hbm.3, bf16[256,128]{1,0:T(8,128)(2,1)} %aggregated_hbm.1, f32[8,128]{1,0:T(8,128)S(1)} %get-tuple-element.15.before_ref), custom_call_target="tpu_custom_call" | custom-call | flops 20000000000 | bytes 1048576 | tf_op jit(solution)/shard_map/pallas_call | solution.py:218
  15.8 7.6 %all-to-all-start = ((bf16[8,128,128]{2,1,0:T(8,128)(2,1)}), bf16[8,128,128]{2,1,0:T(8,128)(2,1)S(1)}, u32[]{:S(2)}, u32[]{:S(2)}) async-start(bf16[8,128,128]{2,1,0:T(8,128)(2,1)} %bitcast.9), calls=%async_computation | async-start | bytes 524288 | tf_op jit(solution)/shard_map/all_to_all | solution.py:199
  24.0 0.0 copy-done
  24.1 0.0 collective-permute-done.four
  24.1 4.3 %collective-permute-start.2 = (bf16[512,128]{1,0:T(8,128)(2,1)S(1)}, bf16[512,128]{1,0:T(8,128)(2,1)S(1)}, u32[]{:S(2)}, u32[]{:S(2)}) collective-permute-start(bf16[512,128]{1,0:T(8,128)(2,1)S(1)} %shard_map.97.packed_in), channel_id=1, source_target_pairs={{0,384},{128,256},{256,128},{384,0},{512,896},{640,768},{768,640},... | collective-permute-start | bytes 393224 | tf_op jit(solution)/shard_map/ppermute | solution.py:193
  28.4 3.7 %collective-permute-start.1 = (bf16[512,128]{1,0:T(8,128)(2,1)S(1)}, bf16[512,128]{1,0:T(8,128)(2,1)S(1)}, u32[]{:S(2)}, u32[]{:S(2)}) collective-permute-start(bf16[512,128]{1,0:T(8,128)(2,1)S(1)} %shard_map.97.packed_in), channel_id=1, source_target_pairs={{0,256},{128,384},{256,0},{384,128},{512,768},{640,896},{768,512},... | collective-permute-start | bytes 393224 | tf_op jit(solution)/shard_map/ppermute | solution.py:193
  32.1 1.4 %all-to-all-done.spread_ref = bf16[8,128,128]{2,1,0:T(8,128)(2,1)S(1)} async-done(((bf16[8,128,128]{2,1,0:T(8,128)(2,1)}), bf16[8,128,128]{2,1,0:T(8,128)(2,1)S(1)}, u32[]{:S(2)}, u32[]{:S(2)}) %all-to-all-start) | async-done | bytes 262176 | tf_op jit(solution)/shard_map/all_to_all | solution.py:199
  33.5 2.0 %collective-permute-start.3 = (bf16[640,128]{1,0:T(8,128)(2,1)S(1)}, bf16[640,128]{1,0:T(8,128)(2,1)S(1)}, u32[]{:S(2)}, u32[]{:S(2)}) collective-permute-start(bf16[640,128]{1,0:T(8,128)(2,1)S(1)} %shard_map.99), channel_id=1, source_target_pairs={{0,128},{128,0},{256,384},{384,256},{512,640},{640,512},{768,896},... | collective-permute-start | bytes 491528 | tf_op jit(solution)/shard_map/ppermute | solution.py:193
  35.5 2.3 %collective-permute-done.2.got_3 = bf16[512,128]{1,0:T(8,128)(2,1)S(1)} collective-permute-done((bf16[512,128]{1,0:T(8,128)(2,1)S(1)}, bf16[512,128]{1,0:T(8,128)(2,1)S(1)}, u32[]{:S(2)}, u32[]{:S(2)}) %collective-permute-start.2) | collective-permute-done | bytes 131104 | tf_op jit(solution)/shard_map/ppermute | solution.py:193
  37.8 1.5 %collective-permute-done.1.got_2 = bf16[512,128]{1,0:T(8,128)(2,1)S(1)} collective-permute-done((bf16[512,128]{1,0:T(8,128)(2,1)S(1)}, bf16[512,128]{1,0:T(8,128)(2,1)S(1)}, u32[]{:S(2)}, u32[]{:S(2)}) %collective-permute-start.1) | collective-permute-done | bytes 131104 | tf_op jit(solution)/shard_map/ppermute | solution.py:193
  39.3 1.5 %collective-permute-done.3.got_1 = bf16[640,128]{1,0:T(8,128)(2,1)S(1)} collective-permute-done((bf16[640,128]{1,0:T(8,128)(2,1)S(1)}, bf16[640,128]{1,0:T(8,128)(2,1)S(1)}, u32[]{:S(2)}, u32[]{:S(2)}) %collective-permute-start.3) | collective-permute-done | bytes 163872 | tf_op jit(solution)/shard_map/ppermute | solution.py:193
  40.8 6.3 %collective-permute-start.4 = (bf16[128,128]{1,0:T(8,128)(2,1)S(1)}, bf16[128,128]{1,0:T(8,128)(2,1)S(1)}, u32[]{:S(2)}, u32[]{:S(2)}) collective-permute-start(bf16[128,128]{1,0:T(8,128)(2,1)S(1)} %add_convert_fusion.1.own), channel_id=1, source_target_pairs={{0,256},{128,384},{256,0},{384,128},{512,768},{640,896},{768,512},... | collective-permute-start | bytes 98312 | tf_op jit(solution)/shard_map/ppermute | solution.py:193
  47.1 5.3 %shard_map.100.sent_in = bf16[8,512,128]{2,1,0:T(8,128)(2,1)} custom-call(s32[1]{0:T(128)} %bitcast.7.live_ref, s32[160]{0:T(256)S(1)} %get-tuple-element.26.row_ref, s32[160]{0:T(256)S(1)} %get-tuple-element.27.col_ref, bf16[160,128,128]{2,1,0:T(8,128)(2,1)} %bitcast.12, bf16[1536,128]{1,0:T(8,128)(2,1)S(1)} %shard_map.98.parts, ...), custom_call_target="tpu_custom_call" | custom-call | flops 20000000000 | bytes 5242880 | tf_op jit(solution)/shard_map/pallas_call | solution.py:272
  52.5 0.0 collective-permute-done.4.other
  52.5 6.2 %all-to-all-start.2 = ((bf16[8,512,128]{2,1,0:T(8,128)(2,1)}), bf16[8,512,128]{2,1,0:T(8,128)(2,1)S(1)}, u32[]{:S(2)}, u32[]{:S(2)}) async-start(bf16[8,512,128]{2,1,0:T(8,128)(2,1)} %get-tuple-element.22), calls=%async_computation.2 | async-start | bytes 2097152 | tf_op jit(solution)/shard_map/all_to_all | solution.py:199
  58.7 2.1 %collective-permute-start.5 = (bf16[128,128]{1,0:T(8,128)(2,1)S(1)}, bf16[128,128]{1,0:T(8,128)(2,1)S(1)}, u32[]{:S(2)}, u32[]{:S(2)}) collective-permute-start(bf16[128,128]{1,0:T(8,128)(2,1)S(1)} %get-tuple-element.18), channel_id=1, source_target_pairs={{0,512},{128,640},{256,768},{384,896},{512,0},{640,128},{768,256},... | collective-permute-start | bytes 98312 | tf_op jit(solution)/shard_map/ppermute | solution.py:193
  60.8 7.6 %collective-permute-done.5 = bf16[128,128]{1,0:T(8,128)(2,1)S(1)} collective-permute-done((bf16[128,128]{1,0:T(8,128)(2,1)S(1)}, bf16[128,128]{1,0:T(8,128)(2,1)S(1)}, u32[]{:S(2)}, u32[]{:S(2)}) %collective-permute-start.5) | collective-permute-done | bytes 32800 | tf_op jit(solution)/shard_map/ppermute | solution.py:193
  68.4 10.2 %collective-permute-start.6 = (bf16[128,128]{1,0:T(8,128)(2,1)S(1)}, bf16[128,128]{1,0:T(8,128)(2,1)S(1)}, u32[]{:S(2)}, u32[]{:S(2)}) collective-permute-start(bf16[128,128]{1,0:T(8,128)(2,1)S(1)} %add_convert_fusion.own), channel_id=1, source_target_pairs={{0,8},{8,0},{16,24},{24,16},{32,40},{40,32},{48,56},{56,48},{64,72... | collective-permute-start | bytes 98312 | tf_op jit(solution)/shard_map/ppermute | solution.py:196
  78.6 4.8 %collective-permute-done.6.other = bf16[128,128]{1,0:T(8,128)(2,1)S(1)} collective-permute-done((bf16[128,128]{1,0:T(8,128)(2,1)S(1)}, bf16[128,128]{1,0:T(8,128)(2,1)S(1)}, u32[]{:S(2)}, u32[]{:S(2)}) %collective-permute-start.6) | collective-permute-done | bytes 32800 | tf_op jit(solution)/shard_map/ppermute | solution.py:196
  83.4 0.7 shard_map.102
  84.2 0.0 all-to-all-done.2.got_ref
  84.2 7.2 %all-to-all-start.1 = ((bf16[8,128,128]{2,1,0:T(8,128)(2,1)}), bf16[8,128,128]{2,1,0:T(8,128)(2,1)S(1)}, u32[]{:S(2)}, u32[]{:S(2)}) async-start(bf16[8,128,128]{2,1,0:T(8,128)(2,1)} %get-tuple-element.19), calls=%async_computation.1 | async-start | bytes 524288 | tf_op jit(solution)/shard_map/all_to_all | solution.py:199
  91.4 0.1 shard_map.104
  91.5 9.7 %collective-permute-start.7 = (bf16[256,128]{1,0:T(8,128)(2,1)S(1)}, bf16[256,128]{1,0:T(8,128)(2,1)S(1)}, u32[]{:S(2)}, u32[]{:S(2)}) collective-permute-start(bf16[256,128]{1,0:T(8,128)(2,1)S(1)} %get-tuple-element.24), channel_id=1, source_target_pairs={{0,8},{8,0},{16,24},{24,16},{32,40},{40,32},{48,56},{56,48},{64,72... | collective-permute-start | bytes 196616 | tf_op jit(solution)/shard_map/ppermute | solution.py:196
  101.2 0.0 all-to-all-done.1.shares_ref
  101.3 0.8 shard_map.103
  102.1 5.7 %collective-permute-done.7.got_ref = bf16[256,128]{1,0:T(8,128)(2,1)S(1)} collective-permute-done((bf16[256,128]{1,0:T(8,128)(2,1)S(1)}, bf16[256,128]{1,0:T(8,128)(2,1)S(1)}, u32[]{:S(2)}, u32[]{:S(2)}) %collective-permute-start.7) | collective-permute-done | bytes 65568 | tf_op jit(solution)/shard_map/ppermute | solution.py:196
  107.8 0.6 shard_map.105
  (8 shorter events, 0.1 us)
Async XLA Ops:
  2.4 21.6 %collective-permute-start = (bf16[256,128]{1,0:T(8,128)(2,1)S(1)}, bf16[256,128]{1,0:T(8,128)(2,1)S(1)}, u32[]{:S(2)}, u32[]{:S(2)}) collective-permute-start(bf16[256,128]{1,0:T(8,128)(2,1)S(1)} %get-tuple-element.14.near), channel_id=1, source_target_pairs={{0,512},{128,640},{256,768},{384,896},{512,0},{640,128},{768,256},... | collective-permute-start | bytes 196616 | tf_op jit(solution)/shard_map/ppermute | solution.py:193
  13.3 10.7 %copy-start = (s32[1,1,160]{2,1,0:T(1,128)S(1)}, s32[1,1,160]{2,1,0:T(1,128)}, u32[]{:S(2)}) copy-start(s32[1,1,160]{2,1,0:T(1,128)} %param.13) | copy-start | bytes 1924
  13.3 10.7 %copy-start.1 = (s32[1,1,160]{2,1,0:T(1,128)S(1)}, s32[1,1,160]{2,1,0:T(1,128)}, u32[]{:S(2)}) copy-start(s32[1,1,160]{2,1,0:T(1,128)} %param.14) | copy-start | bytes 1924
  15.8 17.7 %all-to-all-start = ((bf16[8,128,128]{2,1,0:T(8,128)(2,1)}), bf16[8,128,128]{2,1,0:T(8,128)(2,1)S(1)}, u32[]{:S(2)}, u32[]{:S(2)}) async-start(bf16[8,128,128]{2,1,0:T(8,128)(2,1)} %bitcast.9), calls=%async_computation | async-start | bytes 524288 | tf_op jit(solution)/shard_map/all_to_all | solution.py:199
  24.1 13.7 %collective-permute-start.2 = (bf16[512,128]{1,0:T(8,128)(2,1)S(1)}, bf16[512,128]{1,0:T(8,128)(2,1)S(1)}, u32[]{:S(2)}, u32[]{:S(2)}) collective-permute-start(bf16[512,128]{1,0:T(8,128)(2,1)S(1)} %shard_map.97.packed_in), channel_id=1, source_target_pairs={{0,384},{128,256},{256,128},{384,0},{512,896},{640,768},{768,640},... | collective-permute-start | bytes 393224 | tf_op jit(solution)/shard_map/ppermute | solution.py:193
  28.4 10.9 %collective-permute-start.1 = (bf16[512,128]{1,0:T(8,128)(2,1)S(1)}, bf16[512,128]{1,0:T(8,128)(2,1)S(1)}, u32[]{:S(2)}, u32[]{:S(2)}) collective-permute-start(bf16[512,128]{1,0:T(8,128)(2,1)S(1)} %shard_map.97.packed_in), channel_id=1, source_target_pairs={{0,256},{128,384},{256,0},{384,128},{512,768},{640,896},{768,512},... | collective-permute-start | bytes 393224 | tf_op jit(solution)/shard_map/ppermute | solution.py:193
  33.5 7.3 %collective-permute-start.3 = (bf16[640,128]{1,0:T(8,128)(2,1)S(1)}, bf16[640,128]{1,0:T(8,128)(2,1)S(1)}, u32[]{:S(2)}, u32[]{:S(2)}) collective-permute-start(bf16[640,128]{1,0:T(8,128)(2,1)S(1)} %shard_map.99), channel_id=1, source_target_pairs={{0,128},{128,0},{256,384},{384,256},{512,640},{640,512},{768,896},... | collective-permute-start | bytes 491528 | tf_op jit(solution)/shard_map/ppermute | solution.py:193
  40.8 11.6 %collective-permute-start.4 = (bf16[128,128]{1,0:T(8,128)(2,1)S(1)}, bf16[128,128]{1,0:T(8,128)(2,1)S(1)}, u32[]{:S(2)}, u32[]{:S(2)}) collective-permute-start(bf16[128,128]{1,0:T(8,128)(2,1)S(1)} %add_convert_fusion.1.own), channel_id=1, source_target_pairs={{0,256},{128,384},{256,0},{384,128},{512,768},{640,896},{768,512},... | collective-permute-start | bytes 98312 | tf_op jit(solution)/shard_map/ppermute | solution.py:193
  52.5 31.7 %all-to-all-start.2 = ((bf16[8,512,128]{2,1,0:T(8,128)(2,1)}), bf16[8,512,128]{2,1,0:T(8,128)(2,1)S(1)}, u32[]{:S(2)}, u32[]{:S(2)}) async-start(bf16[8,512,128]{2,1,0:T(8,128)(2,1)} %get-tuple-element.22), calls=%async_computation.2 | async-start | bytes 2097152 | tf_op jit(solution)/shard_map/all_to_all | solution.py:199
  58.7 9.7 %collective-permute-start.5 = (bf16[128,128]{1,0:T(8,128)(2,1)S(1)}, bf16[128,128]{1,0:T(8,128)(2,1)S(1)}, u32[]{:S(2)}, u32[]{:S(2)}) collective-permute-start(bf16[128,128]{1,0:T(8,128)(2,1)S(1)} %get-tuple-element.18), channel_id=1, source_target_pairs={{0,512},{128,640},{256,768},{384,896},{512,0},{640,128},{768,256},... | collective-permute-start | bytes 98312 | tf_op jit(solution)/shard_map/ppermute | solution.py:193
  68.4 15.0 %collective-permute-start.6 = (bf16[128,128]{1,0:T(8,128)(2,1)S(1)}, bf16[128,128]{1,0:T(8,128)(2,1)S(1)}, u32[]{:S(2)}, u32[]{:S(2)}) collective-permute-start(bf16[128,128]{1,0:T(8,128)(2,1)S(1)} %add_convert_fusion.own), channel_id=1, source_target_pairs={{0,8},{8,0},{16,24},{24,16},{32,40},{40,32},{48,56},{56,48},{64,72... | collective-permute-start | bytes 98312 | tf_op jit(solution)/shard_map/ppermute | solution.py:196
  84.2 17.1 %all-to-all-start.1 = ((bf16[8,128,128]{2,1,0:T(8,128)(2,1)}), bf16[8,128,128]{2,1,0:T(8,128)(2,1)S(1)}, u32[]{:S(2)}, u32[]{:S(2)}) async-start(bf16[8,128,128]{2,1,0:T(8,128)(2,1)} %get-tuple-element.19), calls=%async_computation.1 | async-start | bytes 524288 | tf_op jit(solution)/shard_map/all_to_all | solution.py:199
  91.5 16.3 %collective-permute-start.7 = (bf16[256,128]{1,0:T(8,128)(2,1)S(1)}, bf16[256,128]{1,0:T(8,128)(2,1)S(1)}, u32[]{:S(2)}, u32[]{:S(2)}) collective-permute-start(bf16[256,128]{1,0:T(8,128)(2,1)S(1)} %get-tuple-element.24), channel_id=1, source_target_pairs={{0,8},{8,0},{16,24},{24,16},{32,40},{40,32},{48,56},{56,48},{64,72... | collective-permute-start | bytes 196616 | tf_op jit(solution)/shard_map/ppermute | solution.py:196

commit v13 on v12

--- a/solution.py
+++ b/solution.py
@@ -295,8 +295,8 @@
         cost_estimate=cost(4 * extra * LANES, 4 * extra * LANES * 2),
     )(sent, share, row_2)
     got = line_all_to_all(sent)
-    share = (share.astype(f32) + swap(share, 4).astype(f32)).astype(bf)
-    far = swap_pair(share)
+    share = (share.astype(f32) + swap_pair(share).astype(f32)).astype(bf)
+    far = swap(share, 4)
 
     whole, ready = pl.pallas_call(
         share_kernel,

time: 109 us -> 108 us (level)
  the two profiles are of different devices: /device:TPU:72 before, /device:TPU:74 now
where the time goes in v13:
time: 108 us
  starting transfers between devices  70.7 us (65%)
  waiting for transfers between devices  23.4 us (22%)
  Pallas kernels  12 us (11%)
  between operations  1.46 us (1%)
    ppermute x6, starting transfers between devices, swap(): return lax.ppermute(value, 'row', [(i, i ^ mask) for i in range(n_row)])  29.4 us
    ppermute x2, starting transfers between devices, swap_pair(): return lax.ppermute(value, 'col', [(i, i ^ 1) for i in range(n_col)])  21.9 us
    all_to_all x3, starting transfers between devices, line_all_to_all(): lax.all_to_all(value, 'col', 0, 0, axis_index_groups=lines, tiled=True)  19.4 us
    ppermute x6, waiting for transfers between devices, swap(): return lax.ppermute(value, 'row', [(i, i ^ mask) for i in range(n_row)])  12.8 us
    ppermute x2, waiting for transfers between devices, swap_pair(): return lax.ppermute(value, 'col', [(i, i ^ 1) for i in range(n_col)])  8.61 us
    pallas_call x1, Pallas kernels, shards(): pl.pallas_call(tiles_kernel, out_shape=shape((n_y, PAIR * nodes, feats),...  5.32 us
    pallas_call x1, Pallas kernels, shards(): pl.pallas_call(weight_kernel, out_shape=(shape((width // LANES * feats, L...  2.43 us
  transfers between devices with their start and end apart: 11, of which 8 were waited for; matrix products, arithmetic and copies ran while one was open for 0% of the time, Pallas kernels for 9%

profile of v13, /device:TPU:74, one launch (start us, length us, event | category | flops | bytes accessed | tf_op | source)
XLA Modules:
  0.0 107.6 jit_solution(4692888444859280060)
XLA Ops:
  0.6 1.8 %shard_map.95 = (bf16[256,128]{1,0:T(8,128)(2,1)S(1)}, f32[8,128]{1,0:T(8,128)S(1)}) custom-call(bf16[256,1024]{1,0:T(8,128)(2,1)} %grad_hbm.3, s32[256,1024]{1,0:T(8,128)} %mask_hbm.3, bf16[128,1024]{1,0:T(8,128)(2,1)} %weight_hbm.1), custom_call_target="tpu_custom_call" | custom-call | flops 67108864 | bytes 2097152 | tf_op jit(solution)/shard_map/pallas_call | solution.py:201
  2.4 10.9 %collective-permute-start = (bf16[256,128]{1,0:T(8,128)(2,1)S(1)}, bf16[256,128]{1,0:T(8,128)(2,1)S(1)}, u32[]{:S(2)}, u32[]{:S(2)}) collective-permute-start(bf16[256,128]{1,0:T(8,128)(2,1)S(1)} %get-tuple-element.14.near), channel_id=1, source_target_pairs={{0,512},{128,640},{256,768},{384,896},{512,0},{640,128},{768,256},... | collective-permute-start | bytes 196616 | tf_op jit(solution)/shard_map/ppermute | solution.py:193
  13.3 0.0 copy-start
  13.3 0.0 copy-start.1
  13.4 2.4 %shard_map.96 = (bf16[1024,128]{1,0:T(8,128)(2,1)}, f32[8,128]{1,0:T(8,128)S(1)}) custom-call(bf16[256,1024]{1,0:T(8,128)(2,1)} %grad_hbm.3, s32[256,1024]{1,0:T(8,128)} %mask_hbm.3, bf16[256,128]{1,0:T(8,128)(2,1)} %aggregated_hbm.1, f32[8,128]{1,0:T(8,128)S(1)} %get-tuple-element.15.before_ref), custom_call_target="tpu_custom_call" | custom-call | flops 20000000000 | bytes 1048576 | tf_op jit(solution)/shard_map/pallas_call | solution.py:218
  15.8 7.6 %all-to-all-start = ((bf16[8,128,128]{2,1,0:T(8,128)(2,1)}), bf16[8,128,128]{2,1,0:T(8,128)(2,1)S(1)}, u32[]{:S(2)}, u32[]{:S(2)}) async-start(bf16[8,128,128]{2,1,0:T(8,128)(2,1)} %bitcast.9), calls=%async_computation | async-start | bytes 524288 | tf_op jit(solution)/shard_map/all_to_all | solution.py:199
  24.0 0.0 copy-done
  24.1 0.0 collective-permute-done.four
  24.1 4.3 %collective-permute-start.2 = (bf16[512,128]{1,0:T(8,128)(2,1)S(1)}, bf16[512,128]{1,0:T(8,128)(2,1)S(1)}, u32[]{:S(2)}, u32[]{:S(2)}) collective-permute-start(bf16[512,128]{1,0:T(8,128)(2,1)S(1)} %shard_map.97.packed_in), channel_id=1, source_target_pairs={{0,384},{128,256},{256,128},{384,0},{512,896},{640,768},{768,640},... | collective-permute-start | bytes 393224 | tf_op jit(solution)/shard_map/ppermute | solution.py:193
  28.4 3.7 %collective-permute-start.1 = (bf16[512,128]{1,0:T(8,128)(2,1)S(1)}, bf16[512,128]{1,0:T(8,128)(2,1)S(1)}, u32[]{:S(2)}, u32[]{:S(2)}) collective-permute-start(bf16[512,128]{1,0:T(8,128)(2,1)S(1)} %shard_map.97.packed_in), channel_id=1, source_target_pairs={{0,256},{128,384},{256,0},{384,128},{512,768},{640,896},{768,512},... | collective-permute-start | bytes 393224 | tf_op jit(solution)/shard_map/ppermute | solution.py:193
  32.1 1.4 %all-to-all-done.spread_ref = bf16[8,128,128]{2,1,0:T(8,128)(2,1)S(1)} async-done(((bf16[8,128,128]{2,1,0:T(8,128)(2,1)}), bf16[8,128,128]{2,1,0:T(8,128)(2,1)S(1)}, u32[]{:S(2)}, u32[]{:S(2)}) %all-to-all-start) | async-done | bytes 262176 | tf_op jit(solution)/shard_map/all_to_all | solution.py:199
  33.5 2.0 %collective-permute-start.3 = (bf16[640,128]{1,0:T(8,128)(2,1)S(1)}, bf16[640,128]{1,0:T(8,128)(2,1)S(1)}, u32[]{:S(2)}, u32[]{:S(2)}) collective-permute-start(bf16[640,128]{1,0:T(8,128)(2,1)S(1)} %shard_map.99), channel_id=1, source_target_pairs={{0,128},{128,0},{256,384},{384,256},{512,640},{640,512},{768,896},... | collective-permute-start | bytes 491528 | tf_op jit(solution)/shard_map/ppermute | solution.py:193
  35.5 2.3 %collective-permute-done.2.got_3 = bf16[512,128]{1,0:T(8,128)(2,1)S(1)} collective-permute-done((bf16[512,128]{1,0:T(8,128)(2,1)S(1)}, bf16[512,128]{1,0:T(8,128)(2,1)S(1)}, u32[]{:S(2)}, u32[]{:S(2)}) %collective-permute-start.2) | collective-permute-done | bytes 131104 | tf_op jit(solution)/shard_map/ppermute | solution.py:193
  37.8 1.5 %collective-permute-done.1.got_2 = bf16[512,128]{1,0:T(8,128)(2,1)S(1)} collective-permute-done((bf16[512,128]{1,0:T(8,128)(2,1)S(1)}, bf16[512,128]{1,0:T(8,128)(2,1)S(1)}, u32[]{:S(2)}, u32[]{:S(2)}) %collective-permute-start.1) | collective-permute-done | bytes 131104 | tf_op jit(solution)/shard_map/ppermute | solution.py:193
  39.3 1.5 %collective-permute-done.3.got_1 = bf16[640,128]{1,0:T(8,128)(2,1)S(1)} collective-permute-done((bf16[640,128]{1,0:T(8,128)(2,1)S(1)}, bf16[640,128]{1,0:T(8,128)(2,1)S(1)}, u32[]{:S(2)}, u32[]{:S(2)}) %collective-permute-start.3) | collective-permute-done | bytes 163872 | tf_op jit(solution)/shard_map/ppermute | solution.py:193
  40.8 6.3 %collective-permute-start.4 = (bf16[128,128]{1,0:T(8,128)(2,1)S(1)}, bf16[128,128]{1,0:T(8,128)(2,1)S(1)}, u32[]{:S(2)}, u32[]{:S(2)}) collective-permute-start(bf16[128,128]{1,0:T(8,128)(2,1)S(1)} %add_convert_fusion.1.own), channel_id=1, source_target_pairs={{0,256},{128,384},{256,0},{384,128},{512,768},{640,896},{768,512},... | collective-permute-start | bytes 98312 | tf_op jit(solution)/shard_map/ppermute | solution.py:193
  47.2 5.3 %shard_map.100.sent_in = bf16[8,512,128]{2,1,0:T(8,128)(2,1)} custom-call(s32[1]{0:T(128)} %bitcast.7.live_ref, s32[160]{0:T(256)S(1)} %get-tuple-element.26.row_ref, s32[160]{0:T(256)S(1)} %get-tuple-element.27.col_ref, bf16[160,128,128]{2,1,0:T(8,128)(2,1)} %bitcast.12, bf16[1536,128]{1,0:T(8,128)(2,1)S(1)} %shard_map.98.parts, ...), custom_call_target="tpu_custom_call" | custom-call | flops 20000000000 | bytes 5242880 | tf_op jit(solution)/shard_map/pallas_call | solution.py:272
  52.5 0.0 collective-permute-done.4.other
  52.5 5.2 %all-to-all-start.2 = ((bf16[8,512,128]{2,1,0:T(8,128)(2,1)}), bf16[8,512,128]{2,1,0:T(8,128)(2,1)S(1)}, u32[]{:S(2)}, u32[]{:S(2)}) async-start(bf16[8,512,128]{2,1,0:T(8,128)(2,1)} %get-tuple-element.22), calls=%async_computation.2 | async-start | bytes 2097152 | tf_op jit(solution)/shard_map/all_to_all | solution.py:199
  57.7 11.3 %collective-permute-start.5 = (bf16[128,128]{1,0:T(8,128)(2,1)S(1)}, bf16[128,128]{1,0:T(8,128)(2,1)S(1)}, u32[]{:S(2)}, u32[]{:S(2)}) collective-permute-start(bf16[128,128]{1,0:T(8,128)(2,1)S(1)} %get-tuple-element.18), channel_id=1, source_target_pairs={{0,8},{8,0},{16,24},{24,16},{32,40},{40,32},{48,56},{56,48},{64,72... | collective-permute-start | bytes 98312 | tf_op jit(solution)/shard_map/ppermute | solution.py:196
  69.0 3.8 %collective-permute-done.5 = bf16[128,128]{1,0:T(8,128)(2,1)S(1)} collective-permute-done((bf16[128,128]{1,0:T(8,128)(2,1)S(1)}, bf16[128,128]{1,0:T(8,128)(2,1)S(1)}, u32[]{:S(2)}, u32[]{:S(2)}) %collective-permute-start.5) | collective-permute-done | bytes 32800 | tf_op jit(solution)/shard_map/ppermute | solution.py:196
  72.8 2.2 %collective-permute-start.6 = (bf16[128,128]{1,0:T(8,128)(2,1)S(1)}, bf16[128,128]{1,0:T(8,128)(2,1)S(1)}, u32[]{:S(2)}, u32[]{:S(2)}) collective-permute-start(bf16[128,128]{1,0:T(8,128)(2,1)S(1)} %add_convert_fusion.own), channel_id=1, source_target_pairs={{0,512},{128,640},{256,768},{384,896},{512,0},{640,128},{768,256},... | collective-permute-start | bytes 98312 | tf_op jit(solution)/shard_map/ppermute | solution.py:193
  75.0 7.5 %collective-permute-done.6.other = bf16[128,128]{1,0:T(8,128)(2,1)S(1)} collective-permute-done((bf16[128,128]{1,0:T(8,128)(2,1)S(1)}, bf16[128,128]{1,0:T(8,128)(2,1)S(1)}, u32[]{:S(2)}, u32[]{:S(2)}) %collective-permute-start.6) | collective-permute-done | bytes 32800 | tf_op jit(solution)/shard_map/ppermute | solution.py:193
  82.6 0.7 shard_map.102
  83.3 0.6 all-to-all-done.2.got_ref
  83.9 6.6 %all-to-all-start.1 = ((bf16[8,128,128]{2,1,0:T(8,128)(2,1)}), bf16[8,128,128]{2,1,0:T(8,128)(2,1)S(1)}, u32[]{:S(2)}, u32[]{:S(2)}) async-start(bf16[8,128,128]{2,1,0:T(8,128)(2,1)} %get-tuple-element.19), calls=%async_computation.1 | async-start | bytes 524288 | tf_op jit(solution)/shard_map/all_to_all | solution.py:199
  90.5 0.1 shard_map.104
  90.6 10.7 %collective-permute-start.7 = (bf16[256,128]{1,0:T(8,128)(2,1)S(1)}, bf16[256,128]{1,0:T(8,128)(2,1)S(1)}, u32[]{:S(2)}, u32[]{:S(2)}) collective-permute-start(bf16[256,128]{1,0:T(8,128)(2,1)S(1)} %get-tuple-element.24), channel_id=1, source_target_pairs={{0,8},{8,0},{16,24},{24,16},{32,40},{40,32},{48,56},{56,48},{64,72... | collective-permute-start | bytes 196616 | tf_op jit(solution)/shard_map/ppermute | solution.py:196
  101.3 0.0 all-to-all-done.1.shares_ref
  101.3 0.8 shard_map.103
  102.2 4.8 %collective-permute-done.7.got_ref = bf16[256,128]{1,0:T(8,128)(2,1)S(1)} collective-permute-done((bf16[256,128]{1,0:T(8,128)(2,1)S(1)}, bf16[256,128]{1,0:T(8,128)(2,1)S(1)}, u32[]{:S(2)}, u32[]{:S(2)}) %collective-permute-start.7) | collective-permute-done | bytes 65568 | tf_op jit(solution)/shard_map/ppermute | solution.py:196
  107.0 0.6 shard_map.105
  (8 shorter events, 0.1 us)
Async XLA Ops:
  2.4 21.6 %collective-permute-start = (bf16[256,128]{1,0:T(8,128)(2,1)S(1)}, bf16[256,128]{1,0:T(8,128)(2,1)S(1)}, u32[]{:S(2)}, u32[]{:S(2)}) collective-permute-start(bf16[256,128]{1,0:T(8,128)(2,1)S(1)} %get-tuple-element.14.near), channel_id=1, source_target_pairs={{0,512},{128,640},{256,768},{384,896},{512,0},{640,128},{768,256},... | collective-permute-start | bytes 196616 | tf_op jit(solution)/shard_map/ppermute | solution.py:193
  13.3 10.7 %copy-start = (s32[1,1,160]{2,1,0:T(1,128)S(1)}, s32[1,1,160]{2,1,0:T(1,128)}, u32[]{:S(2)}) copy-start(s32[1,1,160]{2,1,0:T(1,128)} %param.13) | copy-start | bytes 1924
  13.3 10.7 %copy-start.1 = (s32[1,1,160]{2,1,0:T(1,128)S(1)}, s32[1,1,160]{2,1,0:T(1,128)}, u32[]{:S(2)}) copy-start(s32[1,1,160]{2,1,0:T(1,128)} %param.14) | copy-start | bytes 1924
  15.8 17.7 %all-to-all-start = ((bf16[8,128,128]{2,1,0:T(8,128)(2,1)}), bf16[8,128,128]{2,1,0:T(8,128)(2,1)S(1)}, u32[]{:S(2)}, u32[]{:S(2)}) async-start(bf16[8,128,128]{2,1,0:T(8,128)(2,1)} %bitcast.9), calls=%async_computation | async-start | bytes 524288 | tf_op jit(solution)/shard_map/all_to_all | solution.py:199
  24.1 13.7 %collective-permute-start.2 = (bf16[512,128]{1,0:T(8,128)(2,1)S(1)}, bf16[512,128]{1,0:T(8,128)(2,1)S(1)}, u32[]{:S(2)}, u32[]{:S(2)}) collective-permute-start(bf16[512,128]{1,0:T(8,128)(2,1)S(1)} %shard_map.97.packed_in), channel_id=1, source_target_pairs={{0,384},{128,256},{256,128},{384,0},{512,896},{640,768},{768,640},... | collective-permute-start | bytes 393224 | tf_op jit(solution)/shard_map/ppermute | solution.py:193
  28.4 10.9 %collective-permute-start.1 = (bf16[512,128]{1,0:T(8,128)(2,1)S(1)}, bf16[512,128]{1,0:T(8,128)(2,1)S(1)}, u32[]{:S(2)}, u32[]{:S(2)}) collective-permute-start(bf16[512,128]{1,0:T(8,128)(2,1)S(1)} %shard_map.97.packed_in), channel_id=1, source_target_pairs={{0,256},{128,384},{256,0},{384,128},{512,768},{640,896},{768,512},... | collective-permute-start | bytes 393224 | tf_op jit(solution)/shard_map/ppermute | solution.py:193
  33.5 7.3 %collective-permute-start.3 = (bf16[640,128]{1,0:T(8,128)(2,1)S(1)}, bf16[640,128]{1,0:T(8,128)(2,1)S(1)}, u32[]{:S(2)}, u32[]{:S(2)}) collective-permute-start(bf16[640,128]{1,0:T(8,128)(2,1)S(1)} %shard_map.99), channel_id=1, source_target_pairs={{0,128},{128,0},{256,384},{384,256},{512,640},{640,512},{768,896},... | collective-permute-start | bytes 491528 | tf_op jit(solution)/shard_map/ppermute | solution.py:193
  40.8 11.6 %collective-permute-start.4 = (bf16[128,128]{1,0:T(8,128)(2,1)S(1)}, bf16[128,128]{1,0:T(8,128)(2,1)S(1)}, u32[]{:S(2)}, u32[]{:S(2)}) collective-permute-start(bf16[128,128]{1,0:T(8,128)(2,1)S(1)} %add_convert_fusion.1.own), channel_id=1, source_target_pairs={{0,256},{128,384},{256,0},{384,128},{512,768},{640,896},{768,512},... | collective-permute-start | bytes 98312 | tf_op jit(solution)/shard_map/ppermute | solution.py:193
  52.5 31.3 %all-to-all-start.2 = ((bf16[8,512,128]{2,1,0:T(8,128)(2,1)}), bf16[8,512,128]{2,1,0:T(8,128)(2,1)S(1)}, u32[]{:S(2)}, u32[]{:S(2)}) async-start(bf16[8,512,128]{2,1,0:T(8,128)(2,1)} %get-tuple-element.22), calls=%async_computation.2 | async-start | bytes 2097152 | tf_op jit(solution)/shard_map/all_to_all | solution.py:199
  57.7 15.1 %collective-permute-start.5 = (bf16[128,128]{1,0:T(8,128)(2,1)S(1)}, bf16[128,128]{1,0:T(8,128)(2,1)S(1)}, u32[]{:S(2)}, u32[]{:S(2)}) collective-permute-start(bf16[128,128]{1,0:T(8,128)(2,1)S(1)} %get-tuple-element.18), channel_id=1, source_target_pairs={{0,8},{8,0},{16,24},{24,16},{32,40},{40,32},{48,56},{56,48},{64,72... | collective-permute-start | bytes 98312 | tf_op jit(solution)/shard_map/ppermute | solution.py:196
  72.8 9.8 %collective-permute-start.6 = (bf16[128,128]{1,0:T(8,128)(2,1)S(1)}, bf16[128,128]{1,0:T(8,128)(2,1)S(1)}, u32[]{:S(2)}, u32[]{:S(2)}) collective-permute-start(bf16[128,128]{1,0:T(8,128)(2,1)S(1)} %add_convert_fusion.own), channel_id=1, source_target_pairs={{0,512},{128,640},{256,768},{384,896},{512,0},{640,128},{768,256},... | collective-permute-start | bytes 98312 | tf_op jit(solution)/shard_map/ppermute | solution.py:193
  83.9 17.5 %all-to-all-start.1 = ((bf16[8,128,128]{2,1,0:T(8,128)(2,1)}), bf16[8,128,128]{2,1,0:T(8,128)(2,1)S(1)}, u32[]{:S(2)}, u32[]{:S(2)}) async-start(bf16[8,128,128]{2,1,0:T(8,128)(2,1)} %get-tuple-element.19), calls=%async_computation.1 | async-start | bytes 524288 | tf_op jit(solution)/shard_map/all_to_all | solution.py:199
  90.6 16.3 %collective-permute-start.7 = (bf16[256,128]{1,0:T(8,128)(2,1)S(1)}, bf16[256,128]{1,0:T(8,128)(2,1)S(1)}, u32[]{:S(2)}, u32[]{:S(2)}) collective-permute-start(bf16[256,128]{1,0:T(8,128)(2,1)S(1)} %get-tuple-element.24), channel_id=1, source_target_pairs={{0,8},{8,0},{16,24},{24,16},{32,40},{40,32},{48,56},{56,48},{64,72... | collective-permute-start | bytes 196616 | tf_op jit(solution)/shard_map/ppermute | solution.py:196
